TPU v7x, 512 devices: a whole 4x4x16 slice. The times are simulated.
512 devices in a mesh: ctx: 64 (over y, z), head: 8 (over x, core).
Axes of the slice: x: 4, y: 4, z: 16, core: 2. Of those that a mesh axis runs over, the one named last changes fastest.
Arguments:
- queries: bfloat16 [65536, 3072], P('ctx', 'head'), may hold values from -20 to 20
- keys: bfloat16 [65536, 3072], P('ctx', 'head'), may hold values from -20 to 20
- values: bfloat16 [65536, 3072], P('ctx', 'head'), may hold values from -6 to 6
- block_mask: int32 [128, 128], replicated, may hold values from 0 to 1, as said below
- head_labels: int32 [24], replicated, may hold values from 0 to 1, as said below
- w_out: bfloat16 [3072, 3072], P('ctx', 'head'), may hold values from -0.109375 to 0.109375
Outputs:
- projected: bfloat16 [65536, 3072], P('ctx', 'head')
Inputs may be any that keep to these rules, and one draw needn't show every extreme that they name: block_mask is 1 only where |a - b| <= 2 or where b = 0 and a > 2; every diagonal entry is 1. `head_labels`: among the 3 heads of each group of consecutive heads, between 1 and 2 are temporal, and some group has exactly 2.
All inputs are finite; a program needn't handle non-finite values.
Results may differ from a plain program's by a relative error of at most 0.0057.
Values may be sent and summed in bfloat16 or wider, within the bound.
No kernel may reach another device: no remote copies, remote signals or barrier semaphores. Data moves between devices by JAX's collectives and lax.ppermute only.
A program may use at most 128 MiB of HBM per device.

v0:
```python
import math

import jax
import jax.numpy as jnp
from jax import lax
from jax.sharding import PartitionSpec as P

HEAD_DIM = 128
BLOCK = 512
REACH = 2


def extended_2(cells, sides, width):
    for axis, dim in sides:
        count = lax.axis_size(axis)
        ends = count - 1
        head = lax.slice_in_dim(cells, 0, width, axis=dim)
        tail = lax.slice_in_dim(cells, cells.shape[dim] - width, cells.shape[dim], axis=dim)
        cells = jnp.concatenate(
            [
                lax.ppermute(tail, axis, [(i, (i + 1) % count) for i in range(ends)]),
                cells,
                lax.ppermute(head, axis, [((i + 1) % count, i) for i in range(ends)]),
            ],
            axis=dim,
        )
    return cells


def broadcast(value, axis, source):
    kept = jnp.where(lax.axis_index(axis) == source, value, 0).astype(value.dtype)
    return lax.psum(kept, axis)


def position_pieces(x, parts):
    return x.reshape(parts, x.shape[0] // parts, 1, x.shape[1])


def frame_pieces(x, parts):
    return x.reshape(1, x.shape[0] // parts, parts, x.shape[1])


def flat_rows(x):
    return x.reshape(-1, x.shape[-1])


def body(queries, keys, values, block_mask, head_labels, w_out):
    parts = lax.axis_size("ctx")
    place = lax.axis_index("ctx")
    group = lax.axis_index("head")
    tok = queries.shape[0]
    heads_here = queries.shape[1] // HEAD_DIM
    labels = lax.dynamic_slice_in_dim(head_labels, group * heads_here, heads_here)
    temporal = labels == 1
    pick = jnp.repeat(temporal, HEAD_DIM)[None, :]
    head_ids = jnp.arange(heads_here, dtype=jnp.int32)
    moved = (
        lax.all_to_all(
            position_pieces(queries, parts), "ctx", split_axis=0, concat_axis=2, tiled=True
        ),
        lax.all_to_all(
            position_pieces(keys, parts), "ctx", split_axis=0, concat_axis=2, tiled=True
        ),
        lax.all_to_all(
            position_pieces(values, parts), "ctx", split_axis=0, concat_axis=2, tiled=True
        ),
    )
    q_use = jnp.where(pick, flat_rows(moved[0]), queries)
    k_use = jnp.where(pick, flat_rows(moved[1]), keys)
    v_use = jnp.where(pick, flat_rows(moved[2]), values)
    paired = jnp.stack([k_use, v_use])
    extended = extended_2(paired, (("ctx", 1),), REACH * BLOCK)
    first_block = broadcast(paired[:, :BLOCK], "ctx", 0)
    scale = 1.0 / math.sqrt(HEAD_DIM)
    qblocks = tok // BLOCK
    total_blocks = block_mask.shape[0]
    span = 2 * REACH + 1
    offsets = jnp.arange(-REACH, REACH + 1, dtype=jnp.int32)
    every_block = jnp.arange(total_blocks, dtype=jnp.int32)
    outputs = []
    for local in range(qblocks):
        index = place * qblocks + local
        cand = index + offsets
        inside = (cand >= 0) & (cand < total_blocks)
        row = lax.dynamic_slice_in_dim(block_mask, index, 1, 0)[0]
        hits = jnp.any((every_block[None, :] == cand[:, None]) & (row[None, :] == 1), axis=1)
        first_bit = (index > REACH) & (row[0] == 1)
        allbits = jnp.concatenate([inside & hits, first_bit[None]])
        columns = jnp.repeat(allbits, BLOCK)
        band = extended[:, local * BLOCK : (local + span) * BLOCK]
        gathered = jnp.concatenate([band, first_block], axis=1)
        q_block = q_use[local * BLOCK : (local + 1) * BLOCK]

        def head_fn(head):
            query = lax.dynamic_slice_in_dim(q_block, head * HEAD_DIM, HEAD_DIM, 1)
            keyrow = lax.dynamic_slice_in_dim(gathered[0], head * HEAD_DIM, HEAD_DIM, 1)
            valrow = lax.dynamic_slice_in_dim(gathered[1], head * HEAD_DIM, HEAD_DIM, 1)
            scores = (
                jnp.einsum("qd,kd->qk", query, keyrow, preferred_element_type=jnp.float32) * scale
            )
            scores = jnp.where(columns[None, :], scores, -jnp.inf)
            top = jnp.max(scores, axis=1, keepdims=True)
            weights = jnp.exp(scores - top)
            total = jnp.sum(weights, axis=1, keepdims=True)
            mixed = jnp.dot(
                weights.astype(jnp.bfloat16), valrow, preferred_element_type=jnp.float32
            )
            return (mixed / total).astype(jnp.bfloat16)

        per_head = lax.map(head_fn, head_ids)
        outputs.append(per_head.transpose(1, 0, 2).reshape(BLOCK, heads_here * HEAD_DIM))
    attended = jnp.concatenate(outputs, axis=0)
    returned = lax.all_to_all(
        frame_pieces(attended, parts), "ctx", split_axis=2, concat_axis=0, tiled=True
    )
    attn = jnp.where(pick, flat_rows(returned), attended)
    weight_cols = lax.all_gather(w_out, "ctx", axis=0, tiled=True)
    summed = jnp.dot(
        lax.all_gather(attn, "head", axis=1, tiled=True),
        weight_cols,
        preferred_element_type=jnp.float32,
    )
    return summed.astype(jnp.bfloat16)


def solution(mesh):
    return jax.shard_map(
        body,
        mesh=mesh,
        in_specs=(P("ctx", "head"), P("ctx", "head"), P("ctx", "head"), P(), P(), P("ctx", "head")),
        out_specs=P("ctx", "head"),
        check_vma=False,
    )
```

profile of v0, /device:TPU:1, one launch (start us, length us, event | category | flops | bytes accessed | tf_op | source)
XLA Modules:
  0.0 640.0 jit_solution(1962932388197803652)
XLA Ops:
  6.5 59.3 %all_to_all.60 = bf16[64,16,1,384]{3,1,2,0:T(8,128)(2,1)} all-to-all(bf16[64,16,1,384]{3,1,2,0:T(8,128)(2,1)} %bitcast.102), channel_id=1, replica_groups=mesh['ctx'=64,'head'=8] {'ctx'}, dimensions={0} | all-to-all | bytes 1572864 | tf_op jit(solution)/shard_map/all_to_all | solution.py:58
  65.9 49.0 %all_to_all.61 = bf16[64,16,1,384]{3,1,2,0:T(8,128)(2,1)S(1)} all-to-all(bf16[64,16,1,384]{3,1,2,0:T(8,128)(2,1)} %bitcast.101), channel_id=1, replica_groups=mesh['ctx'=64,'head'=8] {'ctx'}, dimensions={0} | all-to-all | bytes 1572864 | tf_op jit(solution)/shard_map/all_to_all | solution.py:61
  114.8 9.7 %all-to-all-start.2 = ((bf16[64,16,1,384]{3,1,2,0:T(8,128)(2,1)}), bf16[64,16,1,384]{3,1,2,0:T(8,128)(2,1)S(1)}, u32[]{:S(2)}, u32[]{:S(2)}) async-start(bf16[64,16,1,384]{3,1,2,0:T(8,128)(2,1)} %bitcast.100), calls=%async_computation.2 | async-start | bytes 1572864 | tf_op jit(solution)/shard_map/all_to_all | solution.py:64
  124.8 2.2 copy.50
  127.0 1.1 copy.52
  128.0 36.1 %all-to-all-done.2 = bf16[64,16,1,384]{3,1,2,0:T(8,128)(2,1)S(1)} async-done(((bf16[64,16,1,384]{3,1,2,0:T(8,128)(2,1)}), bf16[64,16,1,384]{3,1,2,0:T(8,128)(2,1)S(1)}, u32[]{:S(2)}, u32[]{:S(2)}) %all-to-all-start.2) | async-done | bytes 786464 | tf_op jit(solution)/shard_map/all_to_all | solution.py:64
  164.1 0.2 copy.54
  164.3 2.8 bitcast_select_fusion.1
  167.1 1.0 fusion.55
  168.2 1.3 pad_maximum_fusion.3
  169.5 6.6 %collective-permute-start = (bf16[2,1024,384]{2,1,0:T(8,128)(2,1)}, bf16[2,1024,384]{2,1,0:T(8,128)(2,1)}, u32[]{:S(2)}, u32[]{:S(2)}) collective-permute-start(bf16[2,1024,384]{2,1,0:T(8,128)(2,1)} %pad_maximum_fusion.3), channel_id=1, source_target_pairs={{0,8},{8,16},{16,24},{24,32},{32,40},{40,48},{48,56},{56,64},{64,7... | collective-permute-start | bytes 4718600 | tf_op jit(solution)/shard_map/ppermute | solution.py:21
  176.1 1.3 collective-permute-start.1
  177.4 0.2 all-gather.3.cloned.1.call-start
  177.7 0.8 compare_bitcast_fusion.1
  178.5 0.2 fusion.59
  178.7 0.2 fusion.57
  179.2 31.2 %collective-permute-done = bf16[2,1024,384]{2,1,0:T(8,128)(2,1)} collective-permute-done((bf16[2,1024,384]{2,1,0:T(8,128)(2,1)}, bf16[2,1024,384]{2,1,0:T(8,128)(2,1)}, u32[]{:S(2)}, u32[]{:S(2)}) %collective-permute-start) | collective-permute-done | bytes 1572896 | tf_op jit(solution)/shard_map/ppermute | solution.py:21
  210.4 6.5 %collective-permute-done.1 = bf16[2,1024,384]{2,1,0:T(8,128)(2,1)} collective-permute-done((bf16[2,1024,384]{2,1,0:T(8,128)(2,1)}, bf16[2,1024,384]{2,1,0:T(8,128)(2,1)}, u32[]{:S(2)}, u32[]{:S(2)}) %collective-permute-start.1) | collective-permute-done | bytes 1572896 | tf_op jit(solution)/shard_map/ppermute | solution.py:23
  216.9 3.0 pad_maximum_fusion.2
  219.9 3.6 fusion.64
  223.5 201.6 %all-reduce.2.cloned.1.call-done = bf16[2,512,384]{2,1,0:T(8,128)(2,1)} async-done(((bf16[2,512,384]{2,1,0:T(8,128)(2,1)}), bf16[2,512,384]{2,1,0:T(8,128)(2,1)}) %all-reduce.2.cloned.1.call-update) | async-done | bytes 786448 | tf_op jit(solution)/shard_map/psum | solution.py:32
  425.1 8.1 %pad_maximum_fusion.1 = (bf16[2,3072,384]{2,1,0:T(8,128)(2,1)}, bf16[2,3072,384]{2,1,0:T(8,128)(2,1)}) fusion(bf16[2,512,384]{2,1,0:T(8,128)(2,1)} %all-reduce.2.cloned.1.call-done, bf16[2,2560,384]{2,1,0:T(8,128)(2,1)} %get-tuple-element.149, bf16[2,2560,384]{2,1,0:T(8,128)(2,1)} %get-tuple-element.150), kind=kLoop, calls=%fused_computation.45 | loop fusion | flops 16515072 | bytes 18087936 | tf_op jit(solution)/shard_map/concatenate | solution.py:91
  433.2 24.9 %while.22 = (s32[]{:T(128)}, bf16[3,512,128]{1,2,0:T(8,128)(2,1)S(1)}, s32[3]{0:T(128)S(1)}, bf16[512,384]{1,0:T(8,128)(2,1)S(1)}, bf16[2,3072,384]{2,1,0:T(8,12...) while((s32[]{:T(128)}, ...), condition=%wide.region_5.6_spmd.clone, body=%wide.region_2.5_spmd.clone.sunk | while | flops 822737920 | bytes 30700716 | solution.py:110
  433.2 0.6 dynamic_slice.101
  434.6 2.9 fusion.82
  437.4 1.2 fusion.83
  438.6 1.4 fusion.84
  440.0 1.3 fusion.85
  441.5 0.6 dynamic_slice.101
  442.8 2.9 fusion.82
  445.7 1.2 fusion.83
  446.9 1.4 fusion.84
  448.3 1.4 fusion.85
  449.6 0.1 copy.66
  449.8 0.6 dynamic_slice.101
  451.1 2.9 fusion.82
  454.0 1.2 fusion.83
  455.1 1.4 fusion.84
  456.6 1.4 fusion.85
  457.9 0.1 copy.66
  458.1 24.9 %while.23 = (s32[]{:T(128)}, bf16[3,512,128]{1,2,0:T(8,128)(2,1)S(1)}, s32[3]{0:T(128)S(1)}, bf16[512,384]{1,0:T(8,128)(2,1)S(1)}, bf16[2,3072,384]{2,1,0:T(8,12...) while((s32[]{:T(128)}, ...), condition=%wide.region_10.11_spmd.clone, body=%wide.region_7.10_spmd.clone.sunk | while | flops 822737920 | bytes 30700716 | solution.py:110
  458.1 0.6 dynamic_slice.105
  459.5 2.9 fusion.88
  462.3 1.2 fusion.89
  463.5 1.4 fusion.90
  464.9 1.4 fusion.91
  466.4 0.6 dynamic_slice.105
  467.8 2.9 fusion.88
  470.6 1.2 fusion.89
  471.8 1.4 fusion.90
  473.2 1.4 fusion.91
  474.7 0.6 dynamic_slice.105
  476.1 2.9 fusion.88
  478.9 1.2 fusion.89
  480.1 1.4 fusion.90
  481.5 1.4 fusion.91
  483.0 0.2 copy.57
  483.2 0.2 copy.58
  483.5 0.5 copy.59
  484.0 38.4 %all_to_all.62 = bf16[1,16,64,384]{3,1,0,2:T(8,128)(2,1)S(1)} all-to-all(bf16[1,16,64,384]{3,1,0,2:T(8,128)(2,1)S(1)} %copy.59), channel_id=1, replica_groups=mesh['ctx'=64,'head'=8] {'ctx'}, dimensions={2} | all-to-all | bytes 1572864 | tf_op jit(solution)/shard_map/all_to_all | solution.py:113
  522.4 1.1 bitcast_select_fusion
  523.6 46.4 %all-gather.5.cloned.1.call-done = bf16[3072,384]{1,0:T(8,128)(2,1)} async-done(((bf16[48,384]{1,0:T(8,128)(2,1)}), bf16[3072,384]{1,0:T(8,128)(2,1)}) %all-gather.5.cloned.1.call-update) | async-done | bytes 2359312 | tf_op jit(solution)/shard_map/all_gather | solution.py:117
  570.0 55.8 %all-gather.3.cloned.1.call-done = bf16[1024,3072]{1,0:T(8,128)(2,1)} async-done(((bf16[1024,384]{1,0:T(8,128)(2,1)}), bf16[1024,3072]{1,0:T(8,128)(2,1)}) %all-gather.3.cloned.1.call-update) | async-done | bytes 6291472 | tf_op jit(solution)/shard_map/all_gather | solution.py:119
  625.7 7.8 %convolution_convert_fusion = bf16[1024,384]{1,0:T(8,128)(2,1)} fusion(bf16[1024,3072]{1,0:T(8,128)(2,1)} %all-gather.3.cloned.1.call-done, bf16[3072,384]{1,0:T(8,128)(2,1)} %all-gather.5.cloned.1.call-done), kind=kOutput, calls=%fused_computation.50 | convolution fusion | flops 2416312320 | bytes 9437184 | tf_op jit(solution)/shard_map/dot_general | solution.py:118
  (48 shorter events, 1.8 us)
Async XLA Ops:
  6.5 118.1 %copy-start.3 = (s32[24]{0:T(128)S(1)}, s32[24]{0:T(128)}, u32[]{:S(2)}) copy-start(s32[24]{0:T(128)} %param.14) | copy-start | bytes 292
  6.5 157.7 %copy-start = (bf16[1024,384]{1,0:T(8,128)(2,1)S(1)}, bf16[1024,384]{1,0:T(8,128)(2,1)}, u32[]{:S(2)}) copy-start(bf16[1024,384]{1,0:T(8,128)(2,1)} %param.12) | copy-start | bytes 2359300
  6.5 157.8 %copy-start.1 = (bf16[1024,384]{1,0:T(8,128)(2,1)S(1)}, bf16[1024,384]{1,0:T(8,128)(2,1)}, u32[]{:S(2)}) copy-start(bf16[1024,384]{1,0:T(8,128)(2,1)} %param.11) | copy-start | bytes 2359300
  114.8 49.2 %all-to-all-start.2 = ((bf16[64,16,1,384]{3,1,2,0:T(8,128)(2,1)}), bf16[64,16,1,384]{3,1,2,0:T(8,128)(2,1)S(1)}, u32[]{:S(2)}, u32[]{:S(2)}) async-start(bf16[64,16,1,384]{3,1,2,0:T(8,128)(2,1)} %bitcast.100), calls=%async_computation.2 | async-start | bytes 1572864 | tf_op jit(solution)/shard_map/all_to_all | solution.py:64
  124.5 300.6 %all-reduce.2.cloned.1.call-start = ((), (), s32[]{:S(2)}) async-start(), calls=%async_computation.4 | async-start | bytes 1572864 | tf_op jit(solution)/shard_map/psum | solution.py:32
  167.1 12.0 %copy-start.2 = (bf16[1024,384]{1,0:T(8,128)(2,1)S(1)}, bf16[1024,384]{1,0:T(8,128)(2,1)}, u32[]{:S(2)}) copy-start(bf16[1024,384]{1,0:T(8,128)(2,1)} %get-tuple-element.159) | copy-start | bytes 2359300
  168.1 401.8 %all-gather.5.cloned.1.call-start = ((), (), s32[]{:S(2)}) async-start(), calls=%async_computation.6 | async-start | bytes 2396160 | tf_op jit(solution)/shard_map/all_gather | solution.py:117
  169.5 40.9 %collective-permute-start = (bf16[2,1024,384]{2,1,0:T(8,128)(2,1)}, bf16[2,1024,384]{2,1,0:T(8,128)(2,1)}, u32[]{:S(2)}, u32[]{:S(2)}) collective-permute-start(bf16[2,1024,384]{2,1,0:T(8,128)(2,1)} %pad_maximum_fusion.3), channel_id=1, source_target_pairs={{0,8},{8,16},{16,24},{24,32},{32,40},{40,48},{48,56},{56,64},{64,7... | collective-permute-start | bytes 4718600 | tf_op jit(solution)/shard_map/ppermute | solution.py:21
  176.1 40.8 %collective-permute-start.1 = (bf16[2,1024,384]{2,1,0:T(8,128)(2,1)}, bf16[2,1024,384]{2,1,0:T(8,128)(2,1)}, u32[]{:S(2)}, u32[]{:S(2)}) collective-permute-start(bf16[2,1024,384]{2,1,0:T(8,128)(2,1)} %pad_maximum_fusion.3), channel_id=1, source_target_pairs={{8,0},{16,8},{24,16},{32,24},{40,32},{48,40},{56,48},{64,56},{72,6... | collective-permute-start | bytes 4718600 | tf_op jit(solution)/shard_map/ppermute | solution.py:23
  177.4 448.3 %all-gather.3.cloned.1.call-start = ((), (), s32[]{:S(2)}) async-start(), calls=%async_computation.5 | async-start | bytes 7077888 | tf_op jit(solution)/shard_map/all_gather | solution.py:119
Sparse Core Ops, SparseCore 0:
  168.3 256.7 all-reduce.1
  428.5 141.4 all-gather.4
  572.3 53.3 all-gather.2
where the time goes:
time: 641 us; the launch traced here: 640 us
  waiting for transfers between devices  378 us (59%)
  blocking collectives  147 us (23%)
  local copies, waits for them, and re-layouts  30.1 us (5%)
  other arithmetic  27.3 us (4%)
  matrix products  22.9 us (4%)
  starting transfers between devices  17.9 us (3%)
  between operations  13.4 us (2%)
    psum x1, waiting for transfers between devices, broadcast(): return lax.psum(kept, axis)  202 us
    all_to_all x1, blocking collectives, body(): lax.all_to_all(position_pieces(queries, parts), 'ctx', split_axis=0, conc...  59.3 us
    all_gather x1, waiting for transfers between devices, body(): lax.all_gather(attn, 'head', axis=1, tiled=True)  55.8 us
    all_to_all x1, blocking collectives, body(): lax.all_to_all(position_pieces(keys, parts), 'ctx', split_axis=0, concat_...  49 us
    all_gather x1, waiting for transfers between devices, body(): weight_cols = lax.all_gather(w_out, 'ctx', axis=0, tiled=True)  46.4 us
    all_to_all x1, blocking collectives, body(): lax.all_to_all(frame_pieces(attended, parts), 'ctx', split_axis=2, concat...  38.4 us
    all_to_all x1, waiting for transfers between devices, body(): lax.all_to_all(position_pieces(values, parts), 'ctx', split_axis=0, conca...  36.1 us
    ppermute x1, waiting for transfers between devices, extended_2(): lax.ppermute(tail, axis, [(i, (i + 1) % count) for i in range(ends)])  31.2 us
  transfers between devices with their start and end apart: 6, of which 6 were waited for; matrix products, arithmetic and copies ran while one was open for 11% of the time, Pallas kernels for 0%

commit v1 on v0

v1 whole, which is shorter than its diff:
```python
import math

import jax
import jax.numpy as jnp
from jax import lax
from jax.experimental import pallas as pl
from jax.experimental.pallas import tpu as pltpu
from jax.sharding import PartitionSpec as P

HEAD_DIM = 128
BLOCK = 512
REACH = 2
BF = jnp.bfloat16
F32 = jnp.float32
RATE = math.log2(math.e) / math.sqrt(HEAD_DIM)
NEAR = ((0, 1, 2, 3, 4, 6), (1, 2, 3, 4, 5, 6))


def lanes(index):
    return slice(index * HEAD_DIM, (index + 1) * HEAD_DIM)


def attention_kernel(heads, bits, q_ref, own_ref, left_ref, right_ref, first_ref, out_ref, s_ref, m_ref, l_ref, acc_ref):
    sides = (left_ref, left_ref, own_ref, own_ref, right_ref, right_ref, first_ref)

    def tile(kind, place, slot):
        if place == 6:
            return first_ref[:, lanes(kind * heads + slot)]
        return sides[place][:, lanes((kind * 2 + place % 2) * heads + slot)]

    for slot in range(heads):
        for b in range(2):
            query = q_ref[:, lanes(b * heads + slot)]
            m_ref[...] = jnp.full_like(m_ref, -jnp.inf)
            l_ref[...] = jnp.zeros_like(l_ref)
            acc_ref[...] = jnp.zeros_like(acc_ref)
            for n, place in enumerate(NEAR[b]):

                @pl.when(bits[b, n] > 0)
                def _():
                    s = lax.dot_general(
                        query, tile(0, place, slot), (((1,), (1,)), ((), ())), preferred_element_type=F32
                    )
                    s_ref[n] = s
                    m = m_ref[...]
                    for c in range(BLOCK // HEAD_DIM):
                        m = jnp.maximum(m, s[:, lanes(c)])
                    m_ref[...] = m

            top = jnp.max(m_ref[...], axis=1, keepdims=True)
            m_ref[...] = jnp.broadcast_to(top, m_ref.shape)
            for n, place in enumerate(NEAR[b]):

                @pl.when(bits[b, n] > 0)
                def _():
                    peak = m_ref[...]
                    total = l_ref[...]
                    parts = []
                    for c in range(BLOCK // HEAD_DIM):
                        w = jnp.exp2((s_ref[n, :, lanes(c)] - peak) * RATE)
                        total = total + w
                        parts.append(w.astype(BF))
                    l_ref[...] = total
                    acc_ref[...] += jnp.dot(
                        jnp.concatenate(parts, axis=1), tile(1, place, slot), preferred_element_type=F32
                    )

            total = jnp.sum(l_ref[...], axis=1, keepdims=True)
            out_ref[:, lanes(b * heads + slot)] = (acc_ref[...] / total).astype(BF)


def attention(heads, bits, query, own, left, right, first):
    vmem = pl.BlockSpec(memory_space=pltpu.VMEM)
    pairs = heads * 2 * 6
    return pl.pallas_call(
        lambda *refs: attention_kernel(heads, *refs),
        out_shape=jax.ShapeDtypeStruct(query.shape, BF),
        in_specs=[pl.BlockSpec(memory_space=pltpu.SMEM)] + [vmem] * 5,
        out_specs=vmem,
        scratch_shapes=[
            pltpu.VMEM((6, BLOCK, BLOCK), F32),
            pltpu.VMEM((BLOCK, HEAD_DIM), F32),
            pltpu.VMEM((BLOCK, HEAD_DIM), F32),
            pltpu.VMEM((BLOCK, HEAD_DIM), F32),
        ],
        compiler_params=pltpu.CompilerParams(vmem_limit_bytes=40 << 20),
        cost_estimate=pl.CostEstimate(
            flops=pairs * 4 * BLOCK * BLOCK * HEAD_DIM,
            bytes_accessed=heads * 16 * BLOCK * HEAD_DIM * 2,
            transcendentals=pairs * BLOCK * BLOCK,
        ),
    )(bits, query, own, left, right, first)


def projection_kernel(groups, order, spatial_ref, mixed_ref, w_ref, out_ref):
    total = None
    for g in range(groups):
        rows = [
            w_ref[pl.ds(pl.multiple_of(order[g * 3 + slot] * HEAD_DIM, HEAD_DIM), HEAD_DIM), :] for slot in range(3)
        ]
        part = jnp.dot(
            mixed_ref[:, 2 * g * HEAD_DIM : 2 * (g + 1) * HEAD_DIM],
            jnp.concatenate(rows[:2], axis=0),
            preferred_element_type=F32,
        )
        part += jnp.dot(spatial_ref[:, lanes(g)], rows[2], preferred_element_type=F32)
        total = part if total is None else total + part
    out_ref[...] = total.astype(BF)


def projection(groups, order, spatial, mixed, w):
    vmem = pl.BlockSpec(memory_space=pltpu.VMEM)
    return pl.pallas_call(
        lambda *refs: projection_kernel(groups, *refs),
        out_shape=jax.ShapeDtypeStruct((spatial.shape[0], w.shape[1]), BF),
        in_specs=[pl.BlockSpec(memory_space=pltpu.SMEM)] + [vmem] * 3,
        out_specs=vmem,
        compiler_params=pltpu.CompilerParams(vmem_limit_bytes=40 << 20),
    )(order, spatial, mixed, w)


def slots_of(labels):
    temporal = labels == 1
    a = jnp.where(temporal[:, 0], 0, jnp.where(temporal[:, 1], 1, 2))
    c = jnp.where(~temporal[:, 2], 2, jnp.where(~temporal[:, 1], 1, 0))
    return jnp.stack([a, 3 - a - c, c], axis=1).astype(jnp.int32)


def split_blocks(x):
    return jnp.concatenate([x[:BLOCK], x[BLOCK:]], axis=1)


def position_pack(x, parts):
    rows = x.shape[0] // parts // 2
    return x.reshape(parts, 2, rows, x.shape[1]).transpose(0, 2, 1, 3).reshape(parts, rows, 2 * x.shape[1])


def exchange(x):
    return lax.all_to_all(x, "ctx", 0, 0, tiled=True)


def both_ways(x, count):
    left = lax.ppermute(x, "ctx", [(i, i + 1) for i in range(count - 1)])
    right = lax.ppermute(x, "ctx", [(i + 1, i) for i in range(count - 1)])
    return left, right


def scattered(x, place, count):
    step = count // 2
    while step >= 1:
        half = x.shape[0] // 2
        got = lax.ppermute(x[half:], "ctx", [(i, i + step) for i in range(0, count, 2 * step)])
        x = jnp.where(place % (2 * step) == step, got, x[:half])
        step //= 2
    return x


def gathered(x, count):
    for unit in (4, 1, 16):
        got = [lax.ppermute(x, "ctx", [(i, i ^ (unit * k)) for i in range(count)]) for k in (1, 2, 3)]
        x = jnp.concatenate([x] + got, axis=0)
    return x


def body(queries, keys, values, block_mask, head_labels, w_out):
    parts = lax.axis_size("ctx")
    groups = lax.axis_size("head")
    place = lax.axis_index("ctx")
    group = lax.axis_index("head")
    slots = slots_of(head_labels.reshape(groups, 3))
    mine = lax.dynamic_slice_in_dim(slots, group, 1, 0)[0]
    labels = lax.dynamic_slice_in_dim(head_labels, group * 3, 3)
    moves = lax.dynamic_slice_in_dim(labels, mine[1], 1)[0] == 1
    order = (slots + 3 * jnp.arange(groups, dtype=jnp.int32)[:, None]).reshape(-1)

    def head_of(x, slot):
        return lax.dynamic_slice_in_dim(x, mine[slot] * HEAD_DIM, HEAD_DIM, 1)

    weight_cols = lax.all_gather(w_out, "ctx", axis=0, tiled=True)

    q0, q1, q2 = (head_of(queries, s) for s in range(3))
    k0, k1, k2 = (head_of(keys, s) for s in range(3))
    v0, v1, v2 = (head_of(values, s) for s in range(3))

    index = place * 2 + jnp.arange(2, dtype=jnp.int32)
    total_blocks = block_mask.shape[0]
    rows = lax.dynamic_slice_in_dim(block_mask, place * 2, 2, 0)
    cand = index[:, None] + jnp.arange(-REACH, REACH + 1, dtype=jnp.int32)[None, :]
    every = jnp.arange(total_blocks, dtype=jnp.int32)
    hits = jnp.any((cand[:, :, None] == every[None, None, :]) & (rows[:, None, :] == 1), axis=2)
    first_bit = (index > REACH) & (rows[:, 0] == 1)
    bits = jnp.concatenate([hits, first_bit[:, None]], axis=1).astype(jnp.int32)

    pack_k = position_pack(jnp.concatenate([k0, k1], axis=1), parts)
    pack_v = position_pack(jnp.concatenate([v0, v1], axis=1), parts)
    moved_kv = exchange(jnp.concatenate([pack_k, pack_v], axis=2)).reshape(BLOCK, -1)
    moved_q = exchange(position_pack(jnp.concatenate([q0, q1], axis=1), parts)).reshape(BLOCK, -1)

    local = jnp.concatenate([k0, k1, v0, v1], axis=1)[: BLOCK // parts]
    shares = scattered(jnp.concatenate([k1, k2, v1, v2], axis=1)[:BLOCK], place, parts)
    piece = jnp.concatenate(
        [
            local[:, lanes(0)],
            jnp.where(moves, local[:, lanes(1)], shares[:, lanes(0)]),
            local[:, lanes(2)],
            jnp.where(moves, local[:, lanes(3)], shares[:, lanes(2)]),
            shares[:, lanes(1)],
            shares[:, lanes(3)],
        ],
        axis=1,
    )
    first = gathered(piece, parts)

    own2 = jnp.concatenate([split_blocks(k2), split_blocks(v2)], axis=1)
    left2, right2 = both_ways(own2, parts)
    out2 = attention(1, bits, split_blocks(q2), own2, left2, right2, first[:, 4 * HEAD_DIM :])
    attn2 = jnp.concatenate([out2[:, lanes(0)], out2[:, lanes(1)]], axis=0)
    spatial = lax.all_gather(attn2, "head", axis=1, tiled=True)

    def mix(moved, still, kinds):
        cols = []
        for n in range(kinds * 2):
            cols.append(moved[:, lanes(2 * n)])
            cols.append(jnp.where(moves, moved[:, lanes(2 * n + 1)], still[:, lanes(n)]))
        return jnp.concatenate(cols, axis=1)

    own = mix(moved_kv, jnp.concatenate([split_blocks(k1), split_blocks(v1)], axis=1), 2)
    left, right = both_ways(own, parts)
    query = mix(moved_q, split_blocks(q1), 1)
    out = attention(2, bits, query, own, left, right, first[:, : 4 * HEAD_DIM])

    back = exchange(out.reshape(parts, BLOCK // parts, -1))
    back = back.reshape(parts, BLOCK // parts, 2, 2 * HEAD_DIM).transpose(0, 2, 1, 3).reshape(2 * BLOCK, 2 * HEAD_DIM)
    still = jnp.concatenate([out[:, lanes(1)], out[:, lanes(3)]], axis=0)
    attn = jnp.concatenate([back[:, lanes(0)], jnp.where(moves, back[:, lanes(1)], still)], axis=1)
    mixed = lax.all_gather(attn, "head", axis=1, tiled=True)
    return projection(groups, order, spatial, mixed, weight_cols)


def solution(mesh):
    return jax.shard_map(
        body,
        mesh=mesh,
        in_specs=(P("ctx", "head"), P("ctx", "head"), P("ctx", "head"), P(), P(), P("ctx", "head")),
        out_specs=P("ctx", "head"),
        check_vma=False,
    )
```

time: 641 us -> 331 us (0.52)
  waiting for transfers between devices: 378 us -> 132 us
  blocking collectives: 147 us -> 0 us
  starting transfers between devices: 17.9 us -> 125 us
  matrix products: 22.9 us -> 0 us
  Pallas kernels: 0 us -> 22.5 us
  other arithmetic: 27.3 us -> 12.9 us
  local copies, waits for them, and re-layouts: 30.1 us -> 20 us
    psum x1 -> x0, waiting for transfers between devices: 202 us -> none  [broadcast(): return lax.psum(kept, axis)]
    all_to_all x3 -> x0, blocking collectives: 147 us -> none  [the longest x1 59.3 us: body(): lax.all_to_all(position_pieces(queries, parts), 'ctx', split_axis=0, conc...]
    ppermute x2 -> x19, starting transfers between devices: 7.86 us -> 73.6 us  [the longest x9 40.3 us: gathered(): lax.ppermute(x, 'ctx', [(i, i ^ unit * k) for i in range(count)])]
    all_gather x1, waiting for transfers between devices: 46.4 us -> 0.01 us  [body(): weight_cols = lax.all_gather(w_out, 'ctx', axis=0, tiled=True)]
    all_to_all x1 -> x3, starting transfers between devices: 9.69 us -> 51 us  [exchange(): return lax.all_to_all(x, 'ctx', 0, 0, tiled=True)]
    dot_general x13 -> x0, matrix products: 22.9 us -> none  [the longest x6 8.14 us: head_fn(): jnp.dot(weights.astype(jnp.bfloat16), valrow, preferred_element_type=jnp....]
    pallas_call x0 -> x3, Pallas kernels: none -> 22.5 us  [the longest x2 17.1 us: attention(): pl.pallas_call(lambda *refs: attention_kernel(heads, *refs), out_shape=ja...]
    slice x8 -> x10, local copies, waits for them, and re-layouts: 20.8 us -> 2.81 us  [the longest x1 1.08 us: body(): out = attention(2, bits, query, own, left, right, first[:, :4 * HEAD_DIM])]
  transfers between devices with their start and end apart: 6 -> 25, of which waited for: 6 -> 11; matrix products, arithmetic and copies ran while one was open for 11% -> 8% of each run, Pallas kernels for 0% -> 5%
where the time goes in v1:
time: 331 us; the launch traced here: 330 us
  waiting for transfers between devices  132 us (40%)
  starting transfers between devices  125 us (38%)
  Pallas kernels  22.5 us (7%)
  local copies, waits for them, and re-layouts  20 us (6%)
  between operations  18.3 us (6%)
  other arithmetic  12.9 us (4%)
    all_to_all x3, starting transfers between devices, exchange(): return lax.all_to_all(x, 'ctx', 0, 0, tiled=True)  51 us
    all_gather x1, waiting for transfers between devices, body(): mixed = lax.all_gather(attn, 'head', axis=1, tiled=True)  41.7 us
    ppermute x9, starting transfers between devices, gathered(): lax.ppermute(x, 'ctx', [(i, i ^ unit * k) for i in range(count)])  40.3 us
    all_to_all x3, waiting for transfers between devices, exchange(): return lax.all_to_all(x, 'ctx', 0, 0, tiled=True)  36.1 us
    ppermute x6, waiting for transfers between devices, scattered(): lax.ppermute(x[half:], 'ctx', [(i, i + step) for i in range(0, count, 2 *...  34 us
    ppermute x6, starting transfers between devices, scattered(): lax.ppermute(x[half:], 'ctx', [(i, i + step) for i in range(0, count, 2 *...  20.6 us
    pallas_call x2, Pallas kernels, attention(): pl.pallas_call(lambda *refs: attention_kernel(heads, *refs), out_shape=ja...  17.1 us
    unnamed x42, local copies, waits for them, and re-layouts  14.3 us
  transfers between devices with their start and end apart: 25, of which 11 were waited for; matrix products, arithmetic and copies ran while one was open for 8% of the time, Pallas kernels for 5%

profile of v1, /device:TPU:1, one launch (start us, length us, event | category | flops | bytes accessed | tf_op | source)
XLA Modules:
  0.0 330.1 jit_solution(266034570066210805)
XLA Ops:
  6.5 0.7 all-gather.8.cloned.1.call-update
  7.3 0.7 broadcast_compare_fusion.1
  8.2 0.7 fusion.15
  10.7 1.5 constant_dynamic-slice_fusion.9
  12.3 5.7 %collective-permute-start.2 = (bf16[256,512]{1,0:T(8,128)(2,1)S(1)}, bf16[256,512]{1,0:T(8,128)(2,1)S(1)}, u32[]{:S(2)}, u32[]{:S(2)}) collective-permute-start(bf16[256,512]{1,0:T(8,128)(2,1)S(1)} %pad_maximum_fusion.10), channel_id=1, source_target_pairs={{0,256},{1,257},{2,258},{3,259},{4,260},{5,261},{6,262},{7,263}} | collective-permute-start | bytes 786440 | tf_op jit(solution)/shard_map/ppermute | solution.py:152
  18.1 1.2 pad_maximum_fusion
  19.2 14.4 %all-to-all-start.1 = ((bf16[64,8,1024]{2,1,0:T(8,128)(2,1)}), bf16[64,8,1024]{2,1,0:T(8,128)(2,1)S(1)}, u32[]{:S(2)}, u32[]{:S(2)}) async-start(bf16[64,8,1024]{2,1,0:T(8,128)(2,1)} %pad_maximum_fusion), calls=%async_computation.1 | async-start | bytes 2097152 | tf_op jit(solution)/shard_map/all_to_all | solution.py:139
  33.8 2.9 collective-permute-start.3
  36.8 0.7 broadcast_compare_fusion
  37.5 1.2 collective-permute-done.3
  38.8 8.2 %collective-permute-start.4 = (bf16[64,512]{1,0:T(8,128)(2,1)S(1)}, bf16[64,512]{1,0:T(8,128)(2,1)S(1)}, u32[]{:S(2)}, u32[]{:S(2)}) collective-permute-start(bf16[64,512]{1,0:T(8,128)(2,1)S(1)} %slice.261), channel_id=1, source_target_pairs={{0,64},{128,192},{256,320},{384,448},{1,65},{129,193},{257,321},{3... | collective-permute-start | bytes 196616 | tf_op jit(solution)/shard_map/ppermute | solution.py:152
  47.0 29.0 %collective-permute-done.4 = bf16[64,512]{1,0:T(8,128)(2,1)S(1)} collective-permute-done((bf16[64,512]{1,0:T(8,128)(2,1)S(1)}, bf16[64,512]{1,0:T(8,128)(2,1)S(1)}, u32[]{:S(2)}, u32[]{:S(2)}) %collective-permute-start.4) | collective-permute-done | bytes 65568 | tf_op jit(solution)/shard_map/ppermute | solution.py:152
  76.0 1.3 collective-permute-start.5
  77.4 2.9 collective-permute-done.5
  80.4 1.3 collective-permute-start.6
  81.9 0.8 collective-permute-done.6
  82.7 1.3 collective-permute-start.7
  84.0 1.3 constant_dynamic-update-slice_fusion.5
  88.5 1.3 constant_dynamic-update-slice_fusion.16
  89.8 1.3 constant_dynamic-update-slice_fusion.3
  91.0 1.3 constant_dynamic-update-slice_fusion.14
  93.5 13.2 %collective-permute-start.10 = (bf16[8,768]{1,0:T(8,128)(2,1)S(1)}, bf16[8,768]{1,0:T(8,128)(2,1)S(1)}, u32[]{:S(2)}, u32[]{:S(2)}) collective-permute-start(bf16[8,768]{1,0:T(8,128)(2,1)S(1)} %get-tuple-element.63), channel_id=1, source_target_pairs={{0,96},{8,104},{16,112},{24,120},{32,64},{40,72},{48,80},{56,88},{... | collective-permute-start | bytes 36872 | tf_op jit(solution)/shard_map/ppermute | solution.py:160
  106.6 2.4 collective-permute-start.9
  109.0 6.5 %collective-permute-start.8 = (bf16[8,768]{1,0:T(8,128)(2,1)S(1)}, bf16[8,768]{1,0:T(8,128)(2,1)S(1)}, u32[]{:S(2)}, u32[]{:S(2)}) collective-permute-start(bf16[8,768]{1,0:T(8,128)(2,1)S(1)} %get-tuple-element.63), channel_id=1, source_target_pairs={{0,32},{8,40},{16,48},{24,56},{32,0},{40,8},{48,16},{56,24},{64,96... | collective-permute-start | bytes 36872 | tf_op jit(solution)/shard_map/ppermute | solution.py:160
  115.6 4.3 %collective-permute-done.9 = bf16[8,768]{1,0:T(8,128)(2,1)S(1)} collective-permute-done((bf16[8,768]{1,0:T(8,128)(2,1)S(1)}, bf16[8,768]{1,0:T(8,128)(2,1)S(1)}, u32[]{:S(2)}, u32[]{:S(2)}) %collective-permute-start.9) | collective-permute-done | bytes 12320 | tf_op jit(solution)/shard_map/ppermute | solution.py:160
  119.9 2.2 collective-permute-start.13
  122.2 4.2 %collective-permute-start.12 = (bf16[32,768]{1,0:T(8,128)(2,1)S(1)}, bf16[32,768]{1,0:T(8,128)(2,1)S(1)}, u32[]{:S(2)}, u32[]{:S(2)}) collective-permute-start(bf16[32,768]{1,0:T(8,128)(2,1)S(1)} %pad_maximum_fusion.13), channel_id=1, source_target_pairs={{0,16},{8,24},{16,0},{24,8},{32,48},{40,56},{48,32},{56,40},{64,80... | collective-permute-start | bytes 147464 | tf_op jit(solution)/shard_map/ppermute | solution.py:160
  126.3 2.9 collective-permute-start.11
  129.8 0.6 constant_dynamic-update-slice_fusion.10
  130.4 0.6 constant_dynamic-update-slice_fusion.9
  131.0 0.7 collective-permute-done.11
  131.7 0.6 constant_dynamic-update-slice_fusion.8
  132.4 0.6 constant_dynamic-update-slice_fusion.7
  133.0 0.6 constant_dynamic-update-slice_fusion.6
  133.6 2.7 collective-permute-start.14
  136.4 0.9 pad_maximum_fusion.2
  137.3 3.3 %collective-permute-start.16 = (bf16[128,768]{1,0:T(8,128)(2,1)}, bf16[128,768]{1,0:T(8,128)(2,1)S(1)}, u32[]{:S(2)}, u32[]{:S(2)}) collective-permute-start(bf16[128,768]{1,0:T(8,128)(2,1)} %get-tuple-element.49), channel_id=1, source_target_pairs={{0,384},{8,392},{16,400},{24,408},{32,416},{40,424},{48,432},{56,4... | collective-permute-start | bytes 589832 | tf_op jit(solution)/shard_map/ppermute | solution.py:160
  140.6 2.9 collective-permute-start.15
  143.6 12.2 %all-to-all-start = ((bf16[64,8,512]{2,1,0:T(8,128)(2,1)}), bf16[64,8,512]{2,1,0:T(8,128)(2,1)}, u32[]{:S(2)}, u32[]{:S(2)}) async-start(bf16[64,8,512]{2,1,0:T(8,128)(2,1)} %bitcast.6), calls=%async_computation | async-start | bytes 1048576 | tf_op jit(solution)/shard_map/all_to_all | solution.py:139
  156.2 1.0 fusion.2
  157.2 1.1 fusion.1
  158.4 1.3 collective-permute-start.1
  159.7 4.8 %collective-permute-start = (bf16[512,512]{1,0:T(8,128)(2,1)S(1)}, bf16[512,512]{1,0:T(8,128)(2,1)}, u32[]{:S(2)}, u32[]{:S(2)}) collective-permute-start(bf16[512,512]{1,0:T(8,128)(2,1)S(1)} %pad_maximum_fusion.1.refs_2_), channel_id=1, source_target_pairs={{0,8},{8,16},{16,24},{24,32},{32,40},{40,48},{48,56},{56,64},{64,7... | collective-permute-start | bytes 1572872 | tf_op jit(solution)/shard_map/ppermute | solution.py:143
  164.5 0.9 constant_dynamic-update-slice_fusion.19
  165.5 0.9 copy-done.7
  166.4 10.2 %all-to-all-done = bf16[64,8,512]{2,1,0:T(8,128)(2,1)} async-done(((bf16[64,8,512]{2,1,0:T(8,128)(2,1)}), bf16[64,8,512]{2,1,0:T(8,128)(2,1)}, u32[]{:S(2)}, u32[]{:S(2)}) %all-to-all-start) | async-done | bytes 524320 | tf_op jit(solution)/shard_map/all_to_all | solution.py:139
  176.6 2.1 fusion.13
  178.7 1.3 collective-permute-start.18
  180.0 5.3 %collective-permute-start.17 = (bf16[512,1024]{1,0:T(8,128)(2,1)S(1)}, bf16[512,1024]{1,0:T(8,128)(2,1)}, u32[]{:S(2)}, u32[]{:S(2)}) collective-permute-start(bf16[512,1024]{1,0:T(8,128)(2,1)S(1)} %get-tuple-element.15.refs_2_), channel_id=1, source_target_pairs={{0,8},{8,16},{16,24},{24,32},{32,40},{40,48},{48,56},{56,64},{64,7... | collective-permute-start | bytes 3145736 | tf_op jit(solution)/shard_map/ppermute | solution.py:143
  185.4 4.1 %collective-permute-done.1.refs_4_ = bf16[512,512]{1,0:T(8,128)(2,1)S(1)} collective-permute-done((bf16[512,512]{1,0:T(8,128)(2,1)S(1)}, bf16[512,512]{1,0:T(8,128)(2,1)S(1)}, u32[]{:S(2)}, u32[]{:S(2)}) %collective-permute-start.1) | collective-permute-done | bytes 524320 | tf_op jit(solution)/shard_map/ppermute | solution.py:144
  189.4 5.7 %shard_map.64 = bf16[512,256]{1,0:T(8,128)(2,1)S(1)} custom-call(s32[2,6]{1,0:T(2,128)S(1)} %add_convert_fusion.refs_0_, bf16[512,256]{1,0:T(8,128)(2,1)S(1)} %pad_maximum_fusion.11.refs_1_, bf16[512,512]{1,0:T(8,128)(2,1)S(1)} %pad_maximum_fusion.1.refs_2_, bf16[512,512]{1,0:T(8,128)(2,1)} %collective-permute-done.refs_3_, ...), custom_call_target="tpu_custom_call" | custom-call | flops 1610612736 | bytes 2097152 | tf_op jit(solution)/shard_map/pallas_call | solution.py:75
  195.2 0.7 pad_maximum_fusion.12
  195.9 1.1 slice.288.refs_5_
  197.1 10.1 %collective-permute-done.18.refs_4_ = bf16[512,1024]{1,0:T(8,128)(2,1)S(1)} collective-permute-done((bf16[512,1024]{1,0:T(8,128)(2,1)S(1)}, bf16[512,1024]{1,0:T(8,128)(2,1)S(1)}, u32[]{:S(2)}, u32[]{:S(2)}) %collective-permute-start.18) | collective-permute-done | bytes 1048608 | tf_op jit(solution)/shard_map/ppermute | solution.py:144
  207.2 11.5 %shard_map.65 = bf16[512,512]{1,0:T(8,128)(2,1)} custom-call(s32[2,6]{1,0:T(2,128)S(1)} %add_convert_fusion.refs_0_, bf16[512,512]{1,0:T(8,128)(2,1)S(1)} %pad_maximum_fusion.3.refs_1_, bf16[512,1024]{1,0:T(8,128)(2,1)S(1)} %get-tuple-element.15.refs_2_, bf16[512,1024]{1,0:T(8,128)(2,1)} %collective-permute-done.17.refs_3_, ...), custom_call_target="tpu_custom_call" | custom-call | flops 3221225472 | bytes 4194304 | tf_op jit(solution)/shard_map/pallas_call | solution.py:75
  218.6 24.4 %all-to-all-start.2 = ((bf16[64,8,512]{2,1,0:T(8,128)(2,1)}), bf16[64,8,512]{2,1,0:T(8,128)(2,1)S(1)}, u32[]{:S(2)}, u32[]{:S(2)}) async-start(bf16[64,8,512]{2,1,0:T(8,128)(2,1)} %bitcast.15), calls=%async_computation.2 | async-start | bytes 1048576 | tf_op jit(solution)/shard_map/all_to_all | solution.py:139
  243.1 1.0 fusion.12
  244.1 25.9 %all-to-all-done.2 = bf16[64,8,512]{2,1,0:T(8,128)(2,1)S(1)} async-done(((bf16[64,8,512]{2,1,0:T(8,128)(2,1)}), bf16[64,8,512]{2,1,0:T(8,128)(2,1)S(1)}, u32[]{:S(2)}, u32[]{:S(2)}) %all-to-all-start.2) | async-done | bytes 524320 | tf_op jit(solution)/shard_map/all_to_all | solution.py:139
  270.1 0.9 pad_maximum_fusion.6
  271.1 41.7 %all-gather.6.cloned.1.call-done.refs_2_ = bf16[1024,2048]{1,0:T(8,128)(2,1)} async-done(((bf16[1024,256]{1,0:T(8,128)(2,1)}), bf16[1024,2048]{1,0:T(8,128)(2,1)}) %all-gather.6.cloned.1.call-update) | async-done | bytes 4194320 | tf_op jit(solution)/shard_map/all_gather | solution.py:236
  312.7 2.2 copy-done
  314.9 1.7 copy-done.1
  316.6 1.6 copy-done.2
  318.2 5.4 %shard_map.66 = bf16[1024,384]{1,0:T(8,128)(2,1)} custom-call(s32[24]{0:T(128)S(1)} %add.105.refs_0_, bf16[1024,1024]{1,0:T(8,128)(2,1)S(1)} %copy-done.2, bf16[1024,2048]{1,0:T(8,128)(2,1)S(1)} %copy-done, bf16[3072,384]{1,0:T(8,128)(2,1)S(1)} %copy-done.1), custom_call_target="tpu_custom_call" | custom-call | tf_op jit(solution)/shard_map/pallas_call | solution.py:113
  (88 shorter events, 4.3 us)
Async XLA Ops:
  6.5 264.5 %all-gather.8.cloned.1.call-start = ((), (), s32[]{:S(2)}) async-start(), calls=%async_computation.5 | async-start | bytes 2396160 | tf_op jit(solution)/shard_map/all_gather | solution.py:179
  12.3 21.5 %collective-permute-start.2 = (bf16[256,512]{1,0:T(8,128)(2,1)S(1)}, bf16[256,512]{1,0:T(8,128)(2,1)S(1)}, u32[]{:S(2)}, u32[]{:S(2)}) collective-permute-start(bf16[256,512]{1,0:T(8,128)(2,1)S(1)} %pad_maximum_fusion.10), channel_id=1, source_target_pairs={{0,256},{1,257},{2,258},{3,259},{4,260},{5,261},{6,262},{7,263}} | collective-permute-start | bytes 786440 | tf_op jit(solution)/shard_map/ppermute | solution.py:152
  19.2 58.1 %copy-start.4 = (bf16[1024,384]{1,0:T(8,128)(2,1)S(1)}, bf16[1024,384]{1,0:T(8,128)(2,1)}, u32[]{:S(2)}) copy-start(bf16[1024,384]{1,0:T(8,128)(2,1)} %param.6) | copy-start | bytes 2359300
  19.2 124.3 %all-to-all-start.1 = ((bf16[64,8,1024]{2,1,0:T(8,128)(2,1)}), bf16[64,8,1024]{2,1,0:T(8,128)(2,1)S(1)}, u32[]{:S(2)}, u32[]{:S(2)}) async-start(bf16[64,8,1024]{2,1,0:T(8,128)(2,1)} %pad_maximum_fusion), calls=%async_computation.1 | async-start | bytes 2097152 | tf_op jit(solution)/shard_map/all_to_all | solution.py:139
  33.7 53.6 %copy-start.11 = (s32[24]{0:T(128)S(1)}, s32[24]{0:T(128)}, u32[]{:S(2)}) copy-start(s32[24]{0:T(128)} %param.10) | copy-start | bytes 292
  33.8 4.9 %collective-permute-start.3 = (bf16[128,512]{1,0:T(8,128)(2,1)S(1)}, bf16[128,512]{1,0:T(8,128)(2,1)S(1)}, u32[]{:S(2)}, u32[]{:S(2)}) collective-permute-start(bf16[128,512]{1,0:T(8,128)(2,1)S(1)} %slice.259), channel_id=1, source_target_pairs={{0,128},{256,384},{1,129},{257,385},{2,130},{258,386},{3,131},{259... | collective-permute-start | bytes 393224 | tf_op jit(solution)/shard_map/ppermute | solution.py:152
  38.8 37.2 %collective-permute-start.4 = (bf16[64,512]{1,0:T(8,128)(2,1)S(1)}, bf16[64,512]{1,0:T(8,128)(2,1)S(1)}, u32[]{:S(2)}, u32[]{:S(2)}) collective-permute-start(bf16[64,512]{1,0:T(8,128)(2,1)S(1)} %slice.261), channel_id=1, source_target_pairs={{0,64},{128,192},{256,320},{384,448},{1,65},{129,193},{257,321},{3... | collective-permute-start | bytes 196616 | tf_op jit(solution)/shard_map/ppermute | solution.py:152
  76.0 4.3 %collective-permute-start.5 = (bf16[32,512]{1,0:T(8,128)(2,1)S(1)}, bf16[32,512]{1,0:T(8,128)(2,1)S(1)}, u32[]{:S(2)}, u32[]{:S(2)}) collective-permute-start(bf16[32,512]{1,0:T(8,128)(2,1)S(1)} %slice.263), channel_id=1, source_target_pairs={{0,32},{64,96},{128,160},{192,224},{256,288},{320,352},{384,416},{... | collective-permute-start | bytes 98312 | tf_op jit(solution)/shard_map/ppermute | solution.py:152
  77.4 78.5 %copy-start.3 = (bf16[1024,384]{1,0:T(8,128)(2,1)S(1)}, bf16[1024,384]{1,0:T(8,128)(2,1)}, u32[]{:S(2)}) copy-start(bf16[1024,384]{1,0:T(8,128)(2,1)} %param.7) | copy-start | bytes 2359300
  80.4 2.3 collective-permute-start.6
  82.7 5.8 %collective-permute-start.7 = (bf16[8,512]{1,0:T(8,128)(2,1)S(1)}, bf16[8,512]{1,0:T(8,128)(2,1)S(1)}, u32[]{:S(2)}, u32[]{:S(2)}) collective-permute-start(bf16[8,512]{1,0:T(8,128)(2,1)S(1)} %slice.267), channel_id=1, source_target_pairs={{0,8},{16,24},{32,40},{48,56},{64,72},{80,88},{96,104},{112,120},{... | collective-permute-start | bytes 24584 | tf_op jit(solution)/shard_map/ppermute | solution.py:152
  93.5 22.1 %collective-permute-start.10 = (bf16[8,768]{1,0:T(8,128)(2,1)S(1)}, bf16[8,768]{1,0:T(8,128)(2,1)S(1)}, u32[]{:S(2)}, u32[]{:S(2)}) collective-permute-start(bf16[8,768]{1,0:T(8,128)(2,1)S(1)} %get-tuple-element.63), channel_id=1, source_target_pairs={{0,96},{8,104},{16,112},{24,120},{32,64},{40,72},{48,80},{56,88},{... | collective-permute-start | bytes 36872 | tf_op jit(solution)/shard_map/ppermute | solution.py:160
  106.6 13.3 %collective-permute-start.9 = (bf16[8,768]{1,0:T(8,128)(2,1)S(1)}, bf16[8,768]{1,0:T(8,128)(2,1)S(1)}, u32[]{:S(2)}, u32[]{:S(2)}) collective-permute-start(bf16[8,768]{1,0:T(8,128)(2,1)S(1)} %get-tuple-element.63), channel_id=1, source_target_pairs={{0,64},{8,72},{16,80},{24,88},{32,96},{40,104},{48,112},{56,120},{... | collective-permute-start | bytes 36872 | tf_op jit(solution)/shard_map/ppermute | solution.py:160
  109.0 10.9 %collective-permute-start.8 = (bf16[8,768]{1,0:T(8,128)(2,1)S(1)}, bf16[8,768]{1,0:T(8,128)(2,1)S(1)}, u32[]{:S(2)}, u32[]{:S(2)}) collective-permute-start(bf16[8,768]{1,0:T(8,128)(2,1)S(1)} %get-tuple-element.63), channel_id=1, source_target_pairs={{0,32},{8,40},{16,48},{24,56},{32,0},{40,8},{48,16},{56,24},{64,96... | collective-permute-start | bytes 36872 | tf_op jit(solution)/shard_map/ppermute | solution.py:160
  119.9 13.1 %collective-permute-start.13 = (bf16[32,768]{1,0:T(8,128)(2,1)S(1)}, bf16[32,768]{1,0:T(8,128)(2,1)S(1)}, u32[]{:S(2)}, u32[]{:S(2)}) collective-permute-start(bf16[32,768]{1,0:T(8,128)(2,1)S(1)} %pad_maximum_fusion.13), channel_id=1, source_target_pairs={{0,24},{8,16},{16,8},{24,0},{32,56},{40,48},{48,40},{56,32},{64,88... | collective-permute-start | bytes 147464 | tf_op jit(solution)/shard_map/ppermute | solution.py:160
  122.2 10.2 %collective-permute-start.12 = (bf16[32,768]{1,0:T(8,128)(2,1)S(1)}, bf16[32,768]{1,0:T(8,128)(2,1)S(1)}, u32[]{:S(2)}, u32[]{:S(2)}) collective-permute-start(bf16[32,768]{1,0:T(8,128)(2,1)S(1)} %pad_maximum_fusion.13), channel_id=1, source_target_pairs={{0,16},{8,24},{16,0},{24,8},{32,48},{40,56},{48,32},{56,40},{64,80... | collective-permute-start | bytes 147464 | tf_op jit(solution)/shard_map/ppermute | solution.py:160
  126.3 5.4 %collective-permute-start.11 = (bf16[32,768]{1,0:T(8,128)(2,1)S(1)}, bf16[32,768]{1,0:T(8,128)(2,1)S(1)}, u32[]{:S(2)}, u32[]{:S(2)}) collective-permute-start(bf16[32,768]{1,0:T(8,128)(2,1)S(1)} %pad_maximum_fusion.13), channel_id=1, source_target_pairs={{0,8},{8,0},{16,24},{24,16},{32,40},{40,32},{48,56},{56,48},{64,72... | collective-permute-start | bytes 147464 | tf_op jit(solution)/shard_map/ppermute | solution.py:160
  133.6 9.9 %collective-permute-start.14 = (bf16[128,768]{1,0:T(8,128)(2,1)}, bf16[128,768]{1,0:T(8,128)(2,1)S(1)}, u32[]{:S(2)}, u32[]{:S(2)}) collective-permute-start(bf16[128,768]{1,0:T(8,128)(2,1)} %get-tuple-element.49), channel_id=1, source_target_pairs={{0,128},{8,136},{16,144},{24,152},{32,160},{40,168},{48,176},{56,1... | collective-permute-start | bytes 589832 | tf_op jit(solution)/shard_map/ppermute | solution.py:160
  137.3 28.2 %collective-permute-start.16 = (bf16[128,768]{1,0:T(8,128)(2,1)}, bf16[128,768]{1,0:T(8,128)(2,1)S(1)}, u32[]{:S(2)}, u32[]{:S(2)}) collective-permute-start(bf16[128,768]{1,0:T(8,128)(2,1)} %get-tuple-element.49), channel_id=1, source_target_pairs={{0,384},{8,392},{16,400},{24,408},{32,416},{40,424},{48,432},{56,4... | collective-permute-start | bytes 589832 | tf_op jit(solution)/shard_map/ppermute | solution.py:160
  140.6 23.9 %collective-permute-start.15 = (bf16[128,768]{1,0:T(8,128)(2,1)}, bf16[128,768]{1,0:T(8,128)(2,1)}, u32[]{:S(2)}, u32[]{:S(2)}) collective-permute-start(bf16[128,768]{1,0:T(8,128)(2,1)} %get-tuple-element.49), channel_id=1, source_target_pairs={{0,256},{8,264},{16,272},{24,280},{32,288},{40,296},{48,304},{56,3... | collective-permute-start | bytes 589832 | tf_op jit(solution)/shard_map/ppermute | solution.py:160
  143.6 12.2 %copy-start.5 = (bf16[512,768]{1,0:T(8,128)(2,1)}, bf16[512,768]{1,0:T(8,128)(2,1)S(1)}, u32[]{:S(2)}) copy-start(bf16[512,768]{1,0:T(8,128)(2,1)S(1)} %constant_dynamic-update-slice_fusion.20) | copy-start | bytes 2359300
  143.6 33.0 %all-to-all-start = ((bf16[64,8,512]{2,1,0:T(8,128)(2,1)}), bf16[64,8,512]{2,1,0:T(8,128)(2,1)}, u32[]{:S(2)}, u32[]{:S(2)}) async-start(bf16[64,8,512]{2,1,0:T(8,128)(2,1)} %bitcast.6), calls=%async_computation | async-start | bytes 1048576 | tf_op jit(solution)/shard_map/all_to_all | solution.py:139
  155.8 115.3 %all-gather.4.cloned.1.call-start = ((), (), s32[]{:S(2)}) async-start(), calls=%async_computation.3 | async-start | bytes 2359296 | tf_op jit(solution)/shard_map/all_gather | solution.py:218
  155.9 8.6 %copy-start.6 = (bf16[512,768]{1,0:T(8,128)(2,1)S(1)}, bf16[512,768]{1,0:T(8,128)(2,1)}, u32[]{:S(2)}) copy-start(bf16[512,768]{1,0:T(8,128)(2,1)} %copy-done.5) | copy-start | bytes 2359300
  158.4 31.0 %collective-permute-start.1 = (bf16[512,512]{1,0:T(8,128)(2,1)S(1)}, bf16[512,512]{1,0:T(8,128)(2,1)S(1)}, u32[]{:S(2)}, u32[]{:S(2)}) collective-permute-start(bf16[512,512]{1,0:T(8,128)(2,1)S(1)} %pad_maximum_fusion.1.refs_2_), channel_id=1, source_target_pairs={{8,0},{16,8},{24,16},{32,24},{40,32},{48,40},{56,48},{64,56},{72,6... | collective-permute-start | bytes 1572872 | tf_op jit(solution)/shard_map/ppermute | solution.py:144
  159.7 29.7 %collective-permute-start = (bf16[512,512]{1,0:T(8,128)(2,1)S(1)}, bf16[512,512]{1,0:T(8,128)(2,1)}, u32[]{:S(2)}, u32[]{:S(2)}) collective-permute-start(bf16[512,512]{1,0:T(8,128)(2,1)S(1)} %pad_maximum_fusion.1.refs_2_), channel_id=1, source_target_pairs={{0,8},{8,16},{16,24},{24,32},{32,40},{40,48},{48,56},{56,64},{64,7... | collective-permute-start | bytes 1572872 | tf_op jit(solution)/shard_map/ppermute | solution.py:143
  165.5 0.9 copy-start.7
  178.7 28.4 %collective-permute-start.18 = (bf16[512,1024]{1,0:T(8,128)(2,1)S(1)}, bf16[512,1024]{1,0:T(8,128)(2,1)S(1)}, u32[]{:S(2)}, u32[]{:S(2)}) collective-permute-start(bf16[512,1024]{1,0:T(8,128)(2,1)S(1)} %get-tuple-element.15.refs_2_), channel_id=1, source_target_pairs={{8,0},{16,8},{24,16},{32,24},{40,32},{48,40},{56,48},{64,56},{72,6... | collective-permute-start | bytes 3145736 | tf_op jit(solution)/shard_map/ppermute | solution.py:144
  180.0 27.1 %collective-permute-start.17 = (bf16[512,1024]{1,0:T(8,128)(2,1)S(1)}, bf16[512,1024]{1,0:T(8,128)(2,1)}, u32[]{:S(2)}, u32[]{:S(2)}) collective-permute-start(bf16[512,1024]{1,0:T(8,128)(2,1)S(1)} %get-tuple-element.15.refs_2_), channel_id=1, source_target_pairs={{0,8},{8,16},{16,24},{24,32},{32,40},{40,48},{48,56},{56,64},{64,7... | collective-permute-start | bytes 3145736 | tf_op jit(solution)/shard_map/ppermute | solution.py:143
  195.1 1.9 copy-start.8
  195.1 1.9 copy-start.9
  195.1 1.9 copy-start.10
  218.6 51.4 %all-to-all-start.2 = ((bf16[64,8,512]{2,1,0:T(8,128)(2,1)}), bf16[64,8,512]{2,1,0:T(8,128)(2,1)S(1)}, u32[]{:S(2)}, u32[]{:S(2)}) async-start(bf16[64,8,512]{2,1,0:T(8,128)(2,1)} %bitcast.15), calls=%async_computation.2 | async-start | bytes 1048576 | tf_op jit(solution)/shard_map/all_to_all | solution.py:139
  243.1 69.7 %all-gather.6.cloned.1.call-start = ((), (), s32[]{:S(2)}) async-start(), calls=%async_computation.4 | async-start | bytes 4718592 | tf_op jit(solution)/shard_map/all_gather | solution.py:236
  312.7 2.2 copy-start
  314.9 1.7 copy-start.1
  316.6 1.6 copy-start.2
Sparse Core Ops, SparseCore 0:
  10.3 148.8 all-gather.7
  196.0 43.2 all-gather.3
  271.1 41.6 all-gather.5

commit v2 on v1

--- a/solution.py
+++ b/solution.py
@@ -92,31 +92,50 @@
     )(bits, query, own, left, right, first)
 
 
-def projection_kernel(groups, order, spatial_ref, mixed_ref, w_ref, out_ref):
-    total = None
+def spatial_kernel(groups, order, spatial_ref, w_ref, part_ref, mixed_w_ref):
+    def rows(g, slot):
+        return w_ref[pl.ds(pl.multiple_of(order[g * 3 + slot] * HEAD_DIM, HEAD_DIM), HEAD_DIM), :]
+
     for g in range(groups):
-        rows = [
-            w_ref[pl.ds(pl.multiple_of(order[g * 3 + slot] * HEAD_DIM, HEAD_DIM), HEAD_DIM), :] for slot in range(3)
-        ]
-        part = jnp.dot(
-            mixed_ref[:, 2 * g * HEAD_DIM : 2 * (g + 1) * HEAD_DIM],
-            jnp.concatenate(rows[:2], axis=0),
-            preferred_element_type=F32,
-        )
-        part += jnp.dot(spatial_ref[:, lanes(g)], rows[2], preferred_element_type=F32)
-        total = part if total is None else total + part
-    out_ref[...] = total.astype(BF)
-
-
-def projection(groups, order, spatial, mixed, w):
+        for slot in range(2):
+            mixed_w_ref[(2 * g + slot) * HEAD_DIM : (2 * g + slot + 1) * HEAD_DIM, :] = rows(g, slot)
+    chosen = jnp.concatenate([rows(g, 2) for g in range(groups)], axis=0)
+    part_ref[...] = jnp.dot(spatial_ref[...], chosen, preferred_element_type=F32)
+
+
+def spatial_projection(groups, order, spatial, w):
     vmem = pl.BlockSpec(memory_space=pltpu.VMEM)
     return pl.pallas_call(
-        lambda *refs: projection_kernel(groups, *refs),
-        out_shape=jax.ShapeDtypeStruct((spatial.shape[0], w.shape[1]), BF),
-        in_specs=[pl.BlockSpec(memory_space=pltpu.SMEM)] + [vmem] * 3,
-        out_specs=vmem,
+        lambda *refs: spatial_kernel(groups, *refs),
+        out_shape=(
+            jax.ShapeDtypeStruct((spatial.shape[0], w.shape[1]), F32),
+            jax.ShapeDtypeStruct((groups * 2 * HEAD_DIM, w.shape[1]), BF),
+        ),
+        in_specs=[pl.BlockSpec(memory_space=pltpu.SMEM)] + [vmem] * 2,
+        out_specs=(vmem, vmem),
         compiler_params=pltpu.CompilerParams(vmem_limit_bytes=40 << 20),
-    )(order, spatial, mixed, w)
+    )(order, spatial, w)
+
+
+def mixed_kernel(part_ref, mixed_ref, w_ref, out_ref):
+    out_ref[...] = (part_ref[...] + jnp.dot(mixed_ref[...], w_ref[...], preferred_element_type=F32)).astype(BF)
+
+
+def mixed_projection(part, mixed, w):
+    rows, cols = part.shape
+    tile = rows // 4
+    return pl.pallas_call(
+        mixed_kernel,
+        out_shape=jax.ShapeDtypeStruct((rows, cols), BF),
+        grid=(rows // tile,),
+        in_specs=[
+            pl.BlockSpec((tile, cols), lambda i: (i, 0)),
+            pl.BlockSpec((tile, mixed.shape[1]), lambda i: (i, 0)),
+            pl.BlockSpec(w.shape, lambda i: (0, 0)),
+        ],
+        out_specs=pl.BlockSpec((tile, cols), lambda i: (i, 0)),
+        compiler_params=pltpu.CompilerParams(vmem_limit_bytes=32 << 20),
+    )(part, mixed, w)
 
 
 def slots_of(labels):
@@ -145,20 +164,14 @@
     return left, right
 
 
-def scattered(x, place, count):
-    step = count // 2
-    while step >= 1:
+def scattered(x, place, steps):
+    count = lax.axis_size("ctx")
+    reach = count
+    for step in steps:
         half = x.shape[0] // 2
-        got = lax.ppermute(x[half:], "ctx", [(i, i + step) for i in range(0, count, 2 * step)])
-        x = jnp.where(place % (2 * step) == step, got, x[:half])
-        step //= 2
-    return x
-
-
-def gathered(x, count):
-    for unit in (4, 1, 16):
-        got = [lax.ppermute(x, "ctx", [(i, i ^ (unit * k)) for i in range(count)]) for k in (1, 2, 3)]
-        x = jnp.concatenate([x] + got, axis=0)
+        got = lax.ppermute(x[half:], "ctx", [(i, i + step) for i in range(0, count, reach)])
+        x = jnp.where(place % reach == step, got, x[:half])
+        reach = step
     return x
 
 
@@ -167,6 +180,9 @@
     groups = lax.axis_size("head")
     place = lax.axis_index("ctx")
     group = lax.axis_index("head")
+    deep = parts // 4
+    along_z = [[y * deep + z for z in range(deep)] for y in range(4)]
+    along_y = [[y * deep + z for y in range(4)] for z in range(deep)]
     slots = slots_of(head_labels.reshape(groups, 3))
     mine = lax.dynamic_slice_in_dim(slots, group, 1, 0)[0]
     labels = lax.dynamic_slice_in_dim(head_labels, group * 3, 3)
@@ -175,8 +191,6 @@
 
     def head_of(x, slot):
         return lax.dynamic_slice_in_dim(x, mine[slot] * HEAD_DIM, HEAD_DIM, 1)
-
-    weight_cols = lax.all_gather(w_out, "ctx", axis=0, tiled=True)
 
     q0, q1, q2 = (head_of(queries, s) for s in range(3))
     k0, k1, k2 = (head_of(keys, s) for s in range(3))
@@ -191,25 +205,41 @@
     first_bit = (index > REACH) & (rows[:, 0] == 1)
     bits = jnp.concatenate([hits, first_bit[:, None]], axis=1).astype(jnp.int32)
 
-    pack_k = position_pack(jnp.concatenate([k0, k1], axis=1), parts)
-    pack_v = position_pack(jnp.concatenate([v0, v1], axis=1), parts)
-    moved_kv = exchange(jnp.concatenate([pack_k, pack_v], axis=2)).reshape(BLOCK, -1)
-    moved_q = exchange(position_pack(jnp.concatenate([q0, q1], axis=1), parts)).reshape(BLOCK, -1)
-
-    local = jnp.concatenate([k0, k1, v0, v1], axis=1)[: BLOCK // parts]
-    shares = scattered(jnp.concatenate([k1, k2, v1, v2], axis=1)[:BLOCK], place, parts)
-    piece = jnp.concatenate(
+    shares = scattered(jnp.concatenate([k1, k2, v1, v2], axis=1)[:BLOCK], place, (2 * deep, deep, deep // 2, deep // 4))
+
+    packs = [position_pack(jnp.concatenate(pair, axis=1), parts) for pair in ((q0, q1), (k0, k1), (v0, v1))]
+    w_rows = w_out.shape[0] * w_out.shape[1] // HEAD_DIM
+    near = BLOCK // parts
+    share = shares.shape[0]
+    sent = jnp.concatenate(
+        [w_out[:, lanes(c)] for c in range(w_out.shape[1] // HEAD_DIM)]
+        + [x[:near] for x in (k0, k1, v0, v1)]
+        + [shares[:, lanes(c)] for c in range(4)],
+        axis=0,
+    )
+    packed, sent = lax.optimization_barrier((jnp.concatenate(packs, axis=2), sent))
+    moved = exchange(packed).reshape(BLOCK, -1)
+    moved_q, moved_kv = moved[:, : 4 * HEAD_DIM], moved[:, 4 * HEAD_DIM :]
+    rows_z = lax.all_gather(sent, "ctx", axis=0, axis_index_groups=along_z)
+    w_z = rows_z[:, :w_rows].reshape(deep, -1, w_out.shape[0], HEAD_DIM)
+    w_z = w_z.transpose(0, 2, 1, 3).reshape(deep * w_out.shape[0], -1)
+    weight_cols = lax.all_gather(w_z, "ctx", axis=0, axis_index_groups=along_y, tiled=True)
+    moving = [rows_z[:, w_rows + n * near : w_rows + (n + 1) * near].reshape(-1, HEAD_DIM) for n in range(4)]
+    base = w_rows + 4 * near
+    still = [rows_z[:: deep // 4, base + n * share : base + (n + 1) * share].reshape(-1, HEAD_DIM) for n in range(4)]
+    quarter = jnp.concatenate(
         [
-            local[:, lanes(0)],
-            jnp.where(moves, local[:, lanes(1)], shares[:, lanes(0)]),
-            local[:, lanes(2)],
-            jnp.where(moves, local[:, lanes(3)], shares[:, lanes(2)]),
-            shares[:, lanes(1)],
-            shares[:, lanes(3)],
+            moving[0],
+            jnp.where(moves, moving[1], still[0]),
+            moving[2],
+            jnp.where(moves, moving[3], still[2]),
+            still[1],
+            still[3],
         ],
         axis=1,
     )
-    first = gathered(piece, parts)
+    others = [lax.ppermute(quarter, "ctx", [(i, i ^ (deep * k)) for i in range(parts)]) for k in (1, 2, 3)]
+    first = jnp.concatenate([quarter] + others, axis=0)
 
     own2 = jnp.concatenate([split_blocks(k2), split_blocks(v2)], axis=1)
     left2, right2 = both_ways(own2, parts)
@@ -234,7 +264,8 @@
     still = jnp.concatenate([out[:, lanes(1)], out[:, lanes(3)]], axis=0)
     attn = jnp.concatenate([back[:, lanes(0)], jnp.where(moves, back[:, lanes(1)], still)], axis=1)
     mixed = lax.all_gather(attn, "head", axis=1, tiled=True)
-    return projection(groups, order, spatial, mixed, weight_cols)
+    part, mixed_w = spatial_projection(groups, order, spatial, weight_cols)
+    return mixed_projection(part, mixed, mixed_w)
 
 
 def solution(mesh):

time: 331 us -> 332 us (level)
  waiting for transfers between devices: 132 us -> 191 us
  starting transfers between devices: 125 us -> 67.7 us
    all_gather x1 -> x2, waiting for transfers between devices: 0.01 us -> 87.9 us  [the longest x1 87.9 us: body(): rows_z = lax.all_gather(sent, 'ctx', axis=0, axis_index_groups=along_z)]
    ppermute x15 -> x7, starting transfers between devices: 60.9 us -> 25.1 us  [the longest x4 16.2 us: scattered(): lax.ppermute(x[half:], 'ctx', [(i, i + step) for i in range(0, count, rea...]
    all_to_all x3 -> x2, starting transfers between devices: 51 us -> 31.8 us  [exchange(): return lax.all_to_all(x, 'ctx', 0, 0, tiled=True)]
    ppermute x15 -> x7, waiting for transfers between devices: 39 us -> 25.8 us  [the longest x3 21.1 us: body(): lax.ppermute(quarter, 'ctx', [(i, i ^ deep * k) for i in range(parts)])]
    all_to_all x3 -> x2, waiting for transfers between devices: 36.1 us -> 26.9 us  [exchange(): return lax.all_to_all(x, 'ctx', 0, 0, tiled=True)]
    all_gather x1, waiting for transfers between devices: 41.7 us -> 35.5 us  [body(): mixed = lax.all_gather(attn, 'head', axis=1, tiled=True)]
    unnamed x42 -> x40, local copies, waits for them, and re-layouts: 14.3 us -> 12 us
  transfers between devices with their start and end apart: 25 -> 17, of which waited for: 11 -> 12; matrix products, arithmetic and copies ran while one was open for 8% -> 7% of each run, Pallas kernels for 5% -> 5%
where the time goes in v2:
time: 332 us; the launch traced here: 330 us
  waiting for transfers between devices  191 us (58%)
  starting transfers between devices  67.7 us (20%)
  local copies, waits for them, and re-layouts  19.6 us (6%)
  Pallas kernels  19.5 us (6%)
  between operations  18 us (5%)
  other arithmetic  14.3 us (4%)
    all_gather x1, waiting for transfers between devices, body(): rows_z = lax.all_gather(sent, 'ctx', axis=0, axis_index_groups=along_z)  87.9 us
    all_gather x1, waiting for transfers between devices, body(): mixed = lax.all_gather(attn, 'head', axis=1, tiled=True)  35.5 us
    all_to_all x2, starting transfers between devices, exchange(): return lax.all_to_all(x, 'ctx', 0, 0, tiled=True)  31.8 us
    all_to_all x2, waiting for transfers between devices, exchange(): return lax.all_to_all(x, 'ctx', 0, 0, tiled=True)  26.9 us
    ppermute x3, waiting for transfers between devices, body(): lax.ppermute(quarter, 'ctx', [(i, i ^ deep * k) for i in range(parts)])  21.1 us
    ppermute x4, starting transfers between devices, scattered(): lax.ppermute(x[half:], 'ctx', [(i, i + step) for i in range(0, count, rea...  16.2 us
    pallas_call x2, Pallas kernels, attention(): pl.pallas_call(lambda *refs: attention_kernel(heads, *refs), out_shape=ja...  14 us
    ppermute x2, waiting for transfers between devices, both_ways(): right = lax.ppermute(x, 'ctx', [(i + 1, i) for i in range(count - 1)])  13.5 us
  transfers between devices with their start and end apart: 17, of which 12 were waited for; matrix products, arithmetic and copies ran while one was open for 7% of the time, Pallas kernels for 5%

profile of v2, /device:TPU:1, one launch (start us, length us, event | category | flops | bytes accessed | tf_op | source)
XLA Modules:
  0.0 330.3 jit_solution(484987520569829201)
XLA Ops:
  6.5 0.7 broadcast_compare_fusion.1
  7.2 0.1 eq.54
  7.4 0.7 fusion.13
  10.0 1.5 constant_dynamic-slice_fusion.13
  11.5 6.4 %collective-permute-start.2 = (bf16[256,512]{1,0:T(8,128)(2,1)S(1)}, bf16[256,512]{1,0:T(8,128)(2,1)}, u32[]{:S(2)}, u32[]{:S(2)}) collective-permute-start(bf16[256,512]{1,0:T(8,128)(2,1)S(1)} %pad_maximum_fusion.14), channel_id=1, source_target_pairs={{0,256},{1,257},{2,258},{3,259},{4,260},{5,261},{6,262},{7,263}} | collective-permute-start | bytes 786440 | tf_op jit(solution)/shard_map/ppermute | solution.py:172
  18.2 1.3 pad_maximum_fusion
  19.5 1.0 collective-permute-done.2
  20.6 1.3 collective-permute-start.3
  22.0 2.7 collective-permute-done.3
  24.7 7.2 %collective-permute-start.4 = (bf16[64,512]{1,0:T(8,128)(2,1)S(1)}, bf16[64,512]{1,0:T(8,128)(2,1)S(1)}, u32[]{:S(2)}, u32[]{:S(2)}) collective-permute-start(bf16[64,512]{1,0:T(8,128)(2,1)S(1)} %slice.298), channel_id=1, source_target_pairs={{0,64},{128,192},{256,320},{384,448},{1,65},{129,193},{257,321},{3... | collective-permute-start | bytes 196616 | tf_op jit(solution)/shard_map/ppermute | solution.py:172
  32.0 0.7 constant_dynamic-update-slice_fusion.5
  32.7 0.6 collective-permute-done.4
  33.3 1.3 collective-permute-start.5
  34.6 0.7 constant_dynamic-update-slice_fusion.4
  35.3 0.3 collective-permute-done.5
  35.7 0.6 copy-done.8
  36.3 16.0 %all-to-all-start = ((bf16[64,8,1536]{2,1,0:T(8,128)(2,1)}), bf16[64,8,1536]{2,1,0:T(8,128)(2,1)S(1)}, u32[]{:S(2)}, u32[]{:S(2)}) async-start(bf16[64,8,1536]{2,1,0:T(8,128)(2,1)} %pad_maximum_fusion), calls=%async_computation | async-start | bytes 3145728 | tf_op jit(solution)/shard_map/all_to_all | solution.py:158
  52.3 0.7 all-gather.12.cloned.1.call-update
  54.9 0.6 dynamic_slice.51
  56.2 0.7 broadcast_compare_fusion
  57.0 87.9 %all-gather.12.cloned.1.call-done = bf16[4864,128]{1,0:T(8,128)(2,1)} async-done(((bf16[304,128]{1,0:T(8,128)(2,1)}), bf16[4864,128]{1,0:T(8,128)(2,1)}) %all-gather.12.cloned.1.call-update) | async-done | bytes 1245200 | tf_op jit(solution)/shard_map/all_gather | solution.py:223
  145.0 1.1 slice.312
  146.1 0.4 copy.9
  146.4 0.9 copy.12
  147.4 1.4 constant_dynamic-update-slice_fusion.16
  148.8 1.4 fusion.9
  150.2 1.4 constant_dynamic-update-slice_fusion.15
  151.6 1.4 constant_dynamic-update-slice_fusion.14
  153.0 1.4 constant_dynamic-update-slice_fusion.13
  154.4 0.6 constant_dynamic-update-slice_fusion.12
  155.2 0.1 fusion.3
  155.3 1.0 fusion.2
  156.4 2.1 fusion.1
  158.5 1.3 collective-permute-start.1
  159.8 4.0 %collective-permute-start = (bf16[512,512]{1,0:T(8,128)(2,1)S(1)}, bf16[512,512]{1,0:T(8,128)(2,1)S(1)}, u32[]{:S(2)}, u32[]{:S(2)}) collective-permute-start(bf16[512,512]{1,0:T(8,128)(2,1)S(1)} %pad_maximum_fusion.4.refs_2_), channel_id=1, source_target_pairs={{0,8},{8,16},{16,24},{24,32},{32,40},{40,48},{48,56},{56,64},{64,7... | collective-permute-start | bytes 1572872 | tf_op jit(solution)/shard_map/ppermute | solution.py:162
  163.9 0.6 constant_dynamic-update-slice_fusion.11
  164.5 4.2 %collective-permute-start.8 = (bf16[128,768]{1,0:T(8,128)(2,1)}, bf16[128,768]{1,0:T(8,128)(2,1)S(1)}, u32[]{:S(2)}, u32[]{:S(2)}) collective-permute-start(bf16[128,768]{1,0:T(8,128)(2,1)} %constant_dynamic-update-slice_fusion.11), channel_id=1, source_target_pairs={{0,384},{8,392},{16,400},{24,408},{32,416},{40,424},{48,432},{56,4... | collective-permute-start | bytes 589832 | tf_op jit(solution)/shard_map/ppermute | solution.py:241
  168.7 1.9 collective-permute-start.7
  170.6 2.8 collective-permute-start.6
  173.5 0.2 fusion.8
  173.8 6.1 %collective-permute-done.8 = bf16[128,768]{1,0:T(8,128)(2,1)S(1)} collective-permute-done((bf16[128,768]{1,0:T(8,128)(2,1)}, bf16[128,768]{1,0:T(8,128)(2,1)S(1)}, u32[]{:S(2)}, u32[]{:S(2)}) %collective-permute-start.8) | collective-permute-done | bytes 196640 | tf_op jit(solution)/shard_map/ppermute | solution.py:241
  179.8 10.2 %collective-permute-done.7 = bf16[128,768]{1,0:T(8,128)(2,1)S(1)} collective-permute-done((bf16[128,768]{1,0:T(8,128)(2,1)}, bf16[128,768]{1,0:T(8,128)(2,1)S(1)}, u32[]{:S(2)}, u32[]{:S(2)}) %collective-permute-start.7) | collective-permute-done | bytes 196640 | tf_op jit(solution)/shard_map/ppermute | solution.py:241
  190.0 4.8 %collective-permute-done.6 = bf16[128,768]{1,0:T(8,128)(2,1)S(1)} collective-permute-done((bf16[128,768]{1,0:T(8,128)(2,1)}, bf16[128,768]{1,0:T(8,128)(2,1)S(1)}, u32[]{:S(2)}, u32[]{:S(2)}) %collective-permute-start.6) | collective-permute-done | bytes 196640 | tf_op jit(solution)/shard_map/ppermute | solution.py:241
  194.8 0.9 pad_maximum_fusion.10.refs_5_
  195.8 1.3 collective-permute-start.10
  197.1 4.1 %collective-permute-start.9 = (bf16[512,1024]{1,0:T(8,128)(2,1)S(1)}, bf16[512,1024]{1,0:T(8,128)(2,1)S(1)}, u32[]{:S(2)}, u32[]{:S(2)}) collective-permute-start(bf16[512,1024]{1,0:T(8,128)(2,1)S(1)} %get-tuple-element.19.refs_2_), channel_id=1, source_target_pairs={{0,8},{8,16},{16,24},{24,32},{32,40},{40,48},{48,56},{56,64},{64,7... | collective-permute-start | bytes 3145736 | tf_op jit(solution)/shard_map/ppermute | solution.py:162
  201.2 4.4 %shard_map.64 = bf16[512,256]{1,0:T(8,128)(2,1)S(1)} custom-call(s32[2,6]{1,0:T(2,128)S(1)} %add_convert_fusion.refs_0_, bf16[512,256]{1,0:T(8,128)(2,1)S(1)} %pad_maximum_fusion.15.refs_1_, bf16[512,512]{1,0:T(8,128)(2,1)S(1)} %pad_maximum_fusion.4.refs_2_, bf16[512,512]{1,0:T(8,128)(2,1)S(1)} %collective-permute-done.refs_3_, ...), custom_call_target="tpu_custom_call" | custom-call | flops 1610612736 | bytes 2097152 | tf_op jit(solution)/shard_map/pallas_call | solution.py:75
  205.6 0.7 pad_maximum_fusion.16
  206.4 1.1 pad_maximum_fusion.1.refs_5_
  207.4 1.1 pad_maximum_fusion.8.refs_1_
  208.5 13.5 %collective-permute-done.10.refs_4_ = bf16[512,1024]{1,0:T(8,128)(2,1)S(1)} collective-permute-done((bf16[512,1024]{1,0:T(8,128)(2,1)S(1)}, bf16[512,1024]{1,0:T(8,128)(2,1)S(1)}, u32[]{:S(2)}, u32[]{:S(2)}) %collective-permute-start.10) | collective-permute-done | bytes 1048608 | tf_op jit(solution)/shard_map/ppermute | solution.py:163
  222.0 0.9 collective-permute-done.9.refs_3_
  222.9 9.6 %shard_map.66 = bf16[512,512]{1,0:T(8,128)(2,1)} custom-call(s32[2,6]{1,0:T(2,128)S(1)} %add_convert_fusion.refs_0_, bf16[512,512]{1,0:T(8,128)(2,1)S(1)} %pad_maximum_fusion.8.refs_1_, bf16[512,1024]{1,0:T(8,128)(2,1)S(1)} %get-tuple-element.19.refs_2_, bf16[512,1024]{1,0:T(8,128)(2,1)S(1)} %collective-permute-done.9.refs_3_, ...), custom_call_target="tpu_custom_call" | custom-call | flops 3221225472 | bytes 4194304 | tf_op jit(solution)/shard_map/pallas_call | solution.py:75
  232.5 15.8 %all-to-all-start.1 = ((bf16[64,8,512]{2,1,0:T(8,128)(2,1)}), bf16[64,8,512]{2,1,0:T(8,128)(2,1)S(1)}, u32[]{:S(2)}, u32[]{:S(2)}) async-start(bf16[64,8,512]{2,1,0:T(8,128)(2,1)} %bitcast.25), calls=%async_computation.1 | async-start | bytes 1048576 | tf_op jit(solution)/shard_map/all_to_all | solution.py:158
  248.4 1.0 fusion.11
  249.4 26.9 %all-to-all-done.1 = bf16[64,8,512]{2,1,0:T(8,128)(2,1)S(1)} async-done(((bf16[64,8,512]{2,1,0:T(8,128)(2,1)}), bf16[64,8,512]{2,1,0:T(8,128)(2,1)S(1)}, u32[]{:S(2)}, u32[]{:S(2)}) %all-to-all-start.1) | async-done | bytes 524320 | tf_op jit(solution)/shard_map/all_to_all | solution.py:158
  276.3 0.1 fusion.10
  276.4 0.9 pad_maximum_fusion.9
  277.4 1.7 copy-done.1
  279.0 1.6 copy-done.2
  280.6 1.9 shard_map.65
  282.5 35.5 %all-gather.10.cloned.1.call-done.mixed_ref = bf16[1024,2048]{1,0:T(8,128)(2,1)} async-done(((bf16[1024,256]{1,0:T(8,128)(2,1)}), bf16[1024,2048]{1,0:T(8,128)(2,1)}) %all-gather.10.cloned.1.call-update) | async-done | bytes 4194320 | tf_op jit(solution)/shard_map/all_gather | solution.py:266
  318.0 2.2 copy-done
  320.2 3.5 %shard_map.67 = bf16[1024,384]{1,0:T(8,128)(2,1)} custom-call(f32[1024,384]{1,0:T(8,128)S(1)} %get-tuple-element.10.part_ref, bf16[1024,2048]{1,0:T(8,128)(2,1)S(1)} %copy-done, bf16[2048,384]{1,0:T(8,128)(2,1)S(1)} %get-tuple-element.12.w_ref), custom_call_target="tpu_custom_call" | custom-call | tf_op jit(solution)/shard_map/pallas_call | solution.py:127
  (69 shorter events, 1.5 us)
Async XLA Ops:
  9.9 8.0 %copy-start.9 = (bf16[48,384]{1,0:T(8,128)(2,1)S(1)}, bf16[48,384]{1,0:T(8,128)(2,1)}, u32[]{:S(2)}) copy-start(bf16[48,384]{1,0:T(8,128)(2,1)} %param.11) | copy-start | bytes 110596
  10.0 8.0 %copy-start.4 = (bf16[1024,384]{1,0:T(8,128)(2,1)S(1)}, bf16[1024,384]{1,0:T(8,128)(2,1)}, u32[]{:S(2)}) copy-start(bf16[1024,384]{1,0:T(8,128)(2,1)} %param.6) | copy-start | bytes 2359300
  11.5 9.0 %collective-permute-start.2 = (bf16[256,512]{1,0:T(8,128)(2,1)S(1)}, bf16[256,512]{1,0:T(8,128)(2,1)}, u32[]{:S(2)}, u32[]{:S(2)}) collective-permute-start(bf16[256,512]{1,0:T(8,128)(2,1)S(1)} %pad_maximum_fusion.14), channel_id=1, source_target_pairs={{0,256},{1,257},{2,258},{3,259},{4,260},{5,261},{6,262},{7,263}} | collective-permute-start | bytes 786440 | tf_op jit(solution)/shard_map/ppermute | solution.py:172
  19.5 2.4 copy-start.3
  20.6 4.1 %collective-permute-start.3 = (bf16[128,512]{1,0:T(8,128)(2,1)S(1)}, bf16[128,512]{1,0:T(8,128)(2,1)S(1)}, u32[]{:S(2)}, u32[]{:S(2)}) collective-permute-start(bf16[128,512]{1,0:T(8,128)(2,1)S(1)} %slice.296), channel_id=1, source_target_pairs={{0,128},{256,384},{1,129},{257,385},{2,130},{258,386},{3,131},{259... | collective-permute-start | bytes 393224 | tf_op jit(solution)/shard_map/ppermute | solution.py:172
  24.7 8.5 %collective-permute-start.4 = (bf16[64,512]{1,0:T(8,128)(2,1)S(1)}, bf16[64,512]{1,0:T(8,128)(2,1)S(1)}, u32[]{:S(2)}, u32[]{:S(2)}) collective-permute-start(bf16[64,512]{1,0:T(8,128)(2,1)S(1)} %slice.298), channel_id=1, source_target_pairs={{0,64},{128,192},{256,320},{384,448},{1,65},{129,193},{257,321},{3... | collective-permute-start | bytes 196616 | tf_op jit(solution)/shard_map/ppermute | solution.py:172
  33.3 2.3 collective-permute-start.5
  35.7 0.6 copy-start.8
  35.7 19.3 %copy-start.10 = (s32[24]{0:T(128)S(1)}, s32[24]{0:T(128)}, u32[]{:S(2)}) copy-start(s32[24]{0:T(128)} %param.10) | copy-start | bytes 292
  36.3 118.7 %all-to-all-start = ((bf16[64,8,1536]{2,1,0:T(8,128)(2,1)}), bf16[64,8,1536]{2,1,0:T(8,128)(2,1)S(1)}, u32[]{:S(2)}, u32[]{:S(2)}) async-start(bf16[64,8,1536]{2,1,0:T(8,128)(2,1)} %pad_maximum_fusion), calls=%async_computation | async-start | bytes 3145728 | tf_op jit(solution)/shard_map/all_to_all | solution.py:158
  52.3 92.7 %all-gather.12.cloned.1.call-start = ((), (), s32[]{:S(2)}) async-start(), calls=%async_computation.5 | async-start | bytes 1323008 | tf_op jit(solution)/shard_map/all_gather | solution.py:223
  53.0 224.3 %all-gather.8.cloned.1.call-start = ((), (), s32[]{:S(2)}) async-start(), calls=%async_computation.3 | async-start | bytes 2949120 | tf_op jit(solution)/shard_map/all_gather | solution.py:226
  147.4 130.0 %all-gather.6.cloned.1.call-start = ((), (), s32[]{:S(2)}) async-start(), calls=%async_computation.2 | async-start | bytes 2359296 | tf_op jit(solution)/shard_map/all_gather | solution.py:248
  156.3 7.5 %copy-start.7 = (bf16[4,32,128]{2,1,0:T(8,128)(2,1)S(1)}, bf16[4,32,128]{2,1,0:T(8,128)(2,1)}, u32[]{:S(2)}) copy-start(bf16[4,32,128]{2,1,0:T(8,128)(2,1)} %get-tuple-element.24) | copy-start | bytes 98308
  158.5 42.7 %collective-permute-start.1 = (bf16[512,512]{1,0:T(8,128)(2,1)S(1)}, bf16[512,512]{1,0:T(8,128)(2,1)S(1)}, u32[]{:S(2)}, u32[]{:S(2)}) collective-permute-start(bf16[512,512]{1,0:T(8,128)(2,1)S(1)} %pad_maximum_fusion.4.refs_2_), channel_id=1, source_target_pairs={{8,0},{16,8},{24,16},{32,24},{40,32},{48,40},{56,48},{64,56},{72,6... | collective-permute-start | bytes 1572872 | tf_op jit(solution)/shard_map/ppermute | solution.py:163
  159.8 41.4 %collective-permute-start = (bf16[512,512]{1,0:T(8,128)(2,1)S(1)}, bf16[512,512]{1,0:T(8,128)(2,1)S(1)}, u32[]{:S(2)}, u32[]{:S(2)}) collective-permute-start(bf16[512,512]{1,0:T(8,128)(2,1)S(1)} %pad_maximum_fusion.4.refs_2_), channel_id=1, source_target_pairs={{0,8},{8,16},{16,24},{24,32},{32,40},{40,48},{48,56},{56,64},{64,7... | collective-permute-start | bytes 1572872 | tf_op jit(solution)/shard_map/ppermute | solution.py:162
  164.5 15.4 %collective-permute-start.8 = (bf16[128,768]{1,0:T(8,128)(2,1)}, bf16[128,768]{1,0:T(8,128)(2,1)S(1)}, u32[]{:S(2)}, u32[]{:S(2)}) collective-permute-start(bf16[128,768]{1,0:T(8,128)(2,1)} %constant_dynamic-update-slice_fusion.11), channel_id=1, source_target_pairs={{0,384},{8,392},{16,400},{24,408},{32,416},{40,424},{48,432},{56,4... | collective-permute-start | bytes 589832 | tf_op jit(solution)/shard_map/ppermute | solution.py:241
  168.7 21.3 %collective-permute-start.7 = (bf16[128,768]{1,0:T(8,128)(2,1)}, bf16[128,768]{1,0:T(8,128)(2,1)S(1)}, u32[]{:S(2)}, u32[]{:S(2)}) collective-permute-start(bf16[128,768]{1,0:T(8,128)(2,1)} %constant_dynamic-update-slice_fusion.11), channel_id=1, source_target_pairs={{0,256},{8,264},{16,272},{24,280},{32,288},{40,296},{48,304},{56,3... | collective-permute-start | bytes 589832 | tf_op jit(solution)/shard_map/ppermute | solution.py:241
  170.6 24.2 %collective-permute-start.6 = (bf16[128,768]{1,0:T(8,128)(2,1)}, bf16[128,768]{1,0:T(8,128)(2,1)S(1)}, u32[]{:S(2)}, u32[]{:S(2)}) collective-permute-start(bf16[128,768]{1,0:T(8,128)(2,1)} %constant_dynamic-update-slice_fusion.11), channel_id=1, source_target_pairs={{0,128},{8,136},{16,144},{24,152},{32,160},{40,168},{48,176},{56,1... | collective-permute-start | bytes 589832 | tf_op jit(solution)/shard_map/ppermute | solution.py:241
  190.0 5.8 %copy-start.5 = (bf16[128,768]{1,0:T(8,128)(2,1)}, bf16[128,768]{1,0:T(8,128)(2,1)S(1)}, u32[]{:S(2)}) copy-start(bf16[128,768]{1,0:T(8,128)(2,1)S(1)} %collective-permute-done.7) | copy-start | bytes 589828
  194.8 0.9 copy-start.6
  195.8 26.2 %collective-permute-start.10 = (bf16[512,1024]{1,0:T(8,128)(2,1)S(1)}, bf16[512,1024]{1,0:T(8,128)(2,1)S(1)}, u32[]{:S(2)}, u32[]{:S(2)}) collective-permute-start(bf16[512,1024]{1,0:T(8,128)(2,1)S(1)} %get-tuple-element.19.refs_2_), channel_id=1, source_target_pairs={{8,0},{16,8},{24,16},{32,24},{40,32},{48,40},{56,48},{64,56},{72,6... | collective-permute-start | bytes 3145736 | tf_op jit(solution)/shard_map/ppermute | solution.py:163
  197.1 25.8 %collective-permute-start.9 = (bf16[512,1024]{1,0:T(8,128)(2,1)S(1)}, bf16[512,1024]{1,0:T(8,128)(2,1)S(1)}, u32[]{:S(2)}, u32[]{:S(2)}) collective-permute-start(bf16[512,1024]{1,0:T(8,128)(2,1)S(1)} %get-tuple-element.19.refs_2_), channel_id=1, source_target_pairs={{0,8},{8,16},{16,24},{24,32},{32,40},{40,48},{48,56},{56,64},{64,7... | collective-permute-start | bytes 3145736 | tf_op jit(solution)/shard_map/ppermute | solution.py:162
  232.5 43.7 %all-to-all-start.1 = ((bf16[64,8,512]{2,1,0:T(8,128)(2,1)}), bf16[64,8,512]{2,1,0:T(8,128)(2,1)S(1)}, u32[]{:S(2)}, u32[]{:S(2)}) async-start(bf16[64,8,512]{2,1,0:T(8,128)(2,1)} %bitcast.25), calls=%async_computation.1 | async-start | bytes 1048576 | tf_op jit(solution)/shard_map/all_to_all | solution.py:158
  248.3 69.7 %all-gather.10.cloned.1.call-start = ((), (), s32[]{:S(2)}) async-start(), calls=%async_computation.4 | async-start | bytes 4718592 | tf_op jit(solution)/shard_map/all_gather | solution.py:266
  277.3 1.7 copy-start.1
  279.0 1.6 copy-start.2
  318.0 2.2 copy-start
Sparse Core Ops, SparseCore 0:
  55.2 89.7 all-gather.11
  147.5 56.7 all-gather.7
  206.5 49.9 all-gather.5
  277.4 40.6 all-gather.9

commit v3 on v2

v3 whole, which is shorter than its diff:
```python
import math

import jax
import jax.numpy as jnp
from jax import lax
from jax.experimental import pallas as pl
from jax.experimental.pallas import tpu as pltpu
from jax.sharding import PartitionSpec as P

HEAD_DIM = 128
BLOCK = 512
REACH = 2
BF = jnp.bfloat16
F32 = jnp.float32
RATE = math.log2(math.e) / math.sqrt(HEAD_DIM)
SPAN = 2 * REACH + 1


def lanes(index):
    return slice(index * HEAD_DIM, (index + 1) * HEAD_DIM)


VMEM = pl.BlockSpec(memory_space=pltpu.VMEM)
SMEM = pl.BlockSpec(memory_space=pltpu.SMEM)


def near_kernel(heads, bits, q_ref, own_ref, left_ref, right_ref, acc_ref, stat_ref, s_ref, m_ref, l_ref):
    sides = (left_ref, left_ref, own_ref, own_ref, right_ref, right_ref)

    def tile(kind, place, slot):
        return sides[place][:, lanes((kind * 2 + place % 2) * heads + slot)]

    for slot in range(heads):
        for b in range(2):
            here = lanes(b * heads + slot)
            query = q_ref[:, here]
            m_ref[...] = jnp.full_like(m_ref, -jnp.inf)
            l_ref[...] = jnp.zeros_like(l_ref)
            acc_ref[:, here] = jnp.zeros_like(m_ref)
            for n in range(SPAN):

                @pl.when(bits[b, n] > 0)
                def _():
                    s = lax.dot_general(
                        query, tile(0, b + n, slot), (((1,), (1,)), ((), ())), preferred_element_type=F32
                    )
                    s_ref[n] = s
                    m = m_ref[...]
                    for c in range(BLOCK // HEAD_DIM):
                        m = jnp.maximum(m, s[:, lanes(c)])
                    m_ref[...] = m

            m_ref[...] = jnp.broadcast_to(jnp.max(m_ref[...], axis=1, keepdims=True), m_ref.shape)
            for n in range(SPAN):

                @pl.when(bits[b, n] > 0)
                def _():
                    peak = m_ref[...]
                    total = l_ref[...]
                    parts = []
                    for c in range(BLOCK // HEAD_DIM):
                        w = jnp.exp2((s_ref[n, :, lanes(c)] - peak) * RATE)
                        total = total + w
                        parts.append(w.astype(BF))
                    l_ref[...] = total
                    acc_ref[:, here] += jnp.dot(
                        jnp.concatenate(parts, axis=1), tile(1, b + n, slot), preferred_element_type=F32
                    )

            total = jnp.sum(l_ref[...], axis=1, keepdims=True)
            lane = lax.broadcasted_iota(jnp.int32, m_ref.shape, 1)
            stat_ref[:, here] = jnp.where(lane < HEAD_DIM // 2, m_ref[...], total)


def near_attention(heads, bits, query, own, left, right):
    state = jax.ShapeDtypeStruct(query.shape, F32)
    pairs = heads * 2 * SPAN
    return pl.pallas_call(
        lambda *refs: near_kernel(heads, *refs),
        out_shape=(state, state),
        in_specs=[SMEM] + [VMEM] * 4,
        out_specs=(VMEM, VMEM),
        scratch_shapes=[
            pltpu.VMEM((SPAN, BLOCK, BLOCK), F32),
            pltpu.VMEM((BLOCK, HEAD_DIM), F32),
            pltpu.VMEM((BLOCK, HEAD_DIM), F32),
        ],
        compiler_params=pltpu.CompilerParams(vmem_limit_bytes=32 << 20),
        cost_estimate=pl.CostEstimate(
            flops=pairs * 4 * BLOCK * BLOCK * HEAD_DIM,
            bytes_accessed=heads * 16 * BLOCK * HEAD_DIM * 2,
            transcendentals=pairs * BLOCK * BLOCK,
        ),
    )(bits, query, own, left, right)


def first_kernel(bits, qm_ref, am_ref, sm_ref, qs_ref, as_ref, ss_ref, f0, f1, f2, f3, outm_ref, outs_ref):
    quarters = (f0, f1, f2, f3)

    def block(column):
        return jnp.concatenate([f[:, lanes(column)] for f in quarters], axis=0)

    for slot in range(3):
        heads = 1 if slot == 2 else 2
        q_ref, acc_ref, stat_ref, out_ref = (
            (qs_ref, as_ref, ss_ref, outs_ref) if slot == 2 else (qm_ref, am_ref, sm_ref, outm_ref)
        )
        key, val = ((0, 2), (1, 3), (4, 5))[slot]
        for b in range(2):
            here = lanes(b * heads + slot % 2)
            start = here.start
            total = stat_ref[:, start + HEAD_DIM - 1 : start + HEAD_DIM]

            @pl.when(bits[b, SPAN] > 0)
            def _():
                peak = stat_ref[:, start : start + 1]
                s = lax.dot_general(q_ref[:, here], block(key), (((1,), (1,)), ((), ())), preferred_element_type=F32)
                top = jnp.maximum(peak, jnp.max(s, axis=1, keepdims=True))
                keep = jnp.exp2((peak - top) * RATE)
                w = jnp.exp2((s - top) * RATE)
                mixed = acc_ref[:, here] * keep + jnp.dot(w.astype(BF), block(val), preferred_element_type=F32)
                out_ref[:, here] = (mixed / (total * keep + jnp.sum(w, axis=1, keepdims=True))).astype(BF)

            @pl.when(bits[b, SPAN] <= 0)
            def _():
                out_ref[:, here] = (acc_ref[:, here] / total).astype(BF)


def first_attention(bits, mixed, spatial, first):
    pairs = 6
    return pl.pallas_call(
        first_kernel,
        out_shape=(jax.ShapeDtypeStruct(mixed[0].shape, BF), jax.ShapeDtypeStruct(spatial[0].shape, BF)),
        in_specs=[SMEM] + [VMEM] * 10,
        out_specs=(VMEM, VMEM),
        compiler_params=pltpu.CompilerParams(vmem_limit_bytes=32 << 20),
        cost_estimate=pl.CostEstimate(
            flops=pairs * 4 * BLOCK * BLOCK * HEAD_DIM,
            bytes_accessed=pairs * 8 * BLOCK * HEAD_DIM * 2,
            transcendentals=pairs * BLOCK * BLOCK,
        ),
    )(bits, *mixed, *spatial, *first)


def unpack_kernel(moves, x_ref, quarter_ref, w_ref):
    deep = x_ref.shape[0]
    blocks = w_ref.shape[1] // HEAD_DIM
    rows = w_ref.shape[0] // deep
    base = blocks * rows
    near = BLOCK // 4 // deep
    share = BLOCK // 16
    for z in range(deep):
        for c in range(blocks):
            w_ref[z * rows : (z + 1) * rows, lanes(c)] = x_ref[z, c * rows : (c + 1) * rows, :]
    pairs = [x_ref[z, base : base + 4 * near, :].astype(F32) for z in range(deep)]
    moving = [
        jnp.concatenate([pair[n * near : (n + 1) * near] for pair in pairs], axis=0).astype(BF) for n in range(4)
    ]
    base += 4 * near
    still = [
        jnp.concatenate(
            [x_ref[z, base + n * share : base + (n + 1) * share, :] for z in range(0, deep, deep // 4)], axis=0
        )
        for n in range(4)
    ]
    flag = moves[0] > 0
    quarter_ref[:, lanes(0)] = moving[0]
    quarter_ref[:, lanes(2)] = moving[2]
    quarter_ref[:, lanes(4)] = still[1]
    quarter_ref[:, lanes(5)] = still[3]
    quarter_ref[:, lanes(1)] = jnp.where(flag, moving[1].astype(F32), still[0].astype(F32)).astype(BF)
    quarter_ref[:, lanes(3)] = jnp.where(flag, moving[3].astype(F32), still[2].astype(F32)).astype(BF)


def unpack(moves, x, w_rows, w_cols):
    return pl.pallas_call(
        unpack_kernel,
        out_shape=(
            jax.ShapeDtypeStruct((BLOCK // 4, 6 * HEAD_DIM), BF),
            jax.ShapeDtypeStruct((w_rows, w_cols), BF),
        ),
        in_specs=[SMEM, VMEM],
        out_specs=(VMEM, VMEM),
        compiler_params=pltpu.CompilerParams(vmem_limit_bytes=16 << 20),
    )(moves.astype(jnp.int32).reshape(1), x)


def spatial_kernel(groups, order, spatial_ref, w0, w1, w2, w3, part_ref, mixed_w_ref, w_ref):
    quarter = w0.shape[0]
    for k, w in enumerate((w0, w1, w2, w3)):
        at = jnp.bitwise_xor(order[groups * 3], k) * quarter
        w_ref[pl.ds(pl.multiple_of(at, HEAD_DIM), quarter), :] = w[...]

    def rows(g, slot):
        return w_ref[pl.ds(pl.multiple_of(order[g * 3 + slot] * HEAD_DIM, HEAD_DIM), HEAD_DIM), :]

    for g in range(groups):
        for slot in range(2):
            mixed_w_ref[(2 * g + slot) * HEAD_DIM : (2 * g + slot + 1) * HEAD_DIM, :] = rows(g, slot)
    chosen = jnp.concatenate([rows(g, 2) for g in range(groups)], axis=0)
    part_ref[...] = jnp.dot(spatial_ref[...], chosen, preferred_element_type=F32)


def spatial_projection(groups, order, spatial, w):
    rows, cols = w[0].shape
    return pl.pallas_call(
        lambda *refs: spatial_kernel(groups, *refs),
        out_shape=(
            jax.ShapeDtypeStruct((spatial.shape[0], cols), F32),
            jax.ShapeDtypeStruct((groups * 2 * HEAD_DIM, cols), BF),
        ),
        in_specs=[SMEM] + [VMEM] * 5,
        out_specs=(VMEM, VMEM),
        scratch_shapes=[pltpu.VMEM((4 * rows, cols), BF)],
        compiler_params=pltpu.CompilerParams(vmem_limit_bytes=32 << 20),
    )(order, spatial, *w)


def mixed_kernel(part_ref, mixed_ref, w_ref, out_ref):
    out_ref[...] = (part_ref[...] + jnp.dot(mixed_ref[...], w_ref[...], preferred_element_type=F32)).astype(BF)


def mixed_projection(part, mixed, w):
    rows, cols = part.shape
    tile = rows // 4
    return pl.pallas_call(
        mixed_kernel,
        out_shape=jax.ShapeDtypeStruct((rows, cols), BF),
        grid=(rows // tile,),
        in_specs=[
            pl.BlockSpec((tile, cols), lambda i: (i, 0)),
            pl.BlockSpec((tile, mixed.shape[1]), lambda i: (i, 0)),
            pl.BlockSpec(w.shape, lambda i: (0, 0)),
        ],
        out_specs=pl.BlockSpec((tile, cols), lambda i: (i, 0)),
        compiler_params=pltpu.CompilerParams(vmem_limit_bytes=32 << 20),
    )(part, mixed, w)


def slots_of(labels):
    temporal = labels == 1
    a = jnp.where(temporal[:, 0], 0, jnp.where(temporal[:, 1], 1, 2))
    c = jnp.where(~temporal[:, 2], 2, jnp.where(~temporal[:, 1], 1, 0))
    return jnp.stack([a, 3 - a - c, c], axis=1).astype(jnp.int32)


def split_blocks(x):
    return jnp.concatenate([x[:BLOCK], x[BLOCK:]], axis=1)


def position_pack(x, parts):
    rows = x.shape[0] // parts // 2
    return x.reshape(parts, 2, rows, x.shape[1]).transpose(0, 2, 1, 3).reshape(parts, rows, 2 * x.shape[1])


def exchange(x):
    return lax.all_to_all(x, "ctx", 0, 0, tiled=True)


def both_ways(x, count):
    left = lax.ppermute(x, "ctx", [(i, i + 1) for i in range(count - 1)])
    right = lax.ppermute(x, "ctx", [(i + 1, i) for i in range(count - 1)])
    return left, right


def scattered(x, place, steps):
    count = lax.axis_size("ctx")
    reach = count
    for step in steps:
        half = x.shape[0] // 2
        got = lax.ppermute(x[half:], "ctx", [(i, i + step) for i in range(0, count, reach)])
        x = jnp.where(place % reach == step, got, x[:half])
        reach = step
    return x


def body(queries, keys, values, block_mask, head_labels, w_out):
    parts = lax.axis_size("ctx")
    groups = lax.axis_size("head")
    place = lax.axis_index("ctx")
    group = lax.axis_index("head")
    deep = parts // 4
    along_z = [[y * deep + z for z in range(deep)] for y in range(4)]
    slots = slots_of(head_labels.reshape(groups, 3))
    mine = lax.dynamic_slice_in_dim(slots, group, 1, 0)[0]
    labels = lax.dynamic_slice_in_dim(head_labels, group * 3, 3)
    moves = lax.dynamic_slice_in_dim(labels, mine[1], 1)[0] == 1
    order = (slots + 3 * jnp.arange(groups, dtype=jnp.int32)[:, None]).reshape(-1)
    order = jnp.concatenate([order, (place // deep)[None].astype(jnp.int32)])

    def head_of(x, slot):
        return lax.dynamic_slice_in_dim(x, mine[slot] * HEAD_DIM, HEAD_DIM, 1)

    q0, q1, q2 = (head_of(queries, s) for s in range(3))
    k0, k1, k2 = (head_of(keys, s) for s in range(3))
    v0, v1, v2 = (head_of(values, s) for s in range(3))

    index = place * 2 + jnp.arange(2, dtype=jnp.int32)
    total_blocks = block_mask.shape[0]
    rows = lax.dynamic_slice_in_dim(block_mask, place * 2, 2, 0)
    cand = index[:, None] + jnp.arange(-REACH, REACH + 1, dtype=jnp.int32)[None, :]
    every = jnp.arange(total_blocks, dtype=jnp.int32)
    hits = jnp.any((cand[:, :, None] == every[None, None, :]) & (rows[:, None, :] == 1), axis=2)
    first_bit = (index > REACH) & (rows[:, 0] == 1)
    bits = jnp.concatenate([hits, first_bit[:, None]], axis=1).astype(jnp.int32)

    own2 = jnp.concatenate([split_blocks(k2), split_blocks(v2)], axis=1)
    left2, right2 = both_ways(own2, parts)

    shares = scattered(jnp.concatenate([k1, k2, v1, v2], axis=1)[:BLOCK], place, (2 * deep, deep, deep // 2, deep // 4))

    packs = [position_pack(jnp.concatenate(pair, axis=1), parts) for pair in ((q0, q1), (k0, k1), (v0, v1))]
    near = BLOCK // parts
    sent = jnp.concatenate(
        [w_out[:, lanes(c)] for c in range(w_out.shape[1] // HEAD_DIM)]
        + [x[:near] for x in (k0, k1, v0, v1)]
        + [shares[:, lanes(c)] for c in range(4)],
        axis=0,
    )
    packed, sent, left2, right2 = lax.optimization_barrier((jnp.concatenate(packs, axis=2), sent, left2, right2))
    moved = exchange(packed).reshape(BLOCK, -1)
    moved_q, moved_kv = moved[:, : 4 * HEAD_DIM], moved[:, 4 * HEAD_DIM :]
    rows_z = lax.all_gather(sent, "ctx", axis=0, axis_index_groups=along_z)
    def mix(moved, still, kinds):
        cols = []
        for n in range(kinds * 2):
            cols.append(moved[:, lanes(2 * n)])
            cols.append(jnp.where(moves, moved[:, lanes(2 * n + 1)], still[:, lanes(n)]))
        return jnp.concatenate(cols, axis=1)

    own = mix(moved_kv, jnp.concatenate([split_blocks(k1), split_blocks(v1)], axis=1), 2)
    left, right = both_ways(own, parts)
    query = mix(moved_q, split_blocks(q1), 1)
    left, right, rows_z = lax.optimization_barrier((left, right, rows_z))
    quarter, w_z = unpack(moves, rows_z, deep * w_out.shape[0], w_out.shape[1])

    def along_y(x):
        return [lax.ppermute(x, "ctx", [(i, i ^ (deep * k)) for i in range(parts)]) for k in (1, 2, 3)]

    first = [quarter] + along_y(quarter)
    w_z, first = lax.optimization_barrier((w_z, first))
    w_parts = [w_z] + along_y(w_z)

    query2 = split_blocks(q2)
    spatial = near_attention(1, bits, query2, own2, left2, right2)
    mixed = near_attention(2, bits, query, own, left, right)
    out, out2 = first_attention(bits, (query, *mixed), (query2, *spatial), first)
    attn2 = jnp.concatenate([out2[:, lanes(0)], out2[:, lanes(1)]], axis=0)
    spatial = lax.all_gather(attn2, "head", axis=1, tiled=True)

    back = exchange(out.reshape(parts, BLOCK // parts, -1))
    back = back.reshape(parts, BLOCK // parts, 2, 2 * HEAD_DIM).transpose(0, 2, 1, 3).reshape(2 * BLOCK, 2 * HEAD_DIM)
    still = jnp.concatenate([out[:, lanes(1)], out[:, lanes(3)]], axis=0)
    attn = jnp.concatenate([back[:, lanes(0)], jnp.where(moves, back[:, lanes(1)], still)], axis=1)
    mixed = lax.all_gather(attn, "head", axis=1, tiled=True)
    part, mixed_w = spatial_projection(groups, order, spatial, w_parts)
    return mixed_projection(part, mixed, mixed_w)


def solution(mesh):
    return jax.shard_map(
        body,
        mesh=mesh,
        in_specs=(P("ctx", "head"), P("ctx", "head"), P("ctx", "head"), P(), P(), P("ctx", "head")),
        out_specs=P("ctx", "head"),
        check_vma=False,
    )
```

time: 332 us -> 319 us (0.961)
  waiting for transfers between devices: 191 us -> 140 us
  starting transfers between devices: 67.7 us -> 90 us
  Pallas kernels: 19.5 us -> 26.1 us
  local copies, waits for them, and re-layouts: 19.6 us -> 25 us
  other arithmetic: 14.3 us -> 19.2 us
    all_gather x1, waiting for transfers between devices: 87.9 us -> 0.02 us  [body(): rows_z = lax.all_gather(sent, 'ctx', axis=0, axis_index_groups=along_z)]
    all_to_all x2, waiting for transfers between devices: 26.9 us -> 95.2 us  [exchange(): return lax.all_to_all(x, 'ctx', 0, 0, tiled=True)]
    all_gather x1, waiting for transfers between devices: 35.5 us -> 3.47 us  [body(): mixed = lax.all_gather(attn, 'head', axis=1, tiled=True)]
    ppermute x3 -> x6, starting transfers between devices: 8.97 us -> 19.2 us  [along_y(): lax.ppermute(x, 'ctx', [(i, i ^ deep * k) for i in range(parts)])]
    ppermute x2, waiting for transfers between devices: 0.87 us -> 10 us  [both_ways(): left = lax.ppermute(x, 'ctx', [(i, i + 1) for i in range(count - 1)])]
    ppermute x2, waiting for transfers between devices: 13.5 us -> 4.55 us  [both_ways(): right = lax.ppermute(x, 'ctx', [(i + 1, i) for i in range(count - 1)])]
    unnamed x40 -> x58, local copies, waits for them, and re-layouts: 12 us -> 18.5 us
    pallas_call x2 -> x4, Pallas kernels: 14 us -> 20.4 us  [the longest x2 17.7 us: near_attention(): pl.pallas_call(lambda *refs: near_kernel(heads, *refs), out_shape=(state,...]
  transfers between devices with their start and end apart: 17 -> 19, of which waited for: 12 -> 11; matrix products, arithmetic and copies ran while one was open for 7% -> 8% of each run, Pallas kernels for 5% -> 6%
where the time goes in v3:
time: 319 us; the launch traced here: 318 us
  waiting for transfers between devices  140 us (44%)
  starting transfers between devices  90 us (28%)
  Pallas kernels  26.1 us (8%)
  local copies, waits for them, and re-layouts  25 us (8%)
  other arithmetic  19.2 us (6%)
  between operations  17.8 us (6%)
    all_to_all x2, waiting for transfers between devices, exchange(): return lax.all_to_all(x, 'ctx', 0, 0, tiled=True)  95.2 us
    all_to_all x2, starting transfers between devices, exchange(): return lax.all_to_all(x, 'ctx', 0, 0, tiled=True)  35.5 us
    ppermute x6, waiting for transfers between devices, along_y(): lax.ppermute(x, 'ctx', [(i, i ^ deep * k) for i in range(parts)])  23.6 us
    ppermute x6, starting transfers between devices, along_y(): lax.ppermute(x, 'ctx', [(i, i ^ deep * k) for i in range(parts)])  19.2 us
    ppermute x4, starting transfers between devices, scattered(): lax.ppermute(x[half:], 'ctx', [(i, i + step) for i in range(0, count, rea...  18.6 us
    unnamed x58, local copies, waits for them, and re-layouts  18.5 us
    pallas_call x2, Pallas kernels, near_attention(): pl.pallas_call(lambda *refs: near_kernel(heads, *refs), out_shape=(state,...  17.7 us
    ppermute x2, starting transfers between devices, both_ways(): left = lax.ppermute(x, 'ctx', [(i, i + 1) for i in range(count - 1)])  14.1 us
  transfers between devices with their start and end apart: 19, of which 11 were waited for; matrix products, arithmetic and copies ran while one was open for 8% of the time, Pallas kernels for 6%

profile of v3, /device:TPU:1, one launch (start us, length us, event | category | flops | bytes accessed | tf_op | source)
XLA Modules:
  0.0 317.7 jit_solution(219493557613491332)
XLA Ops:
  6.5 0.7 broadcast_compare_fusion.1
  9.4 1.1 constant_dynamic-slice_fusion.1
  10.6 4.4 %collective-permute-start.4 = (bf16[512,512]{1,0:T(8,128)(2,1)S(1)}, bf16[512,512]{1,0:T(8,128)(2,1)S(1)}, u32[]{:S(2)}, u32[]{:S(2)}) collective-permute-start(bf16[512,512]{1,0:T(8,128)(2,1)S(1)} %pad_maximum_fusion.4.refs_2_), channel_id=1, source_target_pairs={{0,8},{8,16},{16,24},{24,32},{32,40},{40,48},{48,56},{56,64},{64,7... | collective-permute-start | bytes 1572872 | tf_op jit(solution)/shard_map/ppermute | solution.py:261
  15.0 1.3 collective-permute-start.5
  17.5 2.1 constant_dynamic-slice_fusion.7
  19.6 0.7 pad_maximum_fusion.10
  20.3 13.6 %collective-permute-start = (bf16[256,512]{1,0:T(8,128)(2,1)}, bf16[256,512]{1,0:T(8,128)(2,1)}, u32[]{:S(2)}, u32[]{:S(2)}) collective-permute-start(bf16[256,512]{1,0:T(8,128)(2,1)} %pad_maximum_fusion.10), channel_id=1, source_target_pairs={{0,256},{1,257},{2,258},{3,259},{4,260},{5,261},{6,262},{7,263}} | collective-permute-start | bytes 786440 | tf_op jit(solution)/shard_map/ppermute | solution.py:271
  34.0 1.9 pad_maximum_fusion.3
  35.8 1.8 pad_maximum_fusion.2
  37.7 0.9 constant_dynamic-slice_fusion.14
  38.6 1.9 pad_maximum_fusion.1
  40.4 2.6 pad_maximum_fusion
  43.9 1.3 collective-permute-start.1
  45.2 1.9 collective-permute-done.1
  47.1 0.9 slice_select_fusion.1
  48.0 2.4 collective-permute-start.2
  50.4 0.7 constant_dynamic-update-slice_fusion.5
  51.8 1.3 collective-permute-start.3
  53.1 0.7 constant_dynamic-update-slice_fusion.4
  54.8 16.2 %all-to-all-start = ((bf16[64,8,1536]{2,1,0:T(8,128)(2,1)}), bf16[64,8,1536]{2,1,0:T(8,128)(2,1)}, u32[]{:S(2)}, u32[]{:S(2)}) async-start(bf16[64,8,1536]{2,1,0:T(8,128)(2,1)} %pad_maximum_fusion), calls=%async_computation | async-start | bytes 3145728 | tf_op jit(solution)/shard_map/all_to_all | solution.py:257
  73.9 0.7 broadcast_compare_fusion
  74.7 71.4 %all-to-all-done = bf16[64,8,1536]{2,1,0:T(8,128)(2,1)} async-done(((bf16[64,8,1536]{2,1,0:T(8,128)(2,1)}), bf16[64,8,1536]{2,1,0:T(8,128)(2,1)}, u32[]{:S(2)}, u32[]{:S(2)}) %all-to-all-start) | async-done | bytes 1572896 | tf_op jit(solution)/shard_map/all_to_all | solution.py:257
  146.1 0.9 slice_dynamic-update-slice_fusion.3
  147.1 1.0 fusion.4
  148.1 0.9 slice_dynamic-update-slice_fusion.2
  149.1 1.0 fusion.3
  150.1 0.9 slice_dynamic-update-slice_fusion.1
  151.0 1.0 fusion.2
  152.1 0.9 slice_dynamic-update-slice_fusion
  153.1 1.6 fusion.1
  154.7 9.7 %collective-permute-start.6 = (bf16[512,1024]{1,0:T(8,128)(2,1)S(1)}, bf16[512,1024]{1,0:T(8,128)(2,1)}, u32[]{:S(2)}, u32[]{:S(2)}) collective-permute-start(bf16[512,1024]{1,0:T(8,128)(2,1)S(1)} %get-tuple-element.55.refs_2_), channel_id=1, source_target_pairs={{0,8},{8,16},{16,24},{24,32},{32,40},{40,48},{48,56},{56,64},{64,7... | collective-permute-start | bytes 3145736 | tf_op jit(solution)/shard_map/ppermute | solution.py:261
  164.3 1.3 collective-permute-start.7
  166.1 5.6 %shard_map.65 = (f32[512,256]{1,0:T(8,128)S(1)}, f32[512,256]{1,0:T(8,128)S(1)}) custom-call(s32[2,6]{1,0:T(2,128)S(1)} %add_convert_fusion.refs_0_.bits, bf16[512,256]{1,0:T(8,128)(2,1)S(1)} %pad_maximum_fusion.11.refs_1_.qs_ref, bf16[512,512]{1,0:T(8,128)(2,1)S(1)} %pad_maximum_fusion.4.refs_2_, bf16[512,512]{1,0:T(8,128)(2,1)S(1)} %copy-done.12, ...), custom_call_target="tpu_custom_call" | custom-call | flops 1342177280 | bytes 2097152 | tf_op jit(solution)/shard_map/pallas_call | solution.py:78
  171.8 10.0 %collective-permute-done.6.refs_3_ = bf16[512,1024]{1,0:T(8,128)(2,1)} collective-permute-done((bf16[512,1024]{1,0:T(8,128)(2,1)S(1)}, bf16[512,1024]{1,0:T(8,128)(2,1)}, u32[]{:S(2)}, u32[]{:S(2)}) %collective-permute-start.6) | collective-permute-done | bytes 1048608 | tf_op jit(solution)/shard_map/ppermute | solution.py:261
  181.8 4.5 %collective-permute-done.7.refs_4_ = bf16[512,1024]{1,0:T(8,128)(2,1)} collective-permute-done((bf16[512,1024]{1,0:T(8,128)(2,1)S(1)}, bf16[512,1024]{1,0:T(8,128)(2,1)}, u32[]{:S(2)}, u32[]{:S(2)}) %collective-permute-start.7) | collective-permute-done | bytes 1048608 | tf_op jit(solution)/shard_map/ppermute | solution.py:262
  186.4 1.3 copy-done.2
  187.8 1.9 collective-permute-start.8
  189.7 4.7 %collective-permute-start.9 = (bf16[128,768]{1,0:T(8,128)(2,1)S(1)}, bf16[128,768]{1,0:T(8,128)(2,1)S(1)}, u32[]{:S(2)}, u32[]{:S(2)}) collective-permute-start(bf16[128,768]{1,0:T(8,128)(2,1)S(1)} %get-tuple-element.40.f0), channel_id=1, source_target_pairs={{0,256},{8,264},{16,272},{24,280},{32,288},{40,296},{48,304},{56,3... | collective-permute-start | bytes 589832 | tf_op jit(solution)/shard_map/ppermute | solution.py:338
  194.4 3.0 collective-permute-start.10
  197.4 12.1 %shard_map.64 = (f32[512,512]{1,0:T(8,128)S(1)}, f32[512,512]{1,0:T(8,128)S(1)}) custom-call(s32[2,6]{1,0:T(2,128)S(1)} %add_convert_fusion.refs_0_.bits, bf16[512,512]{1,0:T(8,128)(2,1)S(1)} %pad_maximum_fusion.5.refs_1_.qm_ref, bf16[512,1024]{1,0:T(8,128)(2,1)S(1)} %get-tuple-element.55.refs_2_, bf16[512,1024]{1,0:T(8,128)(2,1)} %collective-permute-done.6.refs_3_, ...), custom_call_target="tpu_custom_call" | custom-call | flops 2684354560 | bytes 4194304 | tf_op jit(solution)/shard_map/pallas_call | solution.py:78
  209.5 2.6 shard_map.67
  212.2 0.7 pad_maximum_fusion.12
  212.9 19.3 %all-to-all-start.1 = ((bf16[64,8,512]{2,1,0:T(8,128)(2,1)}), bf16[64,8,512]{2,1,0:T(8,128)(2,1)S(1)}, u32[]{:S(2)}, u32[]{:S(2)}) async-start(bf16[64,8,512]{2,1,0:T(8,128)(2,1)} %bitcast.16), calls=%async_computation.1 | async-start | bytes 1048576 | tf_op jit(solution)/shard_map/all_to_all | solution.py:257
  232.2 1.0 fusion.8
  233.2 23.7 %all-to-all-done.1 = bf16[64,8,512]{2,1,0:T(8,128)(2,1)S(1)} async-done(((bf16[64,8,512]{2,1,0:T(8,128)(2,1)}), bf16[64,8,512]{2,1,0:T(8,128)(2,1)S(1)}, u32[]{:S(2)}, u32[]{:S(2)}) %all-to-all-start.1) | async-done | bytes 524320 | tf_op jit(solution)/shard_map/all_to_all | solution.py:257
  257.1 0.9 pad_maximum_fusion.6
  258.0 3.1 collective-permute-start.11
  261.1 4.5 %collective-permute-start.12 = (bf16[768,384]{1,0:T(8,128)(2,1)S(1)}, bf16[768,384]{1,0:T(8,128)(2,1)S(1)}, u32[]{:S(2)}, u32[]{:S(2)}) collective-permute-start(bf16[768,384]{1,0:T(8,128)(2,1)S(1)} %get-tuple-element.45.refs_2_), channel_id=1, source_target_pairs={{0,256},{8,264},{16,272},{24,280},{32,288},{40,296},{48,304},{56,3... | collective-permute-start | bytes 1769480 | tf_op jit(solution)/shard_map/ppermute | solution.py:338
  265.6 2.0 collective-permute-start.13
  267.8 0.8 collective-permute-done.11.refs_3_
  268.6 0.8 copy-done.5
  269.5 12.4 %collective-permute-done.12.refs_4_ = bf16[768,384]{1,0:T(8,128)(2,1)S(1)} collective-permute-done((bf16[768,384]{1,0:T(8,128)(2,1)S(1)}, bf16[768,384]{1,0:T(8,128)(2,1)S(1)}, u32[]{:S(2)}, u32[]{:S(2)}) %collective-permute-start.12) | collective-permute-done | bytes 589856 | tf_op jit(solution)/shard_map/ppermute | solution.py:338
  281.8 0.9 copy-done.7
  282.7 10.4 %collective-permute-done.13.refs_5_ = bf16[768,384]{1,0:T(8,128)(2,1)S(1)} collective-permute-done((bf16[768,384]{1,0:T(8,128)(2,1)S(1)}, bf16[768,384]{1,0:T(8,128)(2,1)S(1)}, u32[]{:S(2)}, u32[]{:S(2)}) %collective-permute-start.13) | collective-permute-done | bytes 589856 | tf_op jit(solution)/shard_map/ppermute | solution.py:338
  293.1 0.9 copy-done.9
  293.9 1.6 copy-done.1
  295.5 1.1 copy-done.4
  296.6 1.1 copy-done.6
  297.7 1.1 copy-done.8
  298.8 1.1 copy-done.10
  299.8 2.1 shard_map.68
  302.0 3.5 %all-gather.7.cloned.1.call-done.mixed_ref = bf16[1024,2048]{1,0:T(8,128)(2,1)} async-done(((bf16[1024,256]{1,0:T(8,128)(2,1)}), bf16[1024,2048]{1,0:T(8,128)(2,1)}) %all-gather.7.cloned.1.call-update) | async-done | bytes 4194320 | tf_op jit(solution)/shard_map/all_gather | solution.py:355
  305.4 2.2 copy-done
  307.6 3.5 %shard_map.69 = bf16[1024,384]{1,0:T(8,128)(2,1)} custom-call(f32[1024,384]{1,0:T(8,128)S(1)} %get-tuple-element.46.part_ref, bf16[1024,2048]{1,0:T(8,128)(2,1)S(1)} %copy-done, bf16[2048,384]{1,0:T(8,128)(2,1)S(1)} %get-tuple-element.48.w_ref), custom_call_target="tpu_custom_call" | custom-call | tf_op jit(solution)/shard_map/pallas_call | solution.py:226
  (86 shorter events, 5.6 us)
Async XLA Ops:
  6.5 11.0 %copy-start.15 = (bf16[1024,384]{1,0:T(8,128)(2,1)S(1)}, bf16[1024,384]{1,0:T(8,128)(2,1)}, u32[]{:S(2)}) copy-start(bf16[1024,384]{1,0:T(8,128)(2,1)} %param.7) | copy-start | bytes 2359300
  10.6 43.6 %collective-permute-start.4 = (bf16[512,512]{1,0:T(8,128)(2,1)S(1)}, bf16[512,512]{1,0:T(8,128)(2,1)S(1)}, u32[]{:S(2)}, u32[]{:S(2)}) collective-permute-start(bf16[512,512]{1,0:T(8,128)(2,1)S(1)} %pad_maximum_fusion.4.refs_2_), channel_id=1, source_target_pairs={{0,8},{8,16},{16,24},{24,32},{32,40},{40,48},{48,56},{56,64},{64,7... | collective-permute-start | bytes 1572872 | tf_op jit(solution)/shard_map/ppermute | solution.py:261
  15.0 39.2 %collective-permute-start.5 = (bf16[512,512]{1,0:T(8,128)(2,1)S(1)}, bf16[512,512]{1,0:T(8,128)(2,1)S(1)}, u32[]{:S(2)}, u32[]{:S(2)}) collective-permute-start(bf16[512,512]{1,0:T(8,128)(2,1)S(1)} %pad_maximum_fusion.4.refs_2_), channel_id=1, source_target_pairs={{8,0},{16,8},{24,16},{32,24},{40,32},{48,40},{56,48},{64,56},{72,6... | collective-permute-start | bytes 1572872 | tf_op jit(solution)/shard_map/ppermute | solution.py:262
  20.3 22.7 %collective-permute-start = (bf16[256,512]{1,0:T(8,128)(2,1)}, bf16[256,512]{1,0:T(8,128)(2,1)}, u32[]{:S(2)}, u32[]{:S(2)}) collective-permute-start(bf16[256,512]{1,0:T(8,128)(2,1)} %pad_maximum_fusion.10), channel_id=1, source_target_pairs={{0,256},{1,257},{2,258},{3,259},{4,260},{5,261},{6,262},{7,263}} | collective-permute-start | bytes 786440 | tf_op jit(solution)/shard_map/ppermute | solution.py:271
  34.0 3.7 %copy-start.16 = (bf16[1024,384]{1,0:T(8,128)(2,1)S(1)}, bf16[1024,384]{1,0:T(8,128)(2,1)}, u32[]{:S(2)}) copy-start(bf16[1024,384]{1,0:T(8,128)(2,1)} %param.6) | copy-start | bytes 2359300
  34.0 4.6 %copy-start.19 = (bf16[48,384]{1,0:T(8,128)(2,1)S(1)}, bf16[48,384]{1,0:T(8,128)(2,1)}, u32[]{:S(2)}) copy-start(bf16[48,384]{1,0:T(8,128)(2,1)} %param.11) | copy-start | bytes 110596
  43.2 0.7 copy-start.17
  43.9 3.2 %collective-permute-start.1 = (bf16[128,512]{1,0:T(8,128)(2,1)S(1)}, bf16[128,512]{1,0:T(8,128)(2,1)S(1)}, u32[]{:S(2)}, u32[]{:S(2)}) collective-permute-start(bf16[128,512]{1,0:T(8,128)(2,1)S(1)} %slice.252), channel_id=1, source_target_pairs={{0,128},{256,384},{1,129},{257,385},{2,130},{258,386},{3,131},{259... | collective-permute-start | bytes 393224 | tf_op jit(solution)/shard_map/ppermute | solution.py:271
  48.0 3.7 %collective-permute-start.2 = (bf16[64,512]{1,0:T(8,128)(2,1)S(1)}, bf16[64,512]{1,0:T(8,128)(2,1)S(1)}, u32[]{:S(2)}, u32[]{:S(2)}) collective-permute-start(bf16[64,512]{1,0:T(8,128)(2,1)S(1)} %slice.254), channel_id=1, source_target_pairs={{0,64},{128,192},{256,320},{384,448},{1,65},{129,193},{257,321},{3... | collective-permute-start | bytes 196616 | tf_op jit(solution)/shard_map/ppermute | solution.py:271
  51.8 2.3 collective-permute-start.3
  54.1 0.6 copy-start.18
  54.1 18.6 %copy-start.21 = (s32[24]{0:T(128)S(1)}, s32[24]{0:T(128)}, u32[]{:S(2)}) copy-start(s32[24]{0:T(128)} %param.10) | copy-start | bytes 292
  54.2 16.9 %copy-start.11 = (bf16[512,512]{1,0:T(8,128)(2,1)}, bf16[512,512]{1,0:T(8,128)(2,1)S(1)}, u32[]{:S(2)}) copy-start(bf16[512,512]{1,0:T(8,128)(2,1)S(1)} %collective-permute-done.4.refs_3_) | copy-start | bytes 1572868
  54.2 16.9 %copy-start.13 = (bf16[512,512]{1,0:T(8,128)(2,1)}, bf16[512,512]{1,0:T(8,128)(2,1)S(1)}, u32[]{:S(2)}) copy-start(bf16[512,512]{1,0:T(8,128)(2,1)S(1)} %collective-permute-done.5.refs_4_) | copy-start | bytes 1572868
  54.8 91.4 %all-to-all-start = ((bf16[64,8,1536]{2,1,0:T(8,128)(2,1)}), bf16[64,8,1536]{2,1,0:T(8,128)(2,1)}, u32[]{:S(2)}, u32[]{:S(2)}) async-start(bf16[64,8,1536]{2,1,0:T(8,128)(2,1)} %pad_maximum_fusion), calls=%async_computation | async-start | bytes 3145728 | tf_op jit(solution)/shard_map/all_to_all | solution.py:257
  71.0 100.8 %all-gather.9.cloned.1.call-start = ((), (), s32[]{:S(2)}) async-start(), calls=%async_computation.4 | async-start | bytes 1323008 | tf_op jit(solution)/shard_map/all_gather | solution.py:323
  74.6 219.3 %all-gather.5.cloned.1.call-start = ((), (), s32[]{:S(2)}) async-start(), calls=%async_computation.2 | async-start | bytes 2359296 | tf_op jit(solution)/shard_map/all_gather | solution.py:349
  153.0 13.1 %copy-start.12 = (bf16[512,512]{1,0:T(8,128)(2,1)S(1)}, bf16[512,512]{1,0:T(8,128)(2,1)}, u32[]{:S(2)}) copy-start(bf16[512,512]{1,0:T(8,128)(2,1)} %copy-done.11) | copy-start | bytes 1572868
  153.0 13.1 %copy-start.14 = (bf16[512,512]{1,0:T(8,128)(2,1)S(1)}, bf16[512,512]{1,0:T(8,128)(2,1)}, u32[]{:S(2)}) copy-start(bf16[512,512]{1,0:T(8,128)(2,1)} %copy-done.13) | copy-start | bytes 1572868
  154.7 27.1 %collective-permute-start.6 = (bf16[512,1024]{1,0:T(8,128)(2,1)S(1)}, bf16[512,1024]{1,0:T(8,128)(2,1)}, u32[]{:S(2)}, u32[]{:S(2)}) collective-permute-start(bf16[512,1024]{1,0:T(8,128)(2,1)S(1)} %get-tuple-element.55.refs_2_), channel_id=1, source_target_pairs={{0,8},{8,16},{16,24},{24,32},{32,40},{40,48},{48,56},{56,64},{64,7... | collective-permute-start | bytes 3145736 | tf_op jit(solution)/shard_map/ppermute | solution.py:261
  164.3 22.0 %collective-permute-start.7 = (bf16[512,1024]{1,0:T(8,128)(2,1)S(1)}, bf16[512,1024]{1,0:T(8,128)(2,1)}, u32[]{:S(2)}, u32[]{:S(2)}) collective-permute-start(bf16[512,1024]{1,0:T(8,128)(2,1)S(1)} %get-tuple-element.55.refs_2_), channel_id=1, source_target_pairs={{8,0},{16,8},{24,16},{32,24},{40,32},{48,40},{56,48},{64,56},{72,6... | collective-permute-start | bytes 3145736 | tf_op jit(solution)/shard_map/ppermute | solution.py:262
  186.4 1.3 copy-start.2
  187.8 77.8 %copy-start.3 = (bf16[768,384]{1,0:T(8,128)(2,1)}, bf16[768,384]{1,0:T(8,128)(2,1)S(1)}, u32[]{:S(2)}) copy-start(bf16[768,384]{1,0:T(8,128)(2,1)S(1)} %get-tuple-element.45.refs_2_) | copy-start | bytes 1769476
  187.8 21.7 %collective-permute-start.8 = (bf16[128,768]{1,0:T(8,128)(2,1)S(1)}, bf16[128,768]{1,0:T(8,128)(2,1)S(1)}, u32[]{:S(2)}, u32[]{:S(2)}) collective-permute-start(bf16[128,768]{1,0:T(8,128)(2,1)S(1)} %get-tuple-element.40.f0), channel_id=1, source_target_pairs={{0,128},{8,136},{16,144},{24,152},{32,160},{40,168},{48,176},{56,1... | collective-permute-start | bytes 589832 | tf_op jit(solution)/shard_map/ppermute | solution.py:338
  189.7 19.8 %collective-permute-start.9 = (bf16[128,768]{1,0:T(8,128)(2,1)S(1)}, bf16[128,768]{1,0:T(8,128)(2,1)S(1)}, u32[]{:S(2)}, u32[]{:S(2)}) collective-permute-start(bf16[128,768]{1,0:T(8,128)(2,1)S(1)} %get-tuple-element.40.f0), channel_id=1, source_target_pairs={{0,256},{8,264},{16,272},{24,280},{32,288},{40,296},{48,304},{56,3... | collective-permute-start | bytes 589832 | tf_op jit(solution)/shard_map/ppermute | solution.py:338
  194.4 15.1 %collective-permute-start.10 = (bf16[128,768]{1,0:T(8,128)(2,1)S(1)}, bf16[128,768]{1,0:T(8,128)(2,1)S(1)}, u32[]{:S(2)}, u32[]{:S(2)}) collective-permute-start(bf16[128,768]{1,0:T(8,128)(2,1)S(1)} %get-tuple-element.40.f0), channel_id=1, source_target_pairs={{0,384},{8,392},{16,400},{24,408},{32,416},{40,424},{48,432},{56,4... | collective-permute-start | bytes 589832 | tf_op jit(solution)/shard_map/ppermute | solution.py:338
  212.9 44.1 %all-to-all-start.1 = ((bf16[64,8,512]{2,1,0:T(8,128)(2,1)}), bf16[64,8,512]{2,1,0:T(8,128)(2,1)S(1)}, u32[]{:S(2)}, u32[]{:S(2)}) async-start(bf16[64,8,512]{2,1,0:T(8,128)(2,1)} %bitcast.16), calls=%async_computation.1 | async-start | bytes 1048576 | tf_op jit(solution)/shard_map/all_to_all | solution.py:257
  232.2 73.3 %all-gather.7.cloned.1.call-start = ((), (), s32[]{:S(2)}) async-start(), calls=%async_computation.3 | async-start | bytes 4718592 | tf_op jit(solution)/shard_map/all_gather | solution.py:355
  233.2 34.4 %copy-start.20 = (s32[8,3]{1,0:T(8,128)S(1)}, s32[8,3]{1,0:T(8,128)}, u32[]{:S(2)}) copy-start(s32[8,3]{1,0:T(8,128)} %get-tuple-element.51) | copy-start | bytes 292
  258.0 10.6 %collective-permute-start.11 = (bf16[768,384]{1,0:T(8,128)(2,1)S(1)}, bf16[768,384]{1,0:T(8,128)(2,1)S(1)}, u32[]{:S(2)}, u32[]{:S(2)}) collective-permute-start(bf16[768,384]{1,0:T(8,128)(2,1)S(1)} %get-tuple-element.45.refs_2_), channel_id=1, source_target_pairs={{0,128},{8,136},{16,144},{24,152},{32,160},{40,168},{48,176},{56,1... | collective-permute-start | bytes 1769480 | tf_op jit(solution)/shard_map/ppermute | solution.py:338
  261.1 20.7 %collective-permute-start.12 = (bf16[768,384]{1,0:T(8,128)(2,1)S(1)}, bf16[768,384]{1,0:T(8,128)(2,1)S(1)}, u32[]{:S(2)}, u32[]{:S(2)}) collective-permute-start(bf16[768,384]{1,0:T(8,128)(2,1)S(1)} %get-tuple-element.45.refs_2_), channel_id=1, source_target_pairs={{0,256},{8,264},{16,272},{24,280},{32,288},{40,296},{48,304},{56,3... | collective-permute-start | bytes 1769480 | tf_op jit(solution)/shard_map/ppermute | solution.py:338
  265.6 27.4 %collective-permute-start.13 = (bf16[768,384]{1,0:T(8,128)(2,1)S(1)}, bf16[768,384]{1,0:T(8,128)(2,1)S(1)}, u32[]{:S(2)}, u32[]{:S(2)}) collective-permute-start(bf16[768,384]{1,0:T(8,128)(2,1)S(1)} %get-tuple-element.45.refs_2_), channel_id=1, source_target_pairs={{0,384},{8,392},{16,400},{24,408},{32,416},{40,424},{48,432},{56,4... | collective-permute-start | bytes 1769480 | tf_op jit(solution)/shard_map/ppermute | solution.py:338
  268.6 0.8 copy-start.5
  281.8 0.9 copy-start.7
  293.1 0.9 copy-start.9
  293.9 1.6 copy-start.1
  295.5 1.1 copy-start.4
  296.6 1.1 copy-start.6
  297.7 1.1 copy-start.8
  298.8 1.1 copy-start.10
  305.4 2.2 copy-start
Sparse Core Ops, SparseCore 0:
  74.8 89.3 all-gather.8
  213.0 45.4 all-gather.4
  260.6 44.7 all-gather.6

commit v4 on v3

--- a/solution.py
+++ b/solution.py
@@ -14,6 +14,7 @@
 F32 = jnp.float32
 RATE = math.log2(math.e) / math.sqrt(HEAD_DIM)
 SPAN = 2 * REACH + 1
+COVER = 1 << 35
 
 
 def lanes(index):
@@ -140,6 +141,44 @@
             transcendentals=pairs * BLOCK * BLOCK,
         ),
     )(bits, *mixed, *spatial, *first)
+
+
+def mix_kernel(moves, moved_ref, q1_ref, k1_ref, v1_ref, query_ref, own_ref):
+    kept = (q1_ref, k1_ref, v1_ref)
+
+    def target(n):
+        return (query_ref, lanes(n)) if n < 4 else (own_ref, lanes(n - 4))
+
+    for n in range(12):
+        out_ref, here = target(n)
+        if n % 2 == 0:
+            out_ref[:, here] = moved_ref[:, lanes(n)]
+
+    @pl.when(moves[0] > 0)
+    def _():
+        for n in range(1, 12, 2):
+            out_ref, here = target(n)
+            out_ref[:, here] = moved_ref[:, lanes(n)]
+
+    @pl.when(moves[0] <= 0)
+    def _():
+        for n in range(1, 12, 2):
+            out_ref, here = target(n)
+            b = n // 2 % 2
+            out_ref[:, here] = kept[n // 4][b * BLOCK : (b + 1) * BLOCK, :]
+
+
+def mix(moves, moved, kept):
+    return pl.pallas_call(
+        mix_kernel,
+        out_shape=(
+            jax.ShapeDtypeStruct((BLOCK, 4 * HEAD_DIM), BF),
+            jax.ShapeDtypeStruct((BLOCK, 8 * HEAD_DIM), BF),
+        ),
+        in_specs=[SMEM] + [VMEM] * 4,
+        out_specs=(VMEM, VMEM),
+        compiler_params=pltpu.CompilerParams(vmem_limit_bytes=16 << 20),
+    )(moves, moved, *kept)
 
 
 def unpack_kernel(moves, x_ref, quarter_ref, w_ref):
@@ -182,15 +221,11 @@
         in_specs=[SMEM, VMEM],
         out_specs=(VMEM, VMEM),
         compiler_params=pltpu.CompilerParams(vmem_limit_bytes=16 << 20),
-    )(moves.astype(jnp.int32).reshape(1), x)
-
-
-def spatial_kernel(groups, order, spatial_ref, w0, w1, w2, w3, part_ref, mixed_w_ref, w_ref):
-    quarter = w0.shape[0]
-    for k, w in enumerate((w0, w1, w2, w3)):
-        at = jnp.bitwise_xor(order[groups * 3], k) * quarter
-        w_ref[pl.ds(pl.multiple_of(at, HEAD_DIM), quarter), :] = w[...]
-
+        cost_estimate=pl.CostEstimate(flops=COVER, bytes_accessed=0, transcendentals=0),
+    )(moves, x)
+
+
+def spatial_kernel(groups, order, spatial_ref, w_ref, part_ref, mixed_w_ref):
     def rows(g, slot):
         return w_ref[pl.ds(pl.multiple_of(order[g * 3 + slot] * HEAD_DIM, HEAD_DIM), HEAD_DIM), :]
 
@@ -202,18 +237,16 @@
 
 
 def spatial_projection(groups, order, spatial, w):
-    rows, cols = w[0].shape
     return pl.pallas_call(
         lambda *refs: spatial_kernel(groups, *refs),
         out_shape=(
-            jax.ShapeDtypeStruct((spatial.shape[0], cols), F32),
-            jax.ShapeDtypeStruct((groups * 2 * HEAD_DIM, cols), BF),
-        ),
-        in_specs=[SMEM] + [VMEM] * 5,
-        out_specs=(VMEM, VMEM),
-        scratch_shapes=[pltpu.VMEM((4 * rows, cols), BF)],
+            jax.ShapeDtypeStruct((spatial.shape[0], w.shape[1]), F32),
+            jax.ShapeDtypeStruct((groups * 2 * HEAD_DIM, w.shape[1]), BF),
+        ),
+        in_specs=[SMEM] + [VMEM] * 2,
+        out_specs=(VMEM, VMEM),
         compiler_params=pltpu.CompilerParams(vmem_limit_bytes=32 << 20),
-    )(order, spatial, *w)
+    )(order, spatial, w)
 
 
 def mixed_kernel(part_ref, mixed_ref, w_ref, out_ref):
@@ -233,7 +266,7 @@
             pl.BlockSpec(w.shape, lambda i: (0, 0)),
         ],
         out_specs=pl.BlockSpec((tile, cols), lambda i: (i, 0)),
-        compiler_params=pltpu.CompilerParams(vmem_limit_bytes=32 << 20),
+        compiler_params=pltpu.CompilerParams(vmem_limit_bytes=60 << 20),
     )(part, mixed, w)
 
 
@@ -263,15 +296,14 @@
     return left, right
 
 
-def scattered(x, place, steps):
+def scattered(x, index, unit, live):
     count = lax.axis_size("ctx")
-    reach = count
-    for step in steps:
-        half = x.shape[0] // 2
-        got = lax.ppermute(x[half:], "ctx", [(i, i + step) for i in range(0, count, reach)])
-        x = jnp.where(place % reach == step, got, x[:half])
-        reach = step
-    return x
+    rows = x.shape[0] // 4
+    out = x[:rows]
+    for k in (1, 2, 3):
+        got = lax.ppermute(x[k * rows : (k + 1) * rows], "ctx", [(i, i + k * unit) for i in range(0, count, live)])
+        out = jnp.where(index == k, got, out)
+    return out
 
 
 def body(queries, keys, values, block_mask, head_labels, w_out):
@@ -280,13 +312,13 @@
     place = lax.axis_index("ctx")
     group = lax.axis_index("head")
     deep = parts // 4
+    y_lines = [[y * deep + z for y in range(4)] for z in range(deep)]
     along_z = [[y * deep + z for z in range(deep)] for y in range(4)]
     slots = slots_of(head_labels.reshape(groups, 3))
     mine = lax.dynamic_slice_in_dim(slots, group, 1, 0)[0]
     labels = lax.dynamic_slice_in_dim(head_labels, group * 3, 3)
-    moves = lax.dynamic_slice_in_dim(labels, mine[1], 1)[0] == 1
+    moves = lax.dynamic_slice_in_dim(labels, mine[1], 1)
     order = (slots + 3 * jnp.arange(groups, dtype=jnp.int32)[:, None]).reshape(-1)
-    order = jnp.concatenate([order, (place // deep)[None].astype(jnp.int32)])
 
     def head_of(x, slot):
         return lax.dynamic_slice_in_dim(x, mine[slot] * HEAD_DIM, HEAD_DIM, 1)
@@ -304,10 +336,9 @@
     first_bit = (index > REACH) & (rows[:, 0] == 1)
     bits = jnp.concatenate([hits, first_bit[:, None]], axis=1).astype(jnp.int32)
 
-    own2 = jnp.concatenate([split_blocks(k2), split_blocks(v2)], axis=1)
-    left2, right2 = both_ways(own2, parts)
-
-    shares = scattered(jnp.concatenate([k1, k2, v1, v2], axis=1)[:BLOCK], place, (2 * deep, deep, deep // 2, deep // 4))
+    shares = jnp.concatenate([k1, k2, v1, v2], axis=1)[:BLOCK]
+    shares = scattered(shares, place // deep, deep, parts)
+    shares = scattered(shares, place % deep // (deep // 4), deep // 4, deep)
 
     packs = [position_pack(jnp.concatenate(pair, axis=1), parts) for pair in ((q0, q1), (k0, k1), (v0, v1))]
     near = BLOCK // parts
@@ -317,33 +348,26 @@
         + [shares[:, lanes(c)] for c in range(4)],
         axis=0,
     )
-    packed, sent, left2, right2 = lax.optimization_barrier((jnp.concatenate(packs, axis=2), sent, left2, right2))
+    own2 = jnp.concatenate([split_blocks(k2), split_blocks(v2)], axis=1)
+    packed, sent = lax.optimization_barrier((jnp.concatenate(packs, axis=2), sent))
     moved = exchange(packed).reshape(BLOCK, -1)
-    moved_q, moved_kv = moved[:, : 4 * HEAD_DIM], moved[:, 4 * HEAD_DIM :]
     rows_z = lax.all_gather(sent, "ctx", axis=0, axis_index_groups=along_z)
-    def mix(moved, still, kinds):
-        cols = []
-        for n in range(kinds * 2):
-            cols.append(moved[:, lanes(2 * n)])
-            cols.append(jnp.where(moves, moved[:, lanes(2 * n + 1)], still[:, lanes(n)]))
-        return jnp.concatenate(cols, axis=1)
-
-    own = mix(moved_kv, jnp.concatenate([split_blocks(k1), split_blocks(v1)], axis=1), 2)
+    quarter, w_z = unpack(moves, rows_z, deep * w_out.shape[0], w_out.shape[1])
+    moved, quarter = lax.optimization_barrier((moved, quarter))
+    query, own = mix(moves, moved, (q1, k1, v1))
     left, right = both_ways(own, parts)
-    query = mix(moved_q, split_blocks(q1), 1)
-    left, right, rows_z = lax.optimization_barrier((left, right, rows_z))
-    quarter, w_z = unpack(moves, rows_z, deep * w_out.shape[0], w_out.shape[1])
 
     def along_y(x):
         return [lax.ppermute(x, "ctx", [(i, i ^ (deep * k)) for i in range(parts)]) for k in (1, 2, 3)]
 
     first = [quarter] + along_y(quarter)
-    w_z, first = lax.optimization_barrier((w_z, first))
-    w_parts = [w_z] + along_y(w_z)
-
+    left, right, first = lax.optimization_barrier((left, right, first))
+    w = lax.all_gather(w_z, "ctx", axis=0, axis_index_groups=y_lines, tiled=True)
+
+    mixed = near_attention(2, bits, query, own, left, right)
+    own2, _, _ = lax.optimization_barrier((own2, left, right))
     query2 = split_blocks(q2)
-    spatial = near_attention(1, bits, query2, own2, left2, right2)
-    mixed = near_attention(2, bits, query, own, left, right)
+    spatial = near_attention(1, bits, query2, own2, *both_ways(own2, parts))
     out, out2 = first_attention(bits, (query, *mixed), (query2, *spatial), first)
     attn2 = jnp.concatenate([out2[:, lanes(0)], out2[:, lanes(1)]], axis=0)
     spatial = lax.all_gather(attn2, "head", axis=1, tiled=True)
@@ -351,9 +375,9 @@
     back = exchange(out.reshape(parts, BLOCK // parts, -1))
     back = back.reshape(parts, BLOCK // parts, 2, 2 * HEAD_DIM).transpose(0, 2, 1, 3).reshape(2 * BLOCK, 2 * HEAD_DIM)
     still = jnp.concatenate([out[:, lanes(1)], out[:, lanes(3)]], axis=0)
-    attn = jnp.concatenate([back[:, lanes(0)], jnp.where(moves, back[:, lanes(1)], still)], axis=1)
+    attn = jnp.concatenate([back[:, lanes(0)], jnp.where(moves[0] > 0, back[:, lanes(1)], still)], axis=1)
     mixed = lax.all_gather(attn, "head", axis=1, tiled=True)
-    part, mixed_w = spatial_projection(groups, order, spatial, w_parts)
+    part, mixed_w = spatial_projection(groups, order, spatial, w)
     return mixed_projection(part, mixed, mixed_w)
 
 

time: 319 us -> 319 us (level)
  waiting for transfers between devices: 140 us -> 172 us
  other arithmetic: 19.2 us -> 5.25 us
  starting transfers between devices: 90 us -> 77.4 us
  local copies, waits for them, and re-layouts: 25 us -> 17 us
    all_gather x1, waiting for transfers between devices: 0.02 us -> 80.5 us  [body(): rows_z = lax.all_gather(sent, 'ctx', axis=0, axis_index_groups=along_z)]
    all_to_all x2, waiting for transfers between devices: 95.2 us -> 27.2 us  [exchange(): return lax.all_to_all(x, 'ctx', 0, 0, tiled=True)]
    all_gather x1, waiting for transfers between devices: 3.47 us -> 32.3 us  [body(): mixed = lax.all_gather(attn, 'head', axis=1, tiled=True)]
    ppermute x2, waiting for transfers between devices: 10 us -> 0.01 us  [both_ways(): left = lax.ppermute(x, 'ctx', [(i, i + 1) for i in range(count - 1)])]
    ppermute x2, starting transfers between devices: 14.1 us -> 4.2 us  [both_ways(): left = lax.ppermute(x, 'ctx', [(i, i + 1) for i in range(count - 1)])]
    unnamed x58 -> x28, local copies, waits for them, and re-layouts: 18.5 us -> 10.8 us
    ppermute x6 -> x3, starting transfers between devices: 19.2 us -> 12.3 us  [along_y(): lax.ppermute(x, 'ctx', [(i, i ^ deep * k) for i in range(parts)])]
    concatenate x3, other arithmetic: 5.57 us -> 0.22 us  [body(): jnp.concatenate(pair, axis=1)]
  transfers between devices with their start and end apart: 19 -> 19, of which waited for: 11 -> 7; matrix products, arithmetic and copies ran while one was open for 8% -> 3% of each run, Pallas kernels for 6% -> 7%
where the time goes in v4:
time: 319 us; the launch traced here: 318 us
  waiting for transfers between devices  172 us (54%)
  starting transfers between devices  77.4 us (24%)
  Pallas kernels  28.2 us (9%)
  between operations  18 us (6%)
  local copies, waits for them, and re-layouts  17 us (5%)
  other arithmetic  5.25 us (2%)
    all_gather x1, waiting for transfers between devices, body(): rows_z = lax.all_gather(sent, 'ctx', axis=0, axis_index_groups=along_z)  80.5 us
    all_to_all x2, starting transfers between devices, exchange(): return lax.all_to_all(x, 'ctx', 0, 0, tiled=True)  37.9 us
    all_gather x1, waiting for transfers between devices, body(): mixed = lax.all_gather(attn, 'head', axis=1, tiled=True)  32.3 us
    ppermute x3, waiting for transfers between devices, along_y(): lax.ppermute(x, 'ctx', [(i, i ^ deep * k) for i in range(parts)])  28.1 us
    all_to_all x2, waiting for transfers between devices, exchange(): return lax.all_to_all(x, 'ctx', 0, 0, tiled=True)  27.2 us
    ppermute x6, starting transfers between devices, scattered(): lax.ppermute(x[k * rows:(k + 1) * rows], 'ctx', [(i, i + k * unit) for i...  20.4 us
    pallas_call x2, Pallas kernels, near_attention(): pl.pallas_call(lambda *refs: near_kernel(heads, *refs), out_shape=(state,...  13.6 us
    ppermute x3, starting transfers between devices, along_y(): lax.ppermute(x, 'ctx', [(i, i ^ deep * k) for i in range(parts)])  12.3 us
  transfers between devices with their start and end apart: 19, of which 7 were waited for; matrix products, arithmetic and copies ran while one was open for 3% of the time, Pallas kernels for 7%

profile of v4, /device:TPU:1, one launch (start us, length us, event | category | flops | bytes accessed | tf_op | source)
XLA Modules:
  0.0 317.6 jit_solution(15669794720059552779)
XLA Ops:
  6.5 0.7 broadcast_compare_fusion.1
  7.2 0.1 eq.51
  7.3 0.1 select_select_fusion.1
  7.4 0.1 broadcast_add_fusion
  7.4 0.6 fusion.11
  10.0 1.5 constant_dynamic-slice_fusion.7
  11.5 5.6 %collective-permute-start = (bf16[128,512]{1,0:T(8,128)(2,1)S(1)}, bf16[128,512]{1,0:T(8,128)(2,1)S(1)}, u32[]{:S(2)}, u32[]{:S(2)}) collective-permute-start(bf16[128,512]{1,0:T(8,128)(2,1)S(1)} %get-tuple-element.56), channel_id=1, source_target_pairs={{0,384},{1,385},{2,386},{3,387},{4,388},{5,389},{6,390},{7,391}} | collective-permute-start | bytes 393224 | tf_op jit(solution)/shard_map/ppermute | solution.py:304
  17.2 1.3 collective-permute-start.1
  18.5 1.3 collective-permute-start.2
  19.8 0.1 pad_maximum_fusion.3
  19.9 0.1 pad_maximum_fusion.2
  20.0 0.1 constant_dynamic-slice_fusion.14
  20.0 0.5 copy-done.7
  20.6 0.7 constant_dynamic-update-slice_fusion.7
  21.3 1.3 pad_maximum_fusion
  22.6 0.7 constant_dynamic-update-slice_fusion.6
  23.3 0.7 constant_dynamic-update-slice_fusion.5
  24.0 0.1 fusion.2
  24.1 7.2 %collective-permute-start.3 = (bf16[32,512]{1,0:T(8,128)(2,1)S(1)}, bf16[32,512]{1,0:T(8,128)(2,1)S(1)}, u32[]{:S(2)}, u32[]{:S(2)}) collective-permute-start(bf16[32,512]{1,0:T(8,128)(2,1)S(1)} %get-tuple-element.80), channel_id=1, source_target_pairs={{0,96},{128,224},{256,352},{384,480},{1,97},{129,225},{257,353},{3... | collective-permute-start | bytes 98312 | tf_op jit(solution)/shard_map/ppermute | solution.py:304
  31.3 3.7 %collective-permute-start.4 = (bf16[32,512]{1,0:T(8,128)(2,1)S(1)}, bf16[32,512]{1,0:T(8,128)(2,1)S(1)}, u32[]{:S(2)}, u32[]{:S(2)}) collective-permute-start(bf16[32,512]{1,0:T(8,128)(2,1)S(1)} %get-tuple-element.79), channel_id=1, source_target_pairs={{0,64},{128,192},{256,320},{384,448},{1,65},{129,193},{257,321},{3... | collective-permute-start | bytes 98312 | tf_op jit(solution)/shard_map/ppermute | solution.py:304
  34.9 1.3 collective-permute-start.5
  36.2 0.7 constant_dynamic-update-slice_fusion.4
  36.9 0.4 collective-permute-done.5
  37.4 0.6 copy-done.6
  38.0 14.0 %all-to-all-start = ((bf16[64,8,1536]{2,1,0:T(8,128)(2,1)}), bf16[64,8,1536]{2,1,0:T(8,128)(2,1)S(1)}, u32[]{:S(2)}, u32[]{:S(2)}) async-start(bf16[64,8,1536]{2,1,0:T(8,128)(2,1)} %pad_maximum_fusion), calls=%async_computation | async-start | bytes 3145728 | tf_op jit(solution)/shard_map/all_to_all | solution.py:290
  54.0 0.7 dynamic_slice.42.moves
  54.7 80.5 %all-gather.12.cloned.1.call-done = bf16[4864,128]{1,0:T(8,128)(2,1)} async-done(((bf16[304,128]{1,0:T(8,128)(2,1)}), bf16[4864,128]{1,0:T(8,128)(2,1)}) %all-gather.12.cloned.1.call-update) | async-done | bytes 1245200 | tf_op jit(solution)/shard_map/all_gather | solution.py:354
  135.2 1.3 copy-done.4
  136.5 1.6 shard_map.64
  138.2 2.1 shard_map.65
  140.3 2.9 collective-permute-start.6
  143.2 1.3 collective-permute-start.7
  144.5 0.7 broadcast_compare_fusion
  145.2 0.1 broadcast_add_fusion.1
  145.3 0.2 fusion.6
  145.5 1.1 constant_dynamic-slice_fusion
  146.6 0.1 pad_maximum_fusion.4.refs_2_
  146.7 6.0 %collective-permute-start.8 = (bf16[128,768]{1,0:T(8,128)(2,1)S(1)}, bf16[128,768]{1,0:T(8,128)(2,1)S(1)}, u32[]{:S(2)}, u32[]{:S(2)}) collective-permute-start(bf16[128,768]{1,0:T(8,128)(2,1)S(1)} %get-tuple-element.42.f0), channel_id=1, source_target_pairs={{0,128},{8,136},{16,144},{24,152},{32,160},{40,168},{48,176},{56,1... | collective-permute-start | bytes 589832 | tf_op jit(solution)/shard_map/ppermute | solution.py:361
  152.8 3.3 %collective-permute-start.9 = (bf16[128,768]{1,0:T(8,128)(2,1)S(1)}, bf16[128,768]{1,0:T(8,128)(2,1)S(1)}, u32[]{:S(2)}, u32[]{:S(2)}) collective-permute-start(bf16[128,768]{1,0:T(8,128)(2,1)S(1)} %get-tuple-element.42.f0), channel_id=1, source_target_pairs={{0,256},{8,264},{16,272},{24,280},{32,288},{40,296},{48,304},{56,3... | collective-permute-start | bytes 589832 | tf_op jit(solution)/shard_map/ppermute | solution.py:361
  156.1 2.9 collective-permute-start.10
  159.0 17.5 %collective-permute-done.8.f1 = bf16[128,768]{1,0:T(8,128)(2,1)S(1)} collective-permute-done((bf16[128,768]{1,0:T(8,128)(2,1)S(1)}, bf16[128,768]{1,0:T(8,128)(2,1)S(1)}, u32[]{:S(2)}, u32[]{:S(2)}) %collective-permute-start.8) | collective-permute-done | bytes 196640 | tf_op jit(solution)/shard_map/ppermute | solution.py:361
  176.5 10.6 %collective-permute-done.9.f2 = bf16[128,768]{1,0:T(8,128)(2,1)S(1)} collective-permute-done((bf16[128,768]{1,0:T(8,128)(2,1)S(1)}, bf16[128,768]{1,0:T(8,128)(2,1)S(1)}, u32[]{:S(2)}, u32[]{:S(2)}) %collective-permute-start.9) | collective-permute-done | bytes 196640 | tf_op jit(solution)/shard_map/ppermute | solution.py:361
  187.1 1.3 collective-permute-start.11
  188.5 1.3 collective-permute-start.12
  189.8 0.1 add_convert_fusion.refs_0_.bits
  189.8 1.0 constant_dynamic-slice_fusion.2
  190.9 9.2 %shard_map.66 = (f32[512,512]{1,0:T(8,128)S(1)}, f32[512,512]{1,0:T(8,128)S(1)}) custom-call(s32[2,6]{1,0:T(2,128)S(1)} %add_convert_fusion.refs_0_.bits, bf16[512,512]{1,0:T(8,128)(2,1)S(1)} %get-tuple-element.32.refs_1_.qm_ref, bf16[512,1024]{1,0:T(8,128)(2,1)} %get-tuple-element.33.refs_2_, bf16[512,1024]{1,0:T(8,128)(2,1)S(1)} %collective-permute-done.6.refs_3_, ...), custom_call_target="tpu_custom_call" | custom-call | flops 2684354560 | bytes 4194304 | tf_op jit(solution)/shard_map/pallas_call | solution.py:79
  200.1 3.1 collective-permute-done.12.refs_4_
  203.2 4.4 %shard_map.67 = (f32[512,256]{1,0:T(8,128)S(1)}, f32[512,256]{1,0:T(8,128)S(1)}) custom-call(s32[2,6]{1,0:T(2,128)S(1)} %add_convert_fusion.refs_0_.bits, bf16[512,256]{1,0:T(8,128)(2,1)S(1)} %pad_maximum_fusion.6.refs_1_.qs_ref, bf16[512,512]{1,0:T(8,128)(2,1)S(1)} %pad_maximum_fusion.4.refs_2_, bf16[512,512]{1,0:T(8,128)(2,1)S(1)} %collective-permute-done.11.refs_3_, ...), custom_call_target="tpu_custom_call" | custom-call | flops 1342177280 | bytes 2097152 | tf_op jit(solution)/shard_map/pallas_call | solution.py:79
  207.7 2.6 shard_map.68
  210.3 0.7 pad_maximum_fusion.7
  211.0 23.9 %all-to-all-start.1 = ((bf16[64,8,512]{2,1,0:T(8,128)(2,1)}), bf16[64,8,512]{2,1,0:T(8,128)(2,1)S(1)}, u32[]{:S(2)}, u32[]{:S(2)}) async-start(bf16[64,8,512]{2,1,0:T(8,128)(2,1)} %bitcast.14), calls=%async_computation.1 | async-start | bytes 1048576 | tf_op jit(solution)/shard_map/all_to_all | solution.py:290
  235.6 1.0 fusion.8
  236.6 27.2 %all-to-all-done.1 = bf16[64,8,512]{2,1,0:T(8,128)(2,1)S(1)} async-done(((bf16[64,8,512]{2,1,0:T(8,128)(2,1)}), bf16[64,8,512]{2,1,0:T(8,128)(2,1)S(1)}, u32[]{:S(2)}, u32[]{:S(2)}) %all-to-all-start.1) | async-done | bytes 524320 | tf_op jit(solution)/shard_map/all_to_all | solution.py:290
  263.8 0.1 fusion.7
  263.9 0.9 pad_maximum_fusion.5
  264.8 0.1 add.92.refs_0_
  264.9 1.7 copy-done
  266.5 1.6 copy-done.1
  268.1 1.9 shard_map.69
  270.1 1.2 copy-done.2
  271.3 1.2 copy-done.3
  272.4 32.3 %all-gather.10.cloned.1.call-done.mixed_ref = bf16[1024,2048]{1,0:T(8,128)(2,1)} async-done(((bf16[1024,256]{1,0:T(8,128)(2,1)}), bf16[1024,2048]{1,0:T(8,128)(2,1)}) %all-gather.10.cloned.1.call-update) | async-done | bytes 4194320 | tf_op jit(solution)/shard_map/all_gather | solution.py:379
  304.7 6.3 %shard_map.70 = bf16[1024,384]{1,0:T(8,128)(2,1)} custom-call(f32[1024,384]{1,0:T(8,128)} %copy-done.2, bf16[1024,2048]{1,0:T(8,128)(2,1)} %all-gather.10.cloned.1.call-done.mixed_ref, bf16[2048,384]{1,0:T(8,128)(2,1)} %copy-done.3), custom_call_target="tpu_custom_call" | custom-call | tf_op jit(solution)/shard_map/pallas_call | solution.py:259
  (49 shorter events, 0.5 us)
Async XLA Ops:
  6.5 128.6 %all-gather.12.cloned.1.call-start = ((), (), s32[]{:S(2)}) async-start(), calls=%async_computation.5 | async-start | bytes 1323008 | tf_op jit(solution)/shard_map/all_gather | solution.py:354
  11.5 8.5 %copy-start.5 = (bf16[1024,384]{1,0:T(8,128)(2,1)S(1)}, bf16[1024,384]{1,0:T(8,128)(2,1)}, u32[]{:S(2)}) copy-start(bf16[1024,384]{1,0:T(8,128)(2,1)} %param.6) | copy-start | bytes 2359300
  11.5 12.4 %collective-permute-start = (bf16[128,512]{1,0:T(8,128)(2,1)S(1)}, bf16[128,512]{1,0:T(8,128)(2,1)S(1)}, u32[]{:S(2)}, u32[]{:S(2)}) collective-permute-start(bf16[128,512]{1,0:T(8,128)(2,1)S(1)} %get-tuple-element.56), channel_id=1, source_target_pairs={{0,384},{1,385},{2,386},{3,387},{4,388},{5,389},{6,390},{7,391}} | collective-permute-start | bytes 393224 | tf_op jit(solution)/shard_map/ppermute | solution.py:304
  17.2 6.8 %collective-permute-start.1 = (bf16[128,512]{1,0:T(8,128)(2,1)S(1)}, bf16[128,512]{1,0:T(8,128)(2,1)S(1)}, u32[]{:S(2)}, u32[]{:S(2)}) collective-permute-start(bf16[128,512]{1,0:T(8,128)(2,1)S(1)} %get-tuple-element.57), channel_id=1, source_target_pairs={{0,256},{1,257},{2,258},{3,259},{4,260},{5,261},{6,262},{7,263}} | collective-permute-start | bytes 393224 | tf_op jit(solution)/shard_map/ppermute | solution.py:304
  18.5 5.5 %collective-permute-start.2 = (bf16[128,512]{1,0:T(8,128)(2,1)S(1)}, bf16[128,512]{1,0:T(8,128)(2,1)S(1)}, u32[]{:S(2)}, u32[]{:S(2)}) collective-permute-start(bf16[128,512]{1,0:T(8,128)(2,1)S(1)} %get-tuple-element.55), channel_id=1, source_target_pairs={{0,128},{1,129},{2,130},{3,131},{4,132},{5,133},{6,134},{7,135}} | collective-permute-start | bytes 393224 | tf_op jit(solution)/shard_map/ppermute | solution.py:304
  19.8 0.8 copy-start.7
  24.1 12.9 %collective-permute-start.3 = (bf16[32,512]{1,0:T(8,128)(2,1)S(1)}, bf16[32,512]{1,0:T(8,128)(2,1)S(1)}, u32[]{:S(2)}, u32[]{:S(2)}) collective-permute-start(bf16[32,512]{1,0:T(8,128)(2,1)S(1)} %get-tuple-element.80), channel_id=1, source_target_pairs={{0,96},{128,224},{256,352},{384,480},{1,97},{129,225},{257,353},{3... | collective-permute-start | bytes 98312 | tf_op jit(solution)/shard_map/ppermute | solution.py:304
  31.3 5.7 %collective-permute-start.4 = (bf16[32,512]{1,0:T(8,128)(2,1)S(1)}, bf16[32,512]{1,0:T(8,128)(2,1)S(1)}, u32[]{:S(2)}, u32[]{:S(2)}) collective-permute-start(bf16[32,512]{1,0:T(8,128)(2,1)S(1)} %get-tuple-element.79), channel_id=1, source_target_pairs={{0,64},{128,192},{256,320},{384,448},{1,65},{129,193},{257,321},{3... | collective-permute-start | bytes 98312 | tf_op jit(solution)/shard_map/ppermute | solution.py:304
  34.9 2.4 collective-permute-start.5
  37.4 0.6 copy-start.6
  38.0 16.0 %copy-start.8 = (s32[24]{0:T(128)S(1)}, s32[24]{0:T(128)}, u32[]{:S(2)}) copy-start(s32[24]{0:T(128)} %param.10) | copy-start | bytes 292
  38.0 100.1 %all-to-all-start = ((bf16[64,8,1536]{2,1,0:T(8,128)(2,1)}), bf16[64,8,1536]{2,1,0:T(8,128)(2,1)S(1)}, u32[]{:S(2)}, u32[]{:S(2)}) async-start(bf16[64,8,1536]{2,1,0:T(8,128)(2,1)} %pad_maximum_fusion), calls=%async_computation | async-start | bytes 3145728 | tf_op jit(solution)/shard_map/all_to_all | solution.py:290
  52.1 212.8 %all-gather.8.cloned.1.call-start = ((), (), s32[]{:S(2)}) async-start(), calls=%async_computation.3 | async-start | bytes 2949120 | tf_op jit(solution)/shard_map/all_gather | solution.py:365
  135.2 1.3 copy-start.4
  138.1 126.7 %all-gather.6.cloned.1.call-start = ((), (), s32[]{:S(2)}) async-start(), calls=%async_computation.2 | async-start | bytes 2359296 | tf_op jit(solution)/shard_map/all_gather | solution.py:373
  140.3 46.8 %collective-permute-start.6 = (bf16[512,1024]{1,0:T(8,128)(2,1)}, bf16[512,1024]{1,0:T(8,128)(2,1)S(1)}, u32[]{:S(2)}, u32[]{:S(2)}) collective-permute-start(bf16[512,1024]{1,0:T(8,128)(2,1)} %get-tuple-element.33.refs_2_), channel_id=1, source_target_pairs={{0,8},{8,16},{16,24},{24,32},{32,40},{40,48},{48,56},{56,64},{64,7... | collective-permute-start | bytes 3145736 | tf_op jit(solution)/shard_map/ppermute | solution.py:294
  143.2 43.9 %collective-permute-start.7 = (bf16[512,1024]{1,0:T(8,128)(2,1)}, bf16[512,1024]{1,0:T(8,128)(2,1)S(1)}, u32[]{:S(2)}, u32[]{:S(2)}) collective-permute-start(bf16[512,1024]{1,0:T(8,128)(2,1)} %get-tuple-element.33.refs_2_), channel_id=1, source_target_pairs={{8,0},{16,8},{24,16},{32,24},{40,32},{48,40},{56,48},{64,56},{72,6... | collective-permute-start | bytes 3145736 | tf_op jit(solution)/shard_map/ppermute | solution.py:295
  146.7 29.8 %collective-permute-start.8 = (bf16[128,768]{1,0:T(8,128)(2,1)S(1)}, bf16[128,768]{1,0:T(8,128)(2,1)S(1)}, u32[]{:S(2)}, u32[]{:S(2)}) collective-permute-start(bf16[128,768]{1,0:T(8,128)(2,1)S(1)} %get-tuple-element.42.f0), channel_id=1, source_target_pairs={{0,128},{8,136},{16,144},{24,152},{32,160},{40,168},{48,176},{56,1... | collective-permute-start | bytes 589832 | tf_op jit(solution)/shard_map/ppermute | solution.py:361
  152.8 34.4 %collective-permute-start.9 = (bf16[128,768]{1,0:T(8,128)(2,1)S(1)}, bf16[128,768]{1,0:T(8,128)(2,1)S(1)}, u32[]{:S(2)}, u32[]{:S(2)}) collective-permute-start(bf16[128,768]{1,0:T(8,128)(2,1)S(1)} %get-tuple-element.42.f0), channel_id=1, source_target_pairs={{0,256},{8,264},{16,272},{24,280},{32,288},{40,296},{48,304},{56,3... | collective-permute-start | bytes 589832 | tf_op jit(solution)/shard_map/ppermute | solution.py:361
  156.1 31.0 %collective-permute-start.10 = (bf16[128,768]{1,0:T(8,128)(2,1)S(1)}, bf16[128,768]{1,0:T(8,128)(2,1)S(1)}, u32[]{:S(2)}, u32[]{:S(2)}) collective-permute-start(bf16[128,768]{1,0:T(8,128)(2,1)S(1)} %get-tuple-element.42.f0), channel_id=1, source_target_pairs={{0,384},{8,392},{16,400},{24,408},{32,416},{40,424},{48,432},{56,4... | collective-permute-start | bytes 589832 | tf_op jit(solution)/shard_map/ppermute | solution.py:361
  187.1 13.0 %collective-permute-start.11 = (bf16[512,512]{1,0:T(8,128)(2,1)S(1)}, bf16[512,512]{1,0:T(8,128)(2,1)S(1)}, u32[]{:S(2)}, u32[]{:S(2)}) collective-permute-start(bf16[512,512]{1,0:T(8,128)(2,1)S(1)} %pad_maximum_fusion.4.refs_2_), channel_id=1, source_target_pairs={{0,8},{8,16},{16,24},{24,32},{32,40},{40,48},{48,56},{56,64},{64,7... | collective-permute-start | bytes 1572872 | tf_op jit(solution)/shard_map/ppermute | solution.py:294
  188.5 14.8 %collective-permute-start.12 = (bf16[512,512]{1,0:T(8,128)(2,1)S(1)}, bf16[512,512]{1,0:T(8,128)(2,1)S(1)}, u32[]{:S(2)}, u32[]{:S(2)}) collective-permute-start(bf16[512,512]{1,0:T(8,128)(2,1)S(1)} %pad_maximum_fusion.4.refs_2_), channel_id=1, source_target_pairs={{8,0},{16,8},{24,16},{32,24},{40,32},{48,40},{56,48},{64,56},{72,6... | collective-permute-start | bytes 1572872 | tf_op jit(solution)/shard_map/ppermute | solution.py:295
  211.0 52.8 %all-to-all-start.1 = ((bf16[64,8,512]{2,1,0:T(8,128)(2,1)}), bf16[64,8,512]{2,1,0:T(8,128)(2,1)S(1)}, u32[]{:S(2)}, u32[]{:S(2)}) async-start(bf16[64,8,512]{2,1,0:T(8,128)(2,1)} %bitcast.14), calls=%async_computation.1 | async-start | bytes 1048576 | tf_op jit(solution)/shard_map/all_to_all | solution.py:290
  234.9 69.8 %all-gather.10.cloned.1.call-start = ((), (), s32[]{:S(2)}) async-start(), calls=%async_computation.4 | async-start | bytes 4718592 | tf_op jit(solution)/shard_map/all_gather | solution.py:379
  264.9 1.7 copy-start
  266.5 1.6 copy-start.1
  270.1 1.2 copy-start.2
  271.3 1.2 copy-start.3
Sparse Core Ops, SparseCore 0:
  38.2 96.9 all-gather.11
  138.2 68.8 all-gather.7
  211.1 45.9 all-gather.5
  264.9 39.7 all-gather.9

commit v5 on v4

--- a/solution.py
+++ b/solution.py
@@ -14,7 +14,7 @@
 F32 = jnp.float32
 RATE = math.log2(math.e) / math.sqrt(HEAD_DIM)
 SPAN = 2 * REACH + 1
-COVER = 1 << 35
+COVER = 1 << 36
 
 
 def lanes(index):
@@ -25,11 +25,14 @@
 SMEM = pl.BlockSpec(memory_space=pltpu.SMEM)
 
 
-def near_kernel(heads, bits, q_ref, own_ref, left_ref, right_ref, acc_ref, stat_ref, s_ref, m_ref, l_ref):
+def attention_kernel(heads, bits, q_ref, own_ref, left_ref, right_ref, f0, f1, f2, f3, out_ref, s_ref, m_ref, l_ref, acc_ref):
     sides = (left_ref, left_ref, own_ref, own_ref, right_ref, right_ref)
 
-    def tile(kind, place, slot):
-        return sides[place][:, lanes((kind * 2 + place % 2) * heads + slot)]
+    def tile(kind, b, n, slot):
+        if n == SPAN:
+            column = kind * 2 + slot if heads == 2 else 4 + kind
+            return jnp.concatenate([f[:, lanes(column)] for f in (f0, f1, f2, f3)], axis=0)
+        return sides[b + n][:, lanes((kind * 2 + (b + n) % 2) * heads + slot)]
 
     for slot in range(heads):
         for b in range(2):
@@ -37,13 +40,13 @@
             query = q_ref[:, here]
             m_ref[...] = jnp.full_like(m_ref, -jnp.inf)
             l_ref[...] = jnp.zeros_like(l_ref)
-            acc_ref[:, here] = jnp.zeros_like(m_ref)
-            for n in range(SPAN):
+            acc_ref[...] = jnp.zeros_like(acc_ref)
+            for n in range(SPAN + 1):
 
                 @pl.when(bits[b, n] > 0)
                 def _():
                     s = lax.dot_general(
-                        query, tile(0, b + n, slot), (((1,), (1,)), ((), ())), preferred_element_type=F32
+                        query, tile(0, b, n, slot), (((1,), (1,)), ((), ())), preferred_element_type=F32
                     )
                     s_ref[n] = s
                     m = m_ref[...]
@@ -52,7 +55,7 @@
                     m_ref[...] = m
 
             m_ref[...] = jnp.broadcast_to(jnp.max(m_ref[...], axis=1, keepdims=True), m_ref.shape)
-            for n in range(SPAN):
+            for n in range(SPAN + 1):
 
                 @pl.when(bits[b, n] > 0)
                 def _():
@@ -64,25 +67,24 @@
                         total = total + w
                         parts.append(w.astype(BF))
                     l_ref[...] = total
-                    acc_ref[:, here] += jnp.dot(
-                        jnp.concatenate(parts, axis=1), tile(1, b + n, slot), preferred_element_type=F32
+                    acc_ref[...] += jnp.dot(
+                        jnp.concatenate(parts, axis=1), tile(1, b, n, slot), preferred_element_type=F32
                     )
 
             total = jnp.sum(l_ref[...], axis=1, keepdims=True)
-            lane = lax.broadcasted_iota(jnp.int32, m_ref.shape, 1)
-            stat_ref[:, here] = jnp.where(lane < HEAD_DIM // 2, m_ref[...], total)
-
-
-def near_attention(heads, bits, query, own, left, right):
-    state = jax.ShapeDtypeStruct(query.shape, F32)
-    pairs = heads * 2 * SPAN
-    return pl.pallas_call(
-        lambda *refs: near_kernel(heads, *refs),
-        out_shape=(state, state),
-        in_specs=[SMEM] + [VMEM] * 4,
-        out_specs=(VMEM, VMEM),
+            out_ref[:, here] = (acc_ref[...] / total).astype(BF)
+
+
+def attention(heads, bits, query, own, left, right, first):
+    pairs = heads * 2 * (SPAN + 1)
+    return pl.pallas_call(
+        lambda *refs: attention_kernel(heads, *refs),
+        out_shape=jax.ShapeDtypeStruct(query.shape, BF),
+        in_specs=[SMEM] + [VMEM] * 8,
+        out_specs=VMEM,
         scratch_shapes=[
-            pltpu.VMEM((SPAN, BLOCK, BLOCK), F32),
+            pltpu.VMEM((SPAN + 1, BLOCK, BLOCK), F32),
+            pltpu.VMEM((BLOCK, HEAD_DIM), F32),
             pltpu.VMEM((BLOCK, HEAD_DIM), F32),
             pltpu.VMEM((BLOCK, HEAD_DIM), F32),
         ],
@@ -92,55 +94,7 @@
             bytes_accessed=heads * 16 * BLOCK * HEAD_DIM * 2,
             transcendentals=pairs * BLOCK * BLOCK,
         ),
-    )(bits, query, own, left, right)
-
-
-def first_kernel(bits, qm_ref, am_ref, sm_ref, qs_ref, as_ref, ss_ref, f0, f1, f2, f3, outm_ref, outs_ref):
-    quarters = (f0, f1, f2, f3)
-
-    def block(column):
-        return jnp.concatenate([f[:, lanes(column)] for f in quarters], axis=0)
-
-    for slot in range(3):
-        heads = 1 if slot == 2 else 2
-        q_ref, acc_ref, stat_ref, out_ref = (
-            (qs_ref, as_ref, ss_ref, outs_ref) if slot == 2 else (qm_ref, am_ref, sm_ref, outm_ref)
-        )
-        key, val = ((0, 2), (1, 3), (4, 5))[slot]
-        for b in range(2):
-            here = lanes(b * heads + slot % 2)
-            start = here.start
-            total = stat_ref[:, start + HEAD_DIM - 1 : start + HEAD_DIM]
-
-            @pl.when(bits[b, SPAN] > 0)
-            def _():
-                peak = stat_ref[:, start : start + 1]
-                s = lax.dot_general(q_ref[:, here], block(key), (((1,), (1,)), ((), ())), preferred_element_type=F32)
-                top = jnp.maximum(peak, jnp.max(s, axis=1, keepdims=True))
-                keep = jnp.exp2((peak - top) * RATE)
-                w = jnp.exp2((s - top) * RATE)
-                mixed = acc_ref[:, here] * keep + jnp.dot(w.astype(BF), block(val), preferred_element_type=F32)
-                out_ref[:, here] = (mixed / (total * keep + jnp.sum(w, axis=1, keepdims=True))).astype(BF)
-
-            @pl.when(bits[b, SPAN] <= 0)
-            def _():
-                out_ref[:, here] = (acc_ref[:, here] / total).astype(BF)
-
-
-def first_attention(bits, mixed, spatial, first):
-    pairs = 6
-    return pl.pallas_call(
-        first_kernel,
-        out_shape=(jax.ShapeDtypeStruct(mixed[0].shape, BF), jax.ShapeDtypeStruct(spatial[0].shape, BF)),
-        in_specs=[SMEM] + [VMEM] * 10,
-        out_specs=(VMEM, VMEM),
-        compiler_params=pltpu.CompilerParams(vmem_limit_bytes=32 << 20),
-        cost_estimate=pl.CostEstimate(
-            flops=pairs * 4 * BLOCK * BLOCK * HEAD_DIM,
-            bytes_accessed=pairs * 8 * BLOCK * HEAD_DIM * 2,
-            transcendentals=pairs * BLOCK * BLOCK,
-        ),
-    )(bits, *mixed, *spatial, *first)
+    )(bits, query, own, left, right, *first)
 
 
 def mix_kernel(moves, moved_ref, q1_ref, k1_ref, v1_ref, query_ref, own_ref):
@@ -266,7 +220,7 @@
             pl.BlockSpec(w.shape, lambda i: (0, 0)),
         ],
         out_specs=pl.BlockSpec((tile, cols), lambda i: (i, 0)),
-        compiler_params=pltpu.CompilerParams(vmem_limit_bytes=60 << 20),
+        compiler_params=pltpu.CompilerParams(vmem_limit_bytes=32 << 20),
     )(part, mixed, w)
 
 
@@ -362,13 +316,13 @@
 
     first = [quarter] + along_y(quarter)
     left, right, first = lax.optimization_barrier((left, right, first))
+    w_z, *first = lax.optimization_barrier((w_z, *first))
     w = lax.all_gather(w_z, "ctx", axis=0, axis_index_groups=y_lines, tiled=True)
 
-    mixed = near_attention(2, bits, query, own, left, right)
+    out = attention(2, bits, query, own, left, right, first)
     own2, _, _ = lax.optimization_barrier((own2, left, right))
-    query2 = split_blocks(q2)
-    spatial = near_attention(1, bits, query2, own2, *both_ways(own2, parts))
-    out, out2 = first_attention(bits, (query, *mixed), (query2, *spatial), first)
+    query2, _ = lax.optimization_barrier((split_blocks(q2), out))
+    out2 = attention(1, bits, query2, own2, *both_ways(own2, parts), first)
     attn2 = jnp.concatenate([out2[:, lanes(0)], out2[:, lanes(1)]], axis=0)
     spatial = lax.all_gather(attn2, "head", axis=1, tiled=True)
 

time: 319 us -> 316 us (level)
  starting transfers between devices: 77.4 us -> 69.3 us
  waiting for transfers between devices: 172 us -> 180 us
  Pallas kernels: 28.2 us -> 22.2 us
    all_gather x1, waiting for transfers between devices: 32.3 us -> 41.6 us  [body(): mixed = lax.all_gather(attn, 'head', axis=1, tiled=True)]
    all_to_all x2, starting transfers between devices: 37.9 us -> 28.6 us  [exchange(): return lax.all_to_all(x, 'ctx', 0, 0, tiled=True)]
    ppermute x3, waiting for transfers between devices: 28.1 us -> 22.9 us  [along_y(): lax.ppermute(x, 'ctx', [(i, i ^ deep * k) for i in range(parts)])]
    unnamed x28 -> x48, local copies, waits for them, and re-layouts: 10.8 us -> 13.5 us
    pallas_call x3 -> x2, Pallas kernels: 16.2 us -> 14 us  [attention(): pl.pallas_call(lambda *refs: attention_kernel(heads, *refs), out_shape=ja...]
  transfers between devices with their start and end apart: 19 -> 19, of which waited for: 7 -> 9; matrix products, arithmetic and copies ran while one was open for 3% -> 4% of each run, Pallas kernels for 7% -> 6%
where the time goes in v5:
time: 316 us; the launch traced here: 315 us
  waiting for transfers between devices  180 us (57%)
  starting transfers between devices  69.3 us (22%)
  Pallas kernels  22.2 us (7%)
  local copies, waits for them, and re-layouts  19.8 us (6%)
  between operations  18.2 us (6%)
  other arithmetic  5.29 us (2%)
    all_gather x1, waiting for transfers between devices, body(): rows_z = lax.all_gather(sent, 'ctx', axis=0, axis_index_groups=along_z)  80.7 us
    all_gather x1, waiting for transfers between devices, body(): mixed = lax.all_gather(attn, 'head', axis=1, tiled=True)  41.6 us
    all_to_all x2, starting transfers between devices, exchange(): return lax.all_to_all(x, 'ctx', 0, 0, tiled=True)  28.6 us
    all_to_all x2, waiting for transfers between devices, exchange(): return lax.all_to_all(x, 'ctx', 0, 0, tiled=True)  27.3 us
    ppermute x3, waiting for transfers between devices, along_y(): lax.ppermute(x, 'ctx', [(i, i ^ deep * k) for i in range(parts)])  22.9 us
    ppermute x6, starting transfers between devices, scattered(): lax.ppermute(x[k * rows:(k + 1) * rows], 'ctx', [(i, i + k * unit) for i...  20.4 us
    pallas_call x2, Pallas kernels, attention(): pl.pallas_call(lambda *refs: attention_kernel(heads, *refs), out_shape=ja...  14 us
    unnamed x48, local copies, waits for them, and re-layouts  13.5 us
  transfers between devices with their start and end apart: 19, of which 9 were waited for; matrix products, arithmetic and copies ran while one was open for 4% of the time, Pallas kernels for 6%

profile of v5, /device:TPU:1, one launch (start us, length us, event | category | flops | bytes accessed | tf_op | source)
XLA Modules:
  0.0 314.9 jit_solution(13136869082497580097)
XLA Ops:
  6.5 0.7 broadcast_compare_fusion.1
  7.2 0.1 eq.51
  7.3 0.1 select_select_fusion.1
  7.4 0.7 fusion.11
  10.0 1.5 constant_dynamic-slice_fusion.7
  11.6 5.6 %collective-permute-start = (bf16[128,512]{1,0:T(8,128)(2,1)S(1)}, bf16[128,512]{1,0:T(8,128)(2,1)S(1)}, u32[]{:S(2)}, u32[]{:S(2)}) collective-permute-start(bf16[128,512]{1,0:T(8,128)(2,1)S(1)} %get-tuple-element.56), channel_id=1, source_target_pairs={{0,384},{1,385},{2,386},{3,387},{4,388},{5,389},{6,390},{7,391}} | collective-permute-start | bytes 393224 | tf_op jit(solution)/shard_map/ppermute | solution.py:258
  17.2 1.3 collective-permute-start.1
  18.5 1.3 collective-permute-start.2
  19.8 0.1 pad_maximum_fusion.3
  19.9 0.1 pad_maximum_fusion.2
  20.0 0.1 constant_dynamic-slice_fusion.14
  20.1 0.5 copy-done.17
  20.6 0.7 constant_dynamic-update-slice_fusion.7
  21.3 1.3 pad_maximum_fusion
  22.6 0.7 constant_dynamic-update-slice_fusion.6
  23.3 0.7 constant_dynamic-update-slice_fusion.5
  24.1 7.2 %collective-permute-start.3 = (bf16[32,512]{1,0:T(8,128)(2,1)S(1)}, bf16[32,512]{1,0:T(8,128)(2,1)S(1)}, u32[]{:S(2)}, u32[]{:S(2)}) collective-permute-start(bf16[32,512]{1,0:T(8,128)(2,1)S(1)} %get-tuple-element.80), channel_id=1, source_target_pairs={{0,96},{128,224},{256,352},{384,480},{1,97},{129,225},{257,353},{3... | collective-permute-start | bytes 98312 | tf_op jit(solution)/shard_map/ppermute | solution.py:258
  31.4 3.7 %collective-permute-start.4 = (bf16[32,512]{1,0:T(8,128)(2,1)S(1)}, bf16[32,512]{1,0:T(8,128)(2,1)S(1)}, u32[]{:S(2)}, u32[]{:S(2)}) collective-permute-start(bf16[32,512]{1,0:T(8,128)(2,1)S(1)} %get-tuple-element.79), channel_id=1, source_target_pairs={{0,64},{128,192},{256,320},{384,448},{1,65},{129,193},{257,321},{3... | collective-permute-start | bytes 98312 | tf_op jit(solution)/shard_map/ppermute | solution.py:258
  35.0 1.3 collective-permute-start.5
  36.3 0.7 constant_dynamic-update-slice_fusion.4
  37.0 0.4 collective-permute-done.5
  37.4 0.6 copy-done.16
  40.2 0.6 dynamic_slice.43.moves
  40.8 14.0 %all-to-all-start = ((bf16[64,8,1536]{2,1,0:T(8,128)(2,1)}), bf16[64,8,1536]{2,1,0:T(8,128)(2,1)S(1)}, u32[]{:S(2)}, u32[]{:S(2)}) async-start(bf16[64,8,1536]{2,1,0:T(8,128)(2,1)} %pad_maximum_fusion), calls=%async_computation | async-start | bytes 3145728 | tf_op jit(solution)/shard_map/all_to_all | solution.py:244
  54.9 80.7 %all-gather.12.cloned.1.call-done = bf16[4864,128]{1,0:T(8,128)(2,1)} async-done(((bf16[304,128]{1,0:T(8,128)(2,1)}), bf16[4864,128]{1,0:T(8,128)(2,1)}) %all-gather.12.cloned.1.call-update) | async-done | bytes 1245200 | tf_op jit(solution)/shard_map/all_gather | solution.py:308
  135.6 1.3 copy-done.3
  136.9 1.6 shard_map.64
  138.5 0.7 copy-done.6
  139.1 1.1 shard_map.65
  140.3 0.8 copy-done.4
  141.1 5.0 %collective-permute-start.6 = (bf16[512,1024]{1,0:T(8,128)(2,1)S(1)}, bf16[512,1024]{1,0:T(8,128)(2,1)S(1)}, u32[]{:S(2)}, u32[]{:S(2)}) collective-permute-start(bf16[512,1024]{1,0:T(8,128)(2,1)S(1)} %get-tuple-element.33.refs_2_), channel_id=1, source_target_pairs={{0,8},{8,16},{16,24},{24,32},{32,40},{40,48},{48,56},{56,64},{64,7... | collective-permute-start | bytes 3145736 | tf_op jit(solution)/shard_map/ppermute | solution.py:248
  146.1 1.3 collective-permute-start.7
  147.4 4.7 %collective-permute-start.8 = (bf16[128,768]{1,0:T(8,128)(2,1)S(1)}, bf16[128,768]{1,0:T(8,128)(2,1)S(1)}, u32[]{:S(2)}, u32[]{:S(2)}) collective-permute-start(bf16[128,768]{1,0:T(8,128)(2,1)S(1)} %copy-done.7), channel_id=1, source_target_pairs={{0,128},{8,136},{16,144},{24,152},{32,160},{40,168},{48,176},{56,1... | collective-permute-start | bytes 589832 | tf_op jit(solution)/shard_map/ppermute | solution.py:315
  152.1 4.7 %collective-permute-start.9 = (bf16[128,768]{1,0:T(8,128)(2,1)S(1)}, bf16[128,768]{1,0:T(8,128)(2,1)S(1)}, u32[]{:S(2)}, u32[]{:S(2)}) collective-permute-start(bf16[128,768]{1,0:T(8,128)(2,1)S(1)} %copy-done.7), channel_id=1, source_target_pairs={{0,256},{8,264},{16,272},{24,280},{32,288},{40,296},{48,304},{56,3... | collective-permute-start | bytes 589832 | tf_op jit(solution)/shard_map/ppermute | solution.py:315
  156.8 1.9 collective-permute-start.10
  158.7 15.2 %collective-permute-done.8.refs_6_ = bf16[128,768]{1,0:T(8,128)(2,1)S(1)} collective-permute-done((bf16[128,768]{1,0:T(8,128)(2,1)S(1)}, bf16[128,768]{1,0:T(8,128)(2,1)S(1)}, u32[]{:S(2)}, u32[]{:S(2)}) %collective-permute-start.8) | collective-permute-done | bytes 196640 | tf_op jit(solution)/shard_map/ppermute | solution.py:315
  173.9 7.7 %collective-permute-done.9.refs_7_ = bf16[128,768]{1,0:T(8,128)(2,1)S(1)} collective-permute-done((bf16[128,768]{1,0:T(8,128)(2,1)S(1)}, bf16[128,768]{1,0:T(8,128)(2,1)S(1)}, u32[]{:S(2)}, u32[]{:S(2)}) %collective-permute-start.9) | collective-permute-done | bytes 196640 | tf_op jit(solution)/shard_map/ppermute | solution.py:315
  181.6 0.7 copy-done.11
  182.3 0.7 copy-done.13
  183.0 0.7 broadcast_compare_fusion
  183.8 0.2 fusion.6
  184.1 1.1 constant_dynamic-slice_fusion.6
  185.2 1.1 constant_dynamic-slice_fusion
  186.4 1.3 collective-permute-start.11
  187.7 1.3 collective-permute-start.12
  189.0 0.1 add_convert_fusion.refs_0_
  189.2 9.4 %shard_map.66 = bf16[512,512]{1,0:T(8,128)(2,1)} custom-call(s32[2,6]{1,0:T(2,128)S(1)} %add_convert_fusion.refs_0_, bf16[512,512]{1,0:T(8,128)(2,1)S(1)} %copy-done.5, bf16[512,1024]{1,0:T(8,128)(2,1)S(1)} %get-tuple-element.33.refs_2_, bf16[512,1024]{1,0:T(8,128)(2,1)S(1)} %collective-permute-done.6.refs_3_, ...), custom_call_target="tpu_custom_call" | custom-call | flops 3221225472 | bytes 4194304 | tf_op jit(solution)/shard_map/pallas_call | solution.py:80
  198.6 0.2 collective-permute-done.11.refs_3_
  198.8 3.9 %collective-permute-done.12.refs_4_ = bf16[512,512]{1,0:T(8,128)(2,1)S(1)} collective-permute-done((bf16[512,512]{1,0:T(8,128)(2,1)S(1)}, bf16[512,512]{1,0:T(8,128)(2,1)S(1)}, u32[]{:S(2)}, u32[]{:S(2)}) %collective-permute-start.12) | collective-permute-done | bytes 524320 | tf_op jit(solution)/shard_map/ppermute | solution.py:249
  202.7 4.6 %shard_map.67 = bf16[512,256]{1,0:T(8,128)(2,1)S(1)} custom-call(s32[2,6]{1,0:T(2,128)S(1)} %add_convert_fusion.refs_0_, bf16[512,256]{1,0:T(8,128)(2,1)S(1)} %pad_maximum_fusion.6.refs_1_, bf16[512,512]{1,0:T(8,128)(2,1)S(1)} %pad_maximum_fusion.4.refs_2_, bf16[512,512]{1,0:T(8,128)(2,1)S(1)} %collective-permute-done.11.refs_3_, ...), custom_call_target="tpu_custom_call" | custom-call | flops 1610612736 | bytes 2097152 | tf_op jit(solution)/shard_map/pallas_call | solution.py:80
  207.4 0.7 pad_maximum_fusion.7
  208.2 14.6 %all-to-all-start.1 = ((bf16[64,8,512]{2,1,0:T(8,128)(2,1)}), bf16[64,8,512]{2,1,0:T(8,128)(2,1)S(1)}, u32[]{:S(2)}, u32[]{:S(2)}) async-start(bf16[64,8,512]{2,1,0:T(8,128)(2,1)} %bitcast.14), calls=%async_computation.1 | async-start | bytes 1048576 | tf_op jit(solution)/shard_map/all_to_all | solution.py:244
  223.5 1.0 fusion.8
  224.5 27.3 %all-to-all-done.1 = bf16[64,8,512]{2,1,0:T(8,128)(2,1)S(1)} async-done(((bf16[64,8,512]{2,1,0:T(8,128)(2,1)}), bf16[64,8,512]{2,1,0:T(8,128)(2,1)S(1)}, u32[]{:S(2)}, u32[]{:S(2)}) %all-to-all-start.1) | async-done | bytes 524320 | tf_op jit(solution)/shard_map/all_to_all | solution.py:244
  251.7 0.1 fusion.7
  251.8 0.9 pad_maximum_fusion.5
  252.7 0.1 add.92.refs_0_
  252.8 3.1 all-gather.6.cloned.1.call-done.refs_1_
  255.9 1.7 copy-done.1
  257.6 1.6 copy-done.2
  259.1 1.9 shard_map.68
  261.1 41.6 %all-gather.10.cloned.1.call-done.mixed_ref = bf16[1024,2048]{1,0:T(8,128)(2,1)} async-done(((bf16[1024,256]{1,0:T(8,128)(2,1)}), bf16[1024,2048]{1,0:T(8,128)(2,1)}) %all-gather.10.cloned.1.call-update) | async-done | bytes 4194320 | tf_op jit(solution)/shard_map/all_gather | solution.py:333
  302.7 2.2 copy-done
  304.9 3.5 %shard_map.69 = bf16[1024,384]{1,0:T(8,128)(2,1)} custom-call(f32[1024,384]{1,0:T(8,128)S(1)} %get-tuple-element.49.part_ref, bf16[1024,2048]{1,0:T(8,128)(2,1)S(1)} %copy-done, bf16[2048,384]{1,0:T(8,128)(2,1)S(1)} %get-tuple-element.50.w_ref), custom_call_target="tpu_custom_call" | custom-call | tf_op jit(solution)/shard_map/pallas_call | solution.py:213
  (68 shorter events, 0.8 us)
Async XLA Ops:
  6.5 129.1 %all-gather.12.cloned.1.call-start = ((), (), s32[]{:S(2)}) async-start(), calls=%async_computation.5 | async-start | bytes 1323008 | tf_op jit(solution)/shard_map/all_gather | solution.py:308
  11.5 8.5 %copy-start.15 = (bf16[1024,384]{1,0:T(8,128)(2,1)S(1)}, bf16[1024,384]{1,0:T(8,128)(2,1)}, u32[]{:S(2)}) copy-start(bf16[1024,384]{1,0:T(8,128)(2,1)} %param.6) | copy-start | bytes 2359300
  11.6 12.4 %collective-permute-start = (bf16[128,512]{1,0:T(8,128)(2,1)S(1)}, bf16[128,512]{1,0:T(8,128)(2,1)S(1)}, u32[]{:S(2)}, u32[]{:S(2)}) collective-permute-start(bf16[128,512]{1,0:T(8,128)(2,1)S(1)} %get-tuple-element.56), channel_id=1, source_target_pairs={{0,384},{1,385},{2,386},{3,387},{4,388},{5,389},{6,390},{7,391}} | collective-permute-start | bytes 393224 | tf_op jit(solution)/shard_map/ppermute | solution.py:258
  17.2 6.8 %collective-permute-start.1 = (bf16[128,512]{1,0:T(8,128)(2,1)S(1)}, bf16[128,512]{1,0:T(8,128)(2,1)S(1)}, u32[]{:S(2)}, u32[]{:S(2)}) collective-permute-start(bf16[128,512]{1,0:T(8,128)(2,1)S(1)} %get-tuple-element.57), channel_id=1, source_target_pairs={{0,256},{1,257},{2,258},{3,259},{4,260},{5,261},{6,262},{7,263}} | collective-permute-start | bytes 393224 | tf_op jit(solution)/shard_map/ppermute | solution.py:258
  18.5 5.5 %collective-permute-start.2 = (bf16[128,512]{1,0:T(8,128)(2,1)S(1)}, bf16[128,512]{1,0:T(8,128)(2,1)S(1)}, u32[]{:S(2)}, u32[]{:S(2)}) collective-permute-start(bf16[128,512]{1,0:T(8,128)(2,1)S(1)} %get-tuple-element.55), channel_id=1, source_target_pairs={{0,128},{1,129},{2,130},{3,131},{4,132},{5,133},{6,134},{7,135}} | collective-permute-start | bytes 393224 | tf_op jit(solution)/shard_map/ppermute | solution.py:258
  19.8 0.8 copy-start.17
  22.6 17.6 %copy-start.18 = (s32[24]{0:T(128)S(1)}, s32[24]{0:T(128)}, u32[]{:S(2)}) copy-start(s32[24]{0:T(128)} %param.10) | copy-start | bytes 292
  24.1 12.9 %collective-permute-start.3 = (bf16[32,512]{1,0:T(8,128)(2,1)S(1)}, bf16[32,512]{1,0:T(8,128)(2,1)S(1)}, u32[]{:S(2)}, u32[]{:S(2)}) collective-permute-start(bf16[32,512]{1,0:T(8,128)(2,1)S(1)} %get-tuple-element.80), channel_id=1, source_target_pairs={{0,96},{128,224},{256,352},{384,480},{1,97},{129,225},{257,353},{3... | collective-permute-start | bytes 98312 | tf_op jit(solution)/shard_map/ppermute | solution.py:258
  31.4 5.7 %collective-permute-start.4 = (bf16[32,512]{1,0:T(8,128)(2,1)S(1)}, bf16[32,512]{1,0:T(8,128)(2,1)S(1)}, u32[]{:S(2)}, u32[]{:S(2)}) collective-permute-start(bf16[32,512]{1,0:T(8,128)(2,1)S(1)} %get-tuple-element.79), channel_id=1, source_target_pairs={{0,64},{128,192},{256,320},{384,448},{1,65},{129,193},{257,321},{3... | collective-permute-start | bytes 98312 | tf_op jit(solution)/shard_map/ppermute | solution.py:258
  35.0 2.4 collective-permute-start.5
  37.4 0.6 copy-start.16
  40.8 98.3 %all-to-all-start = ((bf16[64,8,1536]{2,1,0:T(8,128)(2,1)}), bf16[64,8,1536]{2,1,0:T(8,128)(2,1)S(1)}, u32[]{:S(2)}, u32[]{:S(2)}) async-start(bf16[64,8,1536]{2,1,0:T(8,128)(2,1)} %pad_maximum_fusion), calls=%async_computation | async-start | bytes 3145728 | tf_op jit(solution)/shard_map/all_to_all | solution.py:244
  54.8 198.0 %all-gather.8.cloned.1.call-start = ((), (), s32[]{:S(2)}) async-start(), calls=%async_computation.3 | async-start | bytes 2949120 | tf_op jit(solution)/shard_map/all_gather | solution.py:320
  135.6 1.3 copy-start.3
  138.5 0.7 copy-start.6
  139.1 8.2 %copy-start.7 = (bf16[128,768]{1,0:T(8,128)(2,1)S(1)}, bf16[128,768]{1,0:T(8,128)(2,1)}, u32[]{:S(2)}) copy-start(bf16[128,768]{1,0:T(8,128)(2,1)} %copy-done.6) | copy-start | bytes 589828
  140.3 0.8 copy-start.4
  141.1 41.9 %collective-permute-start.6 = (bf16[512,1024]{1,0:T(8,128)(2,1)S(1)}, bf16[512,1024]{1,0:T(8,128)(2,1)S(1)}, u32[]{:S(2)}, u32[]{:S(2)}) collective-permute-start(bf16[512,1024]{1,0:T(8,128)(2,1)S(1)} %get-tuple-element.33.refs_2_), channel_id=1, source_target_pairs={{0,8},{8,16},{16,24},{24,32},{32,40},{40,48},{48,56},{56,64},{64,7... | collective-permute-start | bytes 3145736 | tf_op jit(solution)/shard_map/ppermute | solution.py:248
  146.1 36.9 %collective-permute-start.7 = (bf16[512,1024]{1,0:T(8,128)(2,1)S(1)}, bf16[512,1024]{1,0:T(8,128)(2,1)S(1)}, u32[]{:S(2)}, u32[]{:S(2)}) collective-permute-start(bf16[512,1024]{1,0:T(8,128)(2,1)S(1)} %get-tuple-element.33.refs_2_), channel_id=1, source_target_pairs={{8,0},{16,8},{24,16},{32,24},{40,32},{48,40},{56,48},{64,56},{72,6... | collective-permute-start | bytes 3145736 | tf_op jit(solution)/shard_map/ppermute | solution.py:249
  147.4 26.5 %collective-permute-start.8 = (bf16[128,768]{1,0:T(8,128)(2,1)S(1)}, bf16[128,768]{1,0:T(8,128)(2,1)S(1)}, u32[]{:S(2)}, u32[]{:S(2)}) collective-permute-start(bf16[128,768]{1,0:T(8,128)(2,1)S(1)} %copy-done.7), channel_id=1, source_target_pairs={{0,128},{8,136},{16,144},{24,152},{32,160},{40,168},{48,176},{56,1... | collective-permute-start | bytes 589832 | tf_op jit(solution)/shard_map/ppermute | solution.py:315
  152.1 29.5 %collective-permute-start.9 = (bf16[128,768]{1,0:T(8,128)(2,1)S(1)}, bf16[128,768]{1,0:T(8,128)(2,1)S(1)}, u32[]{:S(2)}, u32[]{:S(2)}) collective-permute-start(bf16[128,768]{1,0:T(8,128)(2,1)S(1)} %copy-done.7), channel_id=1, source_target_pairs={{0,256},{8,264},{16,272},{24,280},{32,288},{40,296},{48,304},{56,3... | collective-permute-start | bytes 589832 | tf_op jit(solution)/shard_map/ppermute | solution.py:315
  156.8 25.5 %collective-permute-start.10 = (bf16[128,768]{1,0:T(8,128)(2,1)S(1)}, bf16[128,768]{1,0:T(8,128)(2,1)S(1)}, u32[]{:S(2)}, u32[]{:S(2)}) collective-permute-start(bf16[128,768]{1,0:T(8,128)(2,1)S(1)} %copy-done.7), channel_id=1, source_target_pairs={{0,384},{8,392},{16,400},{24,408},{32,416},{40,424},{48,432},{56,4... | collective-permute-start | bytes 589832 | tf_op jit(solution)/shard_map/ppermute | solution.py:315
  173.9 9.9 %copy-start.9 = (bf16[128,768]{1,0:T(8,128)(2,1)}, bf16[128,768]{1,0:T(8,128)(2,1)S(1)}, u32[]{:S(2)}) copy-start(bf16[128,768]{1,0:T(8,128)(2,1)S(1)} %collective-permute-done.8.refs_6_) | copy-start | bytes 589828
  181.6 0.7 copy-start.11
  182.3 0.7 copy-start.13
  183.0 72.9 %all-gather.6.cloned.1.call-start = ((), (), s32[]{:S(2)}) async-start(), calls=%async_computation.2 | async-start | bytes 2359296 | tf_op jit(solution)/shard_map/all_gather | solution.py:327
  184.0 5.1 %copy-start.5 = (bf16[512,512]{1,0:T(8,128)(2,1)S(1)}, bf16[512,512]{1,0:T(8,128)(2,1)}, u32[]{:S(2)}) copy-start(bf16[512,512]{1,0:T(8,128)(2,1)} %copy-done.4) | copy-start | bytes 1572868
  184.0 5.1 %copy-start.8 = (bf16[128,768]{1,0:T(8,128)(2,1)S(1)}, bf16[128,768]{1,0:T(8,128)(2,1)}, u32[]{:S(2)}) copy-start(bf16[128,768]{1,0:T(8,128)(2,1)} %copy-done.6) | copy-start | bytes 589828
  184.0 5.1 %copy-start.10 = (bf16[128,768]{1,0:T(8,128)(2,1)S(1)}, bf16[128,768]{1,0:T(8,128)(2,1)}, u32[]{:S(2)}) copy-start(bf16[128,768]{1,0:T(8,128)(2,1)} %copy-done.9) | copy-start | bytes 589828
  184.1 5.1 %copy-start.12 = (bf16[128,768]{1,0:T(8,128)(2,1)S(1)}, bf16[128,768]{1,0:T(8,128)(2,1)}, u32[]{:S(2)}) copy-start(bf16[128,768]{1,0:T(8,128)(2,1)} %copy-done.11) | copy-start | bytes 589828
  184.1 5.1 %copy-start.14 = (bf16[128,768]{1,0:T(8,128)(2,1)S(1)}, bf16[128,768]{1,0:T(8,128)(2,1)}, u32[]{:S(2)}) copy-start(bf16[128,768]{1,0:T(8,128)(2,1)} %copy-done.13) | copy-start | bytes 589828
  186.4 12.4 %collective-permute-start.11 = (bf16[512,512]{1,0:T(8,128)(2,1)S(1)}, bf16[512,512]{1,0:T(8,128)(2,1)S(1)}, u32[]{:S(2)}, u32[]{:S(2)}) collective-permute-start(bf16[512,512]{1,0:T(8,128)(2,1)S(1)} %pad_maximum_fusion.4.refs_2_), channel_id=1, source_target_pairs={{0,8},{8,16},{16,24},{24,32},{32,40},{40,48},{48,56},{56,64},{64,7... | collective-permute-start | bytes 1572872 | tf_op jit(solution)/shard_map/ppermute | solution.py:248
  187.7 15.0 %collective-permute-start.12 = (bf16[512,512]{1,0:T(8,128)(2,1)S(1)}, bf16[512,512]{1,0:T(8,128)(2,1)S(1)}, u32[]{:S(2)}, u32[]{:S(2)}) collective-permute-start(bf16[512,512]{1,0:T(8,128)(2,1)S(1)} %pad_maximum_fusion.4.refs_2_), channel_id=1, source_target_pairs={{8,0},{16,8},{24,16},{32,24},{40,32},{48,40},{56,48},{64,56},{72,6... | collective-permute-start | bytes 1572872 | tf_op jit(solution)/shard_map/ppermute | solution.py:249
  208.2 43.6 %all-to-all-start.1 = ((bf16[64,8,512]{2,1,0:T(8,128)(2,1)}), bf16[64,8,512]{2,1,0:T(8,128)(2,1)S(1)}, u32[]{:S(2)}, u32[]{:S(2)}) async-start(bf16[64,8,512]{2,1,0:T(8,128)(2,1)} %bitcast.14), calls=%async_computation.1 | async-start | bytes 1048576 | tf_op jit(solution)/shard_map/all_to_all | solution.py:244
  222.8 79.9 %all-gather.10.cloned.1.call-start = ((), (), s32[]{:S(2)}) async-start(), calls=%async_computation.4 | async-start | bytes 4718592 | tf_op jit(solution)/shard_map/all_gather | solution.py:333
  255.9 1.7 copy-start.1
  257.6 1.6 copy-start.2
  302.7 2.2 copy-start
Sparse Core Ops, SparseCore 0:
  38.2 97.3 all-gather.11
  183.1 35.9 all-gather.7
  221.2 34.6 all-gather.5
  257.9 44.7 all-gather.9

commit v6 on v5

--- a/solution.py
+++ b/solution.py
@@ -179,49 +179,39 @@
     )(moves, x)
 
 
-def spatial_kernel(groups, order, spatial_ref, w_ref, part_ref, mixed_w_ref):
-    def rows(g, slot):
-        return w_ref[pl.ds(pl.multiple_of(order[g * 3 + slot] * HEAD_DIM, HEAD_DIM), HEAD_DIM), :]
-
-    for g in range(groups):
-        for slot in range(2):
-            mixed_w_ref[(2 * g + slot) * HEAD_DIM : (2 * g + slot + 1) * HEAD_DIM, :] = rows(g, slot)
-    chosen = jnp.concatenate([rows(g, 2) for g in range(groups)], axis=0)
-    part_ref[...] = jnp.dot(spatial_ref[...], chosen, preferred_element_type=F32)
-
-
-def spatial_projection(groups, order, spatial, w):
-    return pl.pallas_call(
-        lambda *refs: spatial_kernel(groups, *refs),
-        out_shape=(
-            jax.ShapeDtypeStruct((spatial.shape[0], w.shape[1]), F32),
-            jax.ShapeDtypeStruct((groups * 2 * HEAD_DIM, w.shape[1]), BF),
-        ),
-        in_specs=[SMEM] + [VMEM] * 2,
-        out_specs=(VMEM, VMEM),
-        compiler_params=pltpu.CompilerParams(vmem_limit_bytes=32 << 20),
-    )(order, spatial, w)
-
-
-def mixed_kernel(part_ref, mixed_ref, w_ref, out_ref):
-    out_ref[...] = (part_ref[...] + jnp.dot(mixed_ref[...], w_ref[...], preferred_element_type=F32)).astype(BF)
-
-
-def mixed_projection(part, mixed, w):
-    rows, cols = part.shape
-    tile = rows // 4
-    return pl.pallas_call(
-        mixed_kernel,
+def order_kernel(order, w_ref, out_ref):
+    for n in range(w_ref.shape[0] // HEAD_DIM):
+        out_ref[n * HEAD_DIM : (n + 1) * HEAD_DIM, :] = w_ref[
+            pl.ds(pl.multiple_of(order[n] * HEAD_DIM, HEAD_DIM), HEAD_DIM), :
+        ]
+
+
+def slot_order(order, w):
+    return pl.pallas_call(
+        order_kernel,
+        out_shape=jax.ShapeDtypeStruct(w.shape, BF),
+        in_specs=[SMEM, VMEM],
+        out_specs=VMEM,
+        compiler_params=pltpu.CompilerParams(vmem_limit_bytes=16 << 20),
+    )(order, w)
+
+
+def projection_kernel(attn_ref, w_ref, out_ref):
+    out_ref[...] = jnp.dot(attn_ref[...], w_ref[...], preferred_element_type=F32).astype(BF)
+
+
+def projection(attn, w):
+    rows, depth = attn.shape
+    cols = w.shape[1]
+    tile = rows // 8
+    return pl.pallas_call(
+        projection_kernel,
         out_shape=jax.ShapeDtypeStruct((rows, cols), BF),
         grid=(rows // tile,),
-        in_specs=[
-            pl.BlockSpec((tile, cols), lambda i: (i, 0)),
-            pl.BlockSpec((tile, mixed.shape[1]), lambda i: (i, 0)),
-            pl.BlockSpec(w.shape, lambda i: (0, 0)),
-        ],
+        in_specs=[pl.BlockSpec((tile, depth), lambda i: (i, 0)), pl.BlockSpec((depth, cols), lambda i: (0, 0))],
         out_specs=pl.BlockSpec((tile, cols), lambda i: (i, 0)),
-        compiler_params=pltpu.CompilerParams(vmem_limit_bytes=32 << 20),
-    )(part, mixed, w)
+        compiler_params=pltpu.CompilerParams(vmem_limit_bytes=56 << 20),
+    )(attn, w)
 
 
 def slots_of(labels):
@@ -306,6 +296,7 @@
     packed, sent = lax.optimization_barrier((jnp.concatenate(packs, axis=2), sent))
     moved = exchange(packed).reshape(BLOCK, -1)
     rows_z = lax.all_gather(sent, "ctx", axis=0, axis_index_groups=along_z)
+    rows_z, own2, query2, bits = lax.optimization_barrier((rows_z, own2, split_blocks(q2), bits))
     quarter, w_z = unpack(moves, rows_z, deep * w_out.shape[0], w_out.shape[1])
     moved, quarter = lax.optimization_barrier((moved, quarter))
     query, own = mix(moves, moved, (q1, k1, v1))
@@ -321,18 +312,15 @@
 
     out = attention(2, bits, query, own, left, right, first)
     own2, _, _ = lax.optimization_barrier((own2, left, right))
-    query2, _ = lax.optimization_barrier((split_blocks(q2), out))
-    out2 = attention(1, bits, query2, own2, *both_ways(own2, parts), first)
+    out, left2, right2 = lax.optimization_barrier((out, *both_ways(own2, parts)))
+    out2 = attention(1, bits, query2, own2, left2, right2, first)
     attn2 = jnp.concatenate([out2[:, lanes(0)], out2[:, lanes(1)]], axis=0)
-    spatial = lax.all_gather(attn2, "head", axis=1, tiled=True)
 
     back = exchange(out.reshape(parts, BLOCK // parts, -1))
     back = back.reshape(parts, BLOCK // parts, 2, 2 * HEAD_DIM).transpose(0, 2, 1, 3).reshape(2 * BLOCK, 2 * HEAD_DIM)
     still = jnp.concatenate([out[:, lanes(1)], out[:, lanes(3)]], axis=0)
-    attn = jnp.concatenate([back[:, lanes(0)], jnp.where(moves[0] > 0, back[:, lanes(1)], still)], axis=1)
-    mixed = lax.all_gather(attn, "head", axis=1, tiled=True)
-    part, mixed_w = spatial_projection(groups, order, spatial, w)
-    return mixed_projection(part, mixed, mixed_w)
+    attn = jnp.concatenate([back[:, lanes(0)], jnp.where(moves[0] > 0, back[:, lanes(1)], still), attn2], axis=1)
+    return projection(lax.all_gather(attn, "head", axis=1, tiled=True), slot_order(order, w))
 
 
 def solution(mesh):

time: 316 us -> 314 us (level)
  waiting for transfers between devices: 180 us -> 160 us
  local copies, waits for them, and re-layouts: 19.8 us -> 29.1 us
  Pallas kernels: 22.2 us -> 30.4 us
    unnamed x48 -> x44, local copies, waits for them, and re-layouts: 13.5 us -> 23.3 us
    all_to_all x2, waiting for transfers between devices: 27.3 us -> 21.7 us  [exchange(): return lax.all_to_all(x, 'ctx', 0, 0, tiled=True)]
    ppermute x2, starting transfers between devices: 6.31 us -> 11.9 us  [both_ways(): left = lax.ppermute(x, 'ctx', [(i, i + 1) for i in range(count - 1)])]
    pallas_call x2, Pallas kernels: 5.46 us -> 9.92 us  [the longest x1 9.16 us: projection(): pl.pallas_call(projection_kernel, out_shape=jax.ShapeDtypeStruct((rows, c...]
    all_gather x2 -> x1, waiting for transfers between devices: 44.7 us -> 40.7 us  [body(): lax.all_gather(attn, 'head', axis=1, tiled=True)]
    ppermute x2, waiting for transfers between devices: 3.93 us -> 0.01 us  [both_ways(): right = lax.ppermute(x, 'ctx', [(i + 1, i) for i in range(count - 1)])]
    pallas_call x2, Pallas kernels: 14 us -> 17.9 us  [attention(): pl.pallas_call(lambda *refs: attention_kernel(heads, *refs), out_shape=ja...]
    all_gather x1, waiting for transfers between devices: 80.7 us -> 77 us  [body(): rows_z = lax.all_gather(sent, 'ctx', axis=0, axis_index_groups=along_z)]
  transfers between devices with their start and end apart: 19 -> 18, of which waited for: 9 -> 6; matrix products, arithmetic and copies ran while one was open for 4% -> 4% of each run, Pallas kernels for 6% -> 6%
where the time goes in v6:
time: 314 us; the launch traced here: 312 us
  waiting for transfers between devices  160 us (51%)
  starting transfers between devices  69.9 us (22%)
  Pallas kernels  30.4 us (10%)
  local copies, waits for them, and re-layouts  29.1 us (9%)
  between operations  17.8 us (6%)
  other arithmetic  5.37 us (2%)
    all_gather x1, waiting for transfers between devices, body(): rows_z = lax.all_gather(sent, 'ctx', axis=0, axis_index_groups=along_z)  77 us
    all_gather x1, waiting for transfers between devices, body(): lax.all_gather(attn, 'head', axis=1, tiled=True)  40.7 us
    all_to_all x2, starting transfers between devices, exchange(): return lax.all_to_all(x, 'ctx', 0, 0, tiled=True)  25.5 us
    unnamed x44, local copies, waits for them, and re-layouts  23.3 us
    all_to_all x2, waiting for transfers between devices, exchange(): return lax.all_to_all(x, 'ctx', 0, 0, tiled=True)  21.7 us
    ppermute x3, waiting for transfers between devices, along_y(): lax.ppermute(x, 'ctx', [(i, i ^ deep * k) for i in range(parts)])  20.4 us
    ppermute x6, starting transfers between devices, scattered(): lax.ppermute(x[k * rows:(k + 1) * rows], 'ctx', [(i, i + k * unit) for i...  20.2 us
    pallas_call x2, Pallas kernels, attention(): pl.pallas_call(lambda *refs: attention_kernel(heads, *refs), out_shape=ja...  17.9 us
  transfers between devices with their start and end apart: 18, of which 6 were waited for; matrix products, arithmetic and copies ran while one was open for 4% of the time, Pallas kernels for 6%

profile of v6, /device:TPU:1, one launch (start us, length us, event | category | flops | bytes accessed | tf_op | source)
XLA Modules:
  0.0 312.4 jit_solution(7909228311619041547)
XLA Ops:
  6.5 0.7 broadcast_compare_fusion.1
  7.4 0.6 fusion.11
  10.0 1.5 constant_dynamic-slice_fusion.8
  11.5 0.7 pad_maximum_fusion.9
  12.3 4.0 %collective-permute-start.2 = (bf16[128,512]{1,0:T(8,128)(2,1)}, bf16[128,512]{1,0:T(8,128)(2,1)S(1)}, u32[]{:S(2)}, u32[]{:S(2)}) collective-permute-start(bf16[128,512]{1,0:T(8,128)(2,1)} %get-tuple-element.63), channel_id=1, source_target_pairs={{0,128},{1,129},{2,130},{3,131},{4,132},{5,133},{6,134},{7,135}} | collective-permute-start | bytes 393224 | tf_op jit(solution)/shard_map/ppermute | solution.py:248
  16.3 2.1 collective-permute-start
  18.4 1.3 collective-permute-start.1
  19.7 0.6 constant_dynamic-update-slice_fusion.10
  20.3 0.6 constant_dynamic-update-slice_fusion.9
  20.9 0.6 constant_dynamic-update-slice_fusion.8
  21.5 1.3 constant_dynamic-update-slice_fusion.7
  23.1 1.3 pad_maximum_fusion
  24.3 1.3 constant_dynamic-update-slice_fusion.6
  25.6 1.2 constant_dynamic-update-slice_fusion.5
  27.0 4.2 %collective-permute-start.5 = (bf16[32,512]{1,0:T(8,128)(2,1)S(1)}, bf16[32,512]{1,0:T(8,128)(2,1)S(1)}, u32[]{:S(2)}, u32[]{:S(2)}) collective-permute-start(bf16[32,512]{1,0:T(8,128)(2,1)S(1)} %get-tuple-element.86), channel_id=1, source_target_pairs={{0,32},{128,160},{256,288},{384,416},{1,33},{129,161},{257,289},{3... | collective-permute-start | bytes 98312 | tf_op jit(solution)/shard_map/ppermute | solution.py:248
  31.2 7.3 %collective-permute-start.4 = (bf16[32,512]{1,0:T(8,128)(2,1)S(1)}, bf16[32,512]{1,0:T(8,128)(2,1)S(1)}, u32[]{:S(2)}, u32[]{:S(2)}) collective-permute-start(bf16[32,512]{1,0:T(8,128)(2,1)S(1)} %get-tuple-element.87), channel_id=1, source_target_pairs={{0,64},{128,192},{256,320},{384,448},{1,65},{129,193},{257,321},{3... | collective-permute-start | bytes 98312 | tf_op jit(solution)/shard_map/ppermute | solution.py:248
  38.5 1.3 collective-permute-start.3
  39.8 1.3 constant_dynamic-update-slice_fusion.4
  41.1 0.6 constant_dynamic-update-slice_fusion.3
  41.7 0.6 constant_dynamic-update-slice_fusion.2
  42.3 0.6 constant_dynamic-update-slice_fusion.1
  42.9 0.6 constant_dynamic-update-slice_fusion
  45.4 0.6 dynamic_slice.51.moves
  46.0 0.7 broadcast_compare_fusion
  46.7 0.2 fusion.6
  47.1 1.1 constant_dynamic-slice_fusion
  48.3 13.8 %all-to-all-start = ((bf16[64,8,1536]{2,1,0:T(8,128)(2,1)}), bf16[64,8,1536]{2,1,0:T(8,128)(2,1)S(1)}, u32[]{:S(2)}, u32[]{:S(2)}) async-start(bf16[64,8,1536]{2,1,0:T(8,128)(2,1)} %pad_maximum_fusion), calls=%async_computation | async-start | bytes 3145728 | tf_op jit(solution)/shard_map/all_to_all | solution.py:234
  62.2 77.0 %all-gather.9.cloned.1.call-done = bf16[4864,128]{1,0:T(8,128)(2,1)} async-done(((bf16[304,128]{1,0:T(8,128)(2,1)}), bf16[4864,128]{1,0:T(8,128)(2,1)}) %all-gather.9.cloned.1.call-update) | async-done | bytes 1245200 | tf_op jit(solution)/shard_map/all_gather | solution.py:298
  139.2 1.3 copy-done.2
  140.5 1.6 shard_map.64
  142.1 3.2 %all-to-all-done = bf16[64,8,1536]{2,1,0:T(8,128)(2,1)S(1)} async-done(((bf16[64,8,1536]{2,1,0:T(8,128)(2,1)}), bf16[64,8,1536]{2,1,0:T(8,128)(2,1)S(1)}, u32[]{:S(2)}, u32[]{:S(2)}) %all-to-all-start) | async-done | bytes 1572896 | tf_op jit(solution)/shard_map/all_to_all | solution.py:234
  145.3 1.0 shard_map.65
  146.3 0.8 copy-done.5
  147.1 1.3 collective-permute-start.7
  148.4 7.9 %collective-permute-start.6 = (bf16[512,1024]{1,0:T(8,128)(2,1)S(1)}, bf16[512,1024]{1,0:T(8,128)(2,1)S(1)}, u32[]{:S(2)}, u32[]{:S(2)}) collective-permute-start(bf16[512,1024]{1,0:T(8,128)(2,1)S(1)} %get-tuple-element.39.refs_2_), channel_id=1, source_target_pairs={{0,8},{8,16},{16,24},{24,32},{32,40},{40,48},{48,56},{56,64},{64,7... | collective-permute-start | bytes 3145736 | tf_op jit(solution)/shard_map/ppermute | solution.py:238
  156.3 1.0 copy-done.3
  157.3 5.2 %collective-permute-start.10 = (bf16[128,768]{1,0:T(8,128)(2,1)S(1)}, bf16[128,768]{1,0:T(8,128)(2,1)S(1)}, u32[]{:S(2)}, u32[]{:S(2)}) collective-permute-start(bf16[128,768]{1,0:T(8,128)(2,1)S(1)} %get-tuple-element.48.refs_5_), channel_id=1, source_target_pairs={{0,384},{8,392},{16,400},{24,408},{32,416},{40,424},{48,432},{56,4... | collective-permute-start | bytes 589832 | tf_op jit(solution)/shard_map/ppermute | solution.py:306
  162.5 2.3 collective-permute-start.9
  164.8 2.1 collective-permute-start.8
  166.9 19.1 %collective-permute-done.9.refs_7_ = bf16[128,768]{1,0:T(8,128)(2,1)S(1)} collective-permute-done((bf16[128,768]{1,0:T(8,128)(2,1)S(1)}, bf16[128,768]{1,0:T(8,128)(2,1)S(1)}, u32[]{:S(2)}, u32[]{:S(2)}) %collective-permute-start.9) | collective-permute-done | bytes 196640 | tf_op jit(solution)/shard_map/ppermute | solution.py:306
  186.0 1.3 collective-permute-done.8.refs_6_
  187.3 0.7 copy-done.11
  188.0 1.3 collective-permute-start.12
  189.3 4.0 %collective-permute-start.11 = (bf16[512,512]{1,0:T(8,128)(2,1)S(1)}, bf16[512,512]{1,0:T(8,128)(2,1)S(1)}, u32[]{:S(2)}, u32[]{:S(2)}) collective-permute-start(bf16[512,512]{1,0:T(8,128)(2,1)S(1)} %pad_maximum_fusion.4.refs_2_), channel_id=1, source_target_pairs={{0,8},{8,16},{16,24},{24,32},{32,40},{40,48},{48,56},{56,64},{64,7... | collective-permute-start | bytes 1572872 | tf_op jit(solution)/shard_map/ppermute | solution.py:238
  193.4 1.2 copy-done.4
  194.6 1.0 copy-done.6
  195.6 0.9 copy-done.12
  196.6 12.0 %shard_map.66 = bf16[512,512]{1,0:T(8,128)(2,1)} custom-call(s32[2,6]{1,0:T(2,128)S(1)} %add_convert_fusion.refs_0_, bf16[512,512]{1,0:T(8,128)(2,1)S(1)} %copy-done.6, bf16[512,1024]{1,0:T(8,128)(2,1)S(1)} %copy-done.4, bf16[512,1024]{1,0:T(8,128)(2,1)S(1)} %collective-permute-done.6.refs_3_, bf16[512,1024]{1,0:T(8,128)(2,1)S(1)} %collective-permute-done.7.refs_4_, ...), custom_call_target="tpu_custom_call" | custom-call | flops 3221225472 | bytes 4194304 | tf_op jit(solution)/shard_map/pallas_call | solution.py:80
  208.6 0.8 copy-done.7
  209.4 0.8 copy-done.9
  210.2 11.7 %all-to-all-start.1 = ((bf16[64,8,512]{2,1,0:T(8,128)(2,1)}), bf16[64,8,512]{2,1,0:T(8,128)(2,1)S(1)}, u32[]{:S(2)}, u32[]{:S(2)}) async-start(bf16[64,8,512]{2,1,0:T(8,128)(2,1)} %bitcast.14), calls=%async_computation.1 | async-start | bytes 1048576 | tf_op jit(solution)/shard_map/all_to_all | solution.py:234
  222.5 1.0 copy-done.8
  223.6 1.0 copy-done.10
  224.6 0.9 copy-done.13
  225.6 5.9 %shard_map.67 = bf16[512,256]{1,0:T(8,128)(2,1)S(1)} custom-call(s32[2,6]{1,0:T(2,128)S(1)} %add_convert_fusion.refs_0_, bf16[512,256]{1,0:T(8,128)(2,1)S(1)} %pad_maximum_fusion.5.refs_1_, bf16[512,512]{1,0:T(8,128)(2,1)S(1)} %pad_maximum_fusion.4.refs_2_, bf16[512,512]{1,0:T(8,128)(2,1)S(1)} %copy-done.10, bf16[512,512]{1,0:T(8,128)(2,1)S(1)} %copy-done.8, ...), custom_call_target="tpu_custom_call" | custom-call | flops 1610612736 | bytes 2097152 | tf_op jit(solution)/shard_map/pallas_call | solution.py:80
  231.4 1.0 fusion.8
  232.5 18.5 %all-to-all-done.1 = bf16[64,8,512]{2,1,0:T(8,128)(2,1)S(1)} async-done(((bf16[64,8,512]{2,1,0:T(8,128)(2,1)}), bf16[64,8,512]{2,1,0:T(8,128)(2,1)S(1)}, u32[]{:S(2)}, u32[]{:S(2)}) %all-to-all-start.1) | async-done | bytes 524320 | tf_op jit(solution)/shard_map/all_to_all | solution.py:234
  250.9 0.1 fusion.7
  251.0 1.0 maximum_maximum_fusion
  252.1 1.7 copy-done.1
  253.8 0.8 shard_map.68.w_ref
  254.6 1.5 copy-done
  256.0 40.7 %all-gather.5.cloned.1.call-done.attn_ref = bf16[1024,3072]{1,0:T(8,128)(2,1)} async-done(((bf16[1024,384]{1,0:T(8,128)(2,1)}), bf16[1024,3072]{1,0:T(8,128)(2,1)}) %all-gather.5.cloned.1.call-update) | async-done | bytes 6291472 | tf_op jit(solution)/shard_map/all_gather | solution.py:323
  296.8 9.2 %shard_map.69 = bf16[1024,384]{1,0:T(8,128)(2,1)} custom-call(bf16[1024,3072]{1,0:T(8,128)(2,1)} %all-gather.5.cloned.1.call-done.attn_ref, bf16[3072,384]{1,0:T(8,128)(2,1)} %copy-done), custom_call_target="tpu_custom_call" | custom-call | tf_op jit(solution)/shard_map/pallas_call | solution.py:207
  (60 shorter events, 1.2 us)
Async XLA Ops:
  6.5 132.7 %all-gather.9.cloned.1.call-start = ((), (), s32[]{:S(2)}) async-start(), calls=%async_computation.4 | async-start | bytes 1323008 | tf_op jit(solution)/shard_map/all_gather | solution.py:298
  10.0 9.8 %copy-start.15 = (bf16[48,384]{1,0:T(8,128)(2,1)S(1)}, bf16[48,384]{1,0:T(8,128)(2,1)}, u32[]{:S(2)}) copy-start(bf16[48,384]{1,0:T(8,128)(2,1)} %param.11) | copy-start | bytes 110596
  10.0 12.8 %copy-start.14 = (bf16[1024,384]{1,0:T(8,128)(2,1)S(1)}, bf16[1024,384]{1,0:T(8,128)(2,1)}, u32[]{:S(2)}) copy-start(bf16[1024,384]{1,0:T(8,128)(2,1)} %param.6) | copy-start | bytes 2359300
  12.3 14.6 %collective-permute-start.2 = (bf16[128,512]{1,0:T(8,128)(2,1)}, bf16[128,512]{1,0:T(8,128)(2,1)S(1)}, u32[]{:S(2)}, u32[]{:S(2)}) collective-permute-start(bf16[128,512]{1,0:T(8,128)(2,1)} %get-tuple-element.63), channel_id=1, source_target_pairs={{0,128},{1,129},{2,130},{3,131},{4,132},{5,133},{6,134},{7,135}} | collective-permute-start | bytes 393224 | tf_op jit(solution)/shard_map/ppermute | solution.py:248
  16.3 10.6 %collective-permute-start = (bf16[128,512]{1,0:T(8,128)(2,1)}, bf16[128,512]{1,0:T(8,128)(2,1)S(1)}, u32[]{:S(2)}, u32[]{:S(2)}) collective-permute-start(bf16[128,512]{1,0:T(8,128)(2,1)} %get-tuple-element.64), channel_id=1, source_target_pairs={{0,384},{1,385},{2,386},{3,387},{4,388},{5,389},{6,390},{7,391}} | collective-permute-start | bytes 393224 | tf_op jit(solution)/shard_map/ppermute | solution.py:248
  18.4 8.5 %collective-permute-start.1 = (bf16[128,512]{1,0:T(8,128)(2,1)}, bf16[128,512]{1,0:T(8,128)(2,1)S(1)}, u32[]{:S(2)}, u32[]{:S(2)}) collective-permute-start(bf16[128,512]{1,0:T(8,128)(2,1)} %get-tuple-element.65), channel_id=1, source_target_pairs={{0,256},{1,257},{2,258},{3,259},{4,260},{5,261},{6,262},{7,263}} | collective-permute-start | bytes 393224 | tf_op jit(solution)/shard_map/ppermute | solution.py:248
  24.3 21.0 %copy-start.16 = (s32[24]{0:T(128)S(1)}, s32[24]{0:T(128)}, u32[]{:S(2)}) copy-start(s32[24]{0:T(128)} %param.10) | copy-start | bytes 292
  27.0 14.1 %collective-permute-start.5 = (bf16[32,512]{1,0:T(8,128)(2,1)S(1)}, bf16[32,512]{1,0:T(8,128)(2,1)S(1)}, u32[]{:S(2)}, u32[]{:S(2)}) collective-permute-start(bf16[32,512]{1,0:T(8,128)(2,1)S(1)} %get-tuple-element.86), channel_id=1, source_target_pairs={{0,32},{128,160},{256,288},{384,416},{1,33},{129,161},{257,289},{3... | collective-permute-start | bytes 98312 | tf_op jit(solution)/shard_map/ppermute | solution.py:248
  31.2 9.9 %collective-permute-start.4 = (bf16[32,512]{1,0:T(8,128)(2,1)S(1)}, bf16[32,512]{1,0:T(8,128)(2,1)S(1)}, u32[]{:S(2)}, u32[]{:S(2)}) collective-permute-start(bf16[32,512]{1,0:T(8,128)(2,1)S(1)} %get-tuple-element.87), channel_id=1, source_target_pairs={{0,64},{128,192},{256,320},{384,448},{1,65},{129,193},{257,321},{3... | collective-permute-start | bytes 98312 | tf_op jit(solution)/shard_map/ppermute | solution.py:248
  38.5 2.6 collective-permute-start.3
  48.3 97.0 %all-to-all-start = ((bf16[64,8,1536]{2,1,0:T(8,128)(2,1)}), bf16[64,8,1536]{2,1,0:T(8,128)(2,1)S(1)}, u32[]{:S(2)}, u32[]{:S(2)}) async-start(bf16[64,8,1536]{2,1,0:T(8,128)(2,1)} %pad_maximum_fusion), calls=%async_computation | async-start | bytes 3145728 | tf_op jit(solution)/shard_map/all_to_all | solution.py:234
  62.1 190.0 %all-gather.7.cloned.1.call-start = ((), (), s32[]{:S(2)}) async-start(), calls=%async_computation.3 | async-start | bytes 2949120 | tf_op jit(solution)/shard_map/all_gather | solution.py:311
  139.2 1.3 copy-start.2
  146.3 0.8 copy-start.5
  147.1 40.9 %collective-permute-start.7 = (bf16[512,1024]{1,0:T(8,128)(2,1)S(1)}, bf16[512,1024]{1,0:T(8,128)(2,1)S(1)}, u32[]{:S(2)}, u32[]{:S(2)}) collective-permute-start(bf16[512,1024]{1,0:T(8,128)(2,1)S(1)} %get-tuple-element.39.refs_2_), channel_id=1, source_target_pairs={{8,0},{16,8},{24,16},{32,24},{40,32},{48,40},{56,48},{64,56},{72,6... | collective-permute-start | bytes 3145736 | tf_op jit(solution)/shard_map/ppermute | solution.py:239
  148.4 39.7 %collective-permute-start.6 = (bf16[512,1024]{1,0:T(8,128)(2,1)S(1)}, bf16[512,1024]{1,0:T(8,128)(2,1)S(1)}, u32[]{:S(2)}, u32[]{:S(2)}) collective-permute-start(bf16[512,1024]{1,0:T(8,128)(2,1)S(1)} %get-tuple-element.39.refs_2_), channel_id=1, source_target_pairs={{0,8},{8,16},{16,24},{24,32},{32,40},{40,48},{48,56},{56,64},{64,7... | collective-permute-start | bytes 3145736 | tf_op jit(solution)/shard_map/ppermute | solution.py:238
  156.2 1.0 copy-start.3
  157.3 9.7 %collective-permute-start.10 = (bf16[128,768]{1,0:T(8,128)(2,1)S(1)}, bf16[128,768]{1,0:T(8,128)(2,1)S(1)}, u32[]{:S(2)}, u32[]{:S(2)}) collective-permute-start(bf16[128,768]{1,0:T(8,128)(2,1)S(1)} %get-tuple-element.48.refs_5_), channel_id=1, source_target_pairs={{0,384},{8,392},{16,400},{24,408},{32,416},{40,424},{48,432},{56,4... | collective-permute-start | bytes 589832 | tf_op jit(solution)/shard_map/ppermute | solution.py:306
  162.5 23.6 %collective-permute-start.9 = (bf16[128,768]{1,0:T(8,128)(2,1)S(1)}, bf16[128,768]{1,0:T(8,128)(2,1)S(1)}, u32[]{:S(2)}, u32[]{:S(2)}) collective-permute-start(bf16[128,768]{1,0:T(8,128)(2,1)S(1)} %get-tuple-element.48.refs_5_), channel_id=1, source_target_pairs={{0,256},{8,264},{16,272},{24,280},{32,288},{40,296},{48,304},{56,3... | collective-permute-start | bytes 589832 | tf_op jit(solution)/shard_map/ppermute | solution.py:306
  164.8 22.5 %collective-permute-start.8 = (bf16[128,768]{1,0:T(8,128)(2,1)S(1)}, bf16[128,768]{1,0:T(8,128)(2,1)S(1)}, u32[]{:S(2)}, u32[]{:S(2)}) collective-permute-start(bf16[128,768]{1,0:T(8,128)(2,1)S(1)} %get-tuple-element.48.refs_5_), channel_id=1, source_target_pairs={{0,128},{8,136},{16,144},{24,152},{32,160},{40,168},{48,176},{56,1... | collective-permute-start | bytes 589832 | tf_op jit(solution)/shard_map/ppermute | solution.py:306
  187.3 0.7 copy-start.11
  188.0 20.5 %collective-permute-start.12 = (bf16[512,512]{1,0:T(8,128)(2,1)S(1)}, bf16[512,512]{1,0:T(8,128)(2,1)S(1)}, u32[]{:S(2)}, u32[]{:S(2)}) collective-permute-start(bf16[512,512]{1,0:T(8,128)(2,1)S(1)} %pad_maximum_fusion.4.refs_2_), channel_id=1, source_target_pairs={{8,0},{16,8},{24,16},{32,24},{40,32},{48,40},{56,48},{64,56},{72,6... | collective-permute-start | bytes 1572872 | tf_op jit(solution)/shard_map/ppermute | solution.py:239
  189.3 20.0 %collective-permute-start.11 = (bf16[512,512]{1,0:T(8,128)(2,1)S(1)}, bf16[512,512]{1,0:T(8,128)(2,1)S(1)}, u32[]{:S(2)}, u32[]{:S(2)}) collective-permute-start(bf16[512,512]{1,0:T(8,128)(2,1)S(1)} %pad_maximum_fusion.4.refs_2_), channel_id=1, source_target_pairs={{0,8},{8,16},{16,24},{24,32},{32,40},{40,48},{48,56},{56,64},{64,7... | collective-permute-start | bytes 1572872 | tf_op jit(solution)/shard_map/ppermute | solution.py:238
  193.4 1.2 copy-start.4
  194.6 1.0 copy-start.6
  195.6 0.9 copy-start.12
  208.6 0.8 copy-start.7
  209.4 0.8 copy-start.9
  210.2 40.8 %all-to-all-start.1 = ((bf16[64,8,512]{2,1,0:T(8,128)(2,1)}), bf16[64,8,512]{2,1,0:T(8,128)(2,1)S(1)}, u32[]{:S(2)}, u32[]{:S(2)}) async-start(bf16[64,8,512]{2,1,0:T(8,128)(2,1)} %bitcast.14), calls=%async_computation.1 | async-start | bytes 1048576 | tf_op jit(solution)/shard_map/all_to_all | solution.py:234
  221.9 74.9 %all-gather.5.cloned.1.call-start = ((), (), s32[]{:S(2)}) async-start(), calls=%async_computation.2 | async-start | bytes 7077888 | tf_op jit(solution)/shard_map/all_gather | solution.py:323
  222.5 1.0 copy-start.8
  223.6 1.0 copy-start.10
  224.6 0.9 copy-start.13
  252.1 1.7 copy-start.1
  254.6 1.5 copy-start
Sparse Core Ops, SparseCore 0:
  43.6 95.5 all-gather.8
  188.2 39.1 all-gather.6
  252.2 44.5 all-gather.4

commit v7 on v6

--- a/solution.py
+++ b/solution.py
@@ -196,20 +196,38 @@
     )(order, w)
 
 
-def projection_kernel(attn_ref, w_ref, out_ref):
-    out_ref[...] = jnp.dot(attn_ref[...], w_ref[...], preferred_element_type=F32).astype(BF)
+def projection_kernel(attn_ref, w_ref, out_ref, total_ref):
+    part = jnp.dot(attn_ref[...], w_ref[...], preferred_element_type=F32)
+    step = pl.program_id(0)
+    last = pl.num_programs(0) - 1
+
+    @pl.when(step == 0)
+    def _():
+        total_ref[...] = part
+
+    @pl.when((step > 0) & (step < last))
+    def _():
+        total_ref[...] += part
+
+    @pl.when(step == last)
+    def _():
+        out_ref[...] = (total_ref[...] + part).astype(BF)
 
 
 def projection(attn, w):
     rows, depth = attn.shape
     cols = w.shape[1]
-    tile = rows // 8
+    steps = 4
     return pl.pallas_call(
         projection_kernel,
         out_shape=jax.ShapeDtypeStruct((rows, cols), BF),
-        grid=(rows // tile,),
-        in_specs=[pl.BlockSpec((tile, depth), lambda i: (i, 0)), pl.BlockSpec((depth, cols), lambda i: (0, 0))],
-        out_specs=pl.BlockSpec((tile, cols), lambda i: (i, 0)),
+        grid=(steps,),
+        in_specs=[
+            pl.BlockSpec((rows, depth // steps), lambda i: (0, i)),
+            pl.BlockSpec((depth // steps, cols), lambda i: (i, 0)),
+        ],
+        out_specs=pl.BlockSpec((rows, cols), lambda i: (0, 0)),
+        scratch_shapes=[pltpu.VMEM((rows, cols), F32)],
         compiler_params=pltpu.CompilerParams(vmem_limit_bytes=56 << 20),
     )(attn, w)
 
@@ -292,13 +310,14 @@
         + [shares[:, lanes(c)] for c in range(4)],
         axis=0,
     )
-    own2 = jnp.concatenate([split_blocks(k2), split_blocks(v2)], axis=1)
     packed, sent = lax.optimization_barrier((jnp.concatenate(packs, axis=2), sent))
     moved = exchange(packed).reshape(BLOCK, -1)
     rows_z = lax.all_gather(sent, "ctx", axis=0, axis_index_groups=along_z)
-    rows_z, own2, query2, bits = lax.optimization_barrier((rows_z, own2, split_blocks(q2), bits))
     quarter, w_z = unpack(moves, rows_z, deep * w_out.shape[0], w_out.shape[1])
-    moved, quarter = lax.optimization_barrier((moved, quarter))
+    q2, k2, v2, quarter = lax.optimization_barrier((q2, k2, v2, quarter))
+    own2 = jnp.concatenate([split_blocks(k2), split_blocks(v2)], axis=1)
+    query2 = split_blocks(q2)
+    moved, quarter, own2 = lax.optimization_barrier((moved, quarter, own2))
     query, own = mix(moves, moved, (q1, k1, v1))
     left, right = both_ways(own, parts)
 

time: 314 us -> 309 us (0.984)
  local copies, waits for them, and re-layouts: 29.1 us -> 21.1 us
  waiting for transfers between devices: 160 us -> 166 us
    unnamed x44 -> x30, local copies, waits for them, and re-layouts: 23.3 us -> 14.7 us
    all_gather x1, waiting for transfers between devices: 77 us -> 81.1 us  [body(): rows_z = lax.all_gather(sent, 'ctx', axis=0, axis_index_groups=along_z)]
    ppermute x3, waiting for transfers between devices: 20.4 us -> 24.1 us  [along_y(): lax.ppermute(x, 'ctx', [(i, i ^ deep * k) for i in range(parts)])]
  transfers between devices with their start and end apart: 18 -> 18, of which waited for: 6 -> 5; matrix products, arithmetic and copies ran while one was open for 4% -> 5% of each run, Pallas kernels for 6% -> 6%
where the time goes in v7:
time: 309 us; the launch traced here: 308 us
  waiting for transfers between devices  166 us (54%)
  starting transfers between devices  68.6 us (22%)
  Pallas kernels  29.3 us (9%)
  local copies, waits for them, and re-layouts  21.1 us (7%)
  between operations  17.8 us (6%)
  other arithmetic  5.32 us (2%)
    all_gather x1, waiting for transfers between devices, body(): rows_z = lax.all_gather(sent, 'ctx', axis=0, axis_index_groups=along_z)  81.1 us
    all_gather x1, waiting for transfers between devices, body(): lax.all_gather(attn, 'head', axis=1, tiled=True)  40.4 us
    all_to_all x2, starting transfers between devices, exchange(): return lax.all_to_all(x, 'ctx', 0, 0, tiled=True)  27 us
    ppermute x3, waiting for transfers between devices, along_y(): lax.ppermute(x, 'ctx', [(i, i ^ deep * k) for i in range(parts)])  24.1 us
    all_to_all x2, waiting for transfers between devices, exchange(): return lax.all_to_all(x, 'ctx', 0, 0, tiled=True)  20.5 us
    ppermute x6, starting transfers between devices, scattered(): lax.ppermute(x[k * rows:(k + 1) * rows], 'ctx', [(i, i + k * unit) for i...  20.2 us
    pallas_call x2, Pallas kernels, attention(): pl.pallas_call(lambda *refs: attention_kernel(heads, *refs), out_shape=ja...  17.4 us
    unnamed x30, local copies, waits for them, and re-layouts  14.7 us
  transfers between devices with their start and end apart: 18, of which 5 were waited for; matrix products, arithmetic and copies ran while one was open for 5% of the time, Pallas kernels for 6%

profile of v7, /device:TPU:1, one launch (start us, length us, event | category | flops | bytes accessed | tf_op | source)
XLA Modules:
  0.0 308.2 jit_solution(6253479188005176236)
XLA Ops:
  6.5 0.7 broadcast_compare_fusion.1
  7.2 0.1 eq.57
  7.3 0.1 select_select_fusion.1
  7.4 0.1 broadcast_add_fusion
  7.4 0.6 fusion.14
  10.0 1.5 constant_dynamic-slice_fusion.8
  11.6 0.7 pad_maximum_fusion.9
  12.3 4.0 %collective-permute-start.2 = (bf16[128,512]{1,0:T(8,128)(2,1)}, bf16[128,512]{1,0:T(8,128)(2,1)S(1)}, u32[]{:S(2)}, u32[]{:S(2)}) collective-permute-start(bf16[128,512]{1,0:T(8,128)(2,1)} %get-tuple-element.65), channel_id=1, source_target_pairs={{0,128},{1,129},{2,130},{3,131},{4,132},{5,133},{6,134},{7,135}} | collective-permute-start | bytes 393224 | tf_op jit(solution)/shard_map/ppermute | solution.py:266
  16.3 2.3 collective-permute-start.1
  18.6 1.3 collective-permute-start
  19.9 0.6 constant_dynamic-update-slice_fusion.10
  20.5 0.6 constant_dynamic-update-slice_fusion.9
  21.1 0.6 constant_dynamic-update-slice_fusion.8
  21.7 1.2 constant_dynamic-update-slice_fusion.7
  22.9 0.8 constant_dynamic-slice_fusion.12
  23.8 0.1 pad_maximum_fusion.2
  24.0 1.3 pad_maximum_fusion
  25.2 1.3 constant_dynamic-update-slice_fusion.6
  26.5 1.3 constant_dynamic-update-slice_fusion.5
  27.8 0.1 fusion.2
  27.9 4.0 %collective-permute-start.5 = (bf16[32,512]{1,0:T(8,128)(2,1)S(1)}, bf16[32,512]{1,0:T(8,128)(2,1)S(1)}, u32[]{:S(2)}, u32[]{:S(2)}) collective-permute-start(bf16[32,512]{1,0:T(8,128)(2,1)S(1)} %get-tuple-element.89), channel_id=1, source_target_pairs={{0,32},{128,160},{256,288},{384,416},{1,33},{129,161},{257,289},{3... | collective-permute-start | bytes 98312 | tf_op jit(solution)/shard_map/ppermute | solution.py:266
  31.9 7.3 %collective-permute-start.4 = (bf16[32,512]{1,0:T(8,128)(2,1)S(1)}, bf16[32,512]{1,0:T(8,128)(2,1)S(1)}, u32[]{:S(2)}, u32[]{:S(2)}) collective-permute-start(bf16[32,512]{1,0:T(8,128)(2,1)S(1)} %get-tuple-element.90), channel_id=1, source_target_pairs={{0,64},{128,192},{256,320},{384,448},{1,65},{129,193},{257,321},{3... | collective-permute-start | bytes 98312 | tf_op jit(solution)/shard_map/ppermute | solution.py:266
  39.2 1.3 collective-permute-start.3
  40.5 1.3 constant_dynamic-update-slice_fusion.4
  41.8 0.6 constant_dynamic-update-slice_fusion.3
  42.4 0.6 constant_dynamic-update-slice_fusion.2
  43.0 0.6 constant_dynamic-update-slice_fusion.1
  43.6 0.6 constant_dynamic-update-slice_fusion
  46.1 0.6 dynamic_slice.42.moves
  46.7 13.8 %all-to-all-start = ((bf16[64,8,1536]{2,1,0:T(8,128)(2,1)}), bf16[64,8,1536]{2,1,0:T(8,128)(2,1)S(1)}, u32[]{:S(2)}, u32[]{:S(2)}) async-start(bf16[64,8,1536]{2,1,0:T(8,128)(2,1)} %pad_maximum_fusion), calls=%async_computation | async-start | bytes 3145728 | tf_op jit(solution)/shard_map/all_to_all | solution.py:252
  60.6 81.1 %all-gather.9.cloned.1.call-done = bf16[4864,128]{1,0:T(8,128)(2,1)} async-done(((bf16[304,128]{1,0:T(8,128)(2,1)}), bf16[4864,128]{1,0:T(8,128)(2,1)}) %all-gather.9.cloned.1.call-update) | async-done | bytes 1245200 | tf_op jit(solution)/shard_map/all_gather | solution.py:315
  141.6 1.3 copy-done.2
  142.9 1.6 shard_map.64
  144.6 0.1 pad_maximum_fusion.4.refs_2_
  144.7 2.0 shard_map.65
  146.7 1.3 collective-permute-start.7
  148.0 5.7 %collective-permute-start.6 = (bf16[512,1024]{1,0:T(8,128)(2,1)}, bf16[512,1024]{1,0:T(8,128)(2,1)S(1)}, u32[]{:S(2)}, u32[]{:S(2)}) collective-permute-start(bf16[512,1024]{1,0:T(8,128)(2,1)} %get-tuple-element.41.refs_2_), channel_id=1, source_target_pairs={{0,8},{8,16},{16,24},{24,32},{32,40},{40,48},{48,56},{56,64},{64,7... | collective-permute-start | bytes 3145736 | tf_op jit(solution)/shard_map/ppermute | solution.py:256
  153.7 4.2 %collective-permute-start.10 = (bf16[128,768]{1,0:T(8,128)(2,1)}, bf16[128,768]{1,0:T(8,128)(2,1)S(1)}, u32[]{:S(2)}, u32[]{:S(2)}) collective-permute-start(bf16[128,768]{1,0:T(8,128)(2,1)} %get-tuple-element.50.refs_5_), channel_id=1, source_target_pairs={{0,384},{8,392},{16,400},{24,408},{32,416},{40,424},{48,432},{56,4... | collective-permute-start | bytes 589832 | tf_op jit(solution)/shard_map/ppermute | solution.py:325
  158.0 2.3 collective-permute-start.9
  160.3 2.4 collective-permute-start.8
  162.8 22.3 %collective-permute-done.9.refs_7_ = bf16[128,768]{1,0:T(8,128)(2,1)} collective-permute-done((bf16[128,768]{1,0:T(8,128)(2,1)}, bf16[128,768]{1,0:T(8,128)(2,1)}, u32[]{:S(2)}, u32[]{:S(2)}) %collective-permute-start.9) | collective-permute-done | bytes 196640 | tf_op jit(solution)/shard_map/ppermute | solution.py:325
  185.0 1.8 collective-permute-done.8.refs_6_
  186.9 0.7 broadcast_compare_fusion
  187.6 0.1 broadcast_add_fusion.1
  187.7 1.3 collective-permute-start.12
  189.0 4.0 %collective-permute-start.11 = (bf16[512,512]{1,0:T(8,128)(2,1)S(1)}, bf16[512,512]{1,0:T(8,128)(2,1)S(1)}, u32[]{:S(2)}, u32[]{:S(2)}) collective-permute-start(bf16[512,512]{1,0:T(8,128)(2,1)S(1)} %pad_maximum_fusion.4.refs_2_), channel_id=1, source_target_pairs={{0,8},{8,16},{16,24},{24,32},{32,40},{40,48},{48,56},{56,64},{64,7... | collective-permute-start | bytes 1572872 | tf_op jit(solution)/shard_map/ppermute | solution.py:256
  193.0 0.2 fusion.6
  193.2 0.1 add_convert_fusion.refs_0_
  193.3 11.6 %shard_map.66 = bf16[512,512]{1,0:T(8,128)(2,1)} custom-call(s32[2,6]{1,0:T(2,128)S(1)} %add_convert_fusion.refs_0_, bf16[512,512]{1,0:T(8,128)(2,1)S(1)} %get-tuple-element.40.refs_1_, bf16[512,1024]{1,0:T(8,128)(2,1)} %get-tuple-element.41.refs_2_, bf16[512,1024]{1,0:T(8,128)(2,1)S(1)} %collective-permute-done.6.refs_3_, ...), custom_call_target="tpu_custom_call" | custom-call | flops 3221225472 | bytes 4194304 | tf_op jit(solution)/shard_map/pallas_call | solution.py:80
  204.9 0.8 copy-done.3
  205.7 0.8 copy-done.5
  206.5 13.2 %all-to-all-start.1 = ((bf16[64,8,512]{2,1,0:T(8,128)(2,1)}), bf16[64,8,512]{2,1,0:T(8,128)(2,1)S(1)}, u32[]{:S(2)}, u32[]{:S(2)}) async-start(bf16[64,8,512]{2,1,0:T(8,128)(2,1)} %bitcast.14), calls=%async_computation.1 | async-start | bytes 1048576 | tf_op jit(solution)/shard_map/all_to_all | solution.py:252
  220.4 1.0 fusion.12
  221.4 5.8 %shard_map.67 = bf16[512,256]{1,0:T(8,128)(2,1)S(1)} custom-call(s32[2,6]{1,0:T(2,128)S(1)} %add_convert_fusion.refs_0_, bf16[512,256]{1,0:T(8,128)(2,1)S(1)} %pad_maximum_fusion.5.refs_1_, bf16[512,512]{1,0:T(8,128)(2,1)S(1)} %pad_maximum_fusion.4.refs_2_, bf16[512,512]{1,0:T(8,128)(2,1)S(1)} %copy-done.6, bf16[512,512]{1,0:T(8,128)(2,1)S(1)} %copy-done.4, ...), custom_call_target="tpu_custom_call" | custom-call | flops 1610612736 | bytes 2097152 | tf_op jit(solution)/shard_map/pallas_call | solution.py:80
  227.2 1.0 fusion.8
  228.3 20.5 %all-to-all-done.1 = bf16[64,8,512]{2,1,0:T(8,128)(2,1)S(1)} async-done(((bf16[64,8,512]{2,1,0:T(8,128)(2,1)}), bf16[64,8,512]{2,1,0:T(8,128)(2,1)S(1)}, u32[]{:S(2)}, u32[]{:S(2)}) %all-to-all-start.1) | async-done | bytes 524320 | tf_op jit(solution)/shard_map/all_to_all | solution.py:252
  248.8 0.1 fusion.7
  248.9 1.0 maximum_maximum_fusion
  249.9 0.1 add.108.order
  250.0 1.7 copy-done.1
  251.6 0.8 shard_map.68.w_ref
  252.4 1.4 copy-done
  253.9 40.4 %all-gather.5.cloned.1.call-done.attn_ref = bf16[1024,3072]{1,0:T(8,128)(2,1)} async-done(((bf16[1024,384]{1,0:T(8,128)(2,1)}), bf16[1024,3072]{1,0:T(8,128)(2,1)}) %all-gather.5.cloned.1.call-update) | async-done | bytes 6291472 | tf_op jit(solution)/shard_map/all_gather | solution.py:342
  294.2 7.5 %shard_map.69 = bf16[1024,384]{1,0:T(8,128)(2,1)} custom-call(bf16[1024,3072]{1,0:T(8,128)(2,1)} %all-gather.5.cloned.1.call-done.attn_ref, bf16[3072,384]{1,0:T(8,128)(2,1)} %copy-done), custom_call_target="tpu_custom_call" | custom-call | tf_op jit(solution)/shard_map/pallas_call | solution.py:221
  (47 shorter events, 0.5 us)
Async XLA Ops:
  6.5 135.1 %all-gather.9.cloned.1.call-start = ((), (), s32[]{:S(2)}) async-start(), calls=%async_computation.4 | async-start | bytes 1323008 | tf_op jit(solution)/shard_map/all_gather | solution.py:315
  10.0 9.9 %copy-start.8 = (bf16[48,384]{1,0:T(8,128)(2,1)S(1)}, bf16[48,384]{1,0:T(8,128)(2,1)}, u32[]{:S(2)}) copy-start(bf16[48,384]{1,0:T(8,128)(2,1)} %param.11) | copy-start | bytes 110596
  10.0 12.9 %copy-start.7 = (bf16[1024,384]{1,0:T(8,128)(2,1)S(1)}, bf16[1024,384]{1,0:T(8,128)(2,1)}, u32[]{:S(2)}) copy-start(bf16[1024,384]{1,0:T(8,128)(2,1)} %param.6) | copy-start | bytes 2359300
  12.3 15.5 %collective-permute-start.2 = (bf16[128,512]{1,0:T(8,128)(2,1)}, bf16[128,512]{1,0:T(8,128)(2,1)S(1)}, u32[]{:S(2)}, u32[]{:S(2)}) collective-permute-start(bf16[128,512]{1,0:T(8,128)(2,1)} %get-tuple-element.65), channel_id=1, source_target_pairs={{0,128},{1,129},{2,130},{3,131},{4,132},{5,133},{6,134},{7,135}} | collective-permute-start | bytes 393224 | tf_op jit(solution)/shard_map/ppermute | solution.py:266
  16.3 11.5 %collective-permute-start.1 = (bf16[128,512]{1,0:T(8,128)(2,1)S(1)}, bf16[128,512]{1,0:T(8,128)(2,1)S(1)}, u32[]{:S(2)}, u32[]{:S(2)}) collective-permute-start(bf16[128,512]{1,0:T(8,128)(2,1)S(1)} %get-tuple-element.66), channel_id=1, source_target_pairs={{0,256},{1,257},{2,258},{3,259},{4,260},{5,261},{6,262},{7,263}} | collective-permute-start | bytes 393224 | tf_op jit(solution)/shard_map/ppermute | solution.py:266
  18.6 9.2 %collective-permute-start = (bf16[128,512]{1,0:T(8,128)(2,1)S(1)}, bf16[128,512]{1,0:T(8,128)(2,1)S(1)}, u32[]{:S(2)}, u32[]{:S(2)}) collective-permute-start(bf16[128,512]{1,0:T(8,128)(2,1)S(1)} %get-tuple-element.67), channel_id=1, source_target_pairs={{0,384},{1,385},{2,386},{3,387},{4,388},{5,389},{6,390},{7,391}} | collective-permute-start | bytes 393224 | tf_op jit(solution)/shard_map/ppermute | solution.py:266
  25.2 20.8 %copy-start.9 = (s32[24]{0:T(128)S(1)}, s32[24]{0:T(128)}, u32[]{:S(2)}) copy-start(s32[24]{0:T(128)} %param.10) | copy-start | bytes 292
  27.9 13.9 %collective-permute-start.5 = (bf16[32,512]{1,0:T(8,128)(2,1)S(1)}, bf16[32,512]{1,0:T(8,128)(2,1)S(1)}, u32[]{:S(2)}, u32[]{:S(2)}) collective-permute-start(bf16[32,512]{1,0:T(8,128)(2,1)S(1)} %get-tuple-element.89), channel_id=1, source_target_pairs={{0,32},{128,160},{256,288},{384,416},{1,33},{129,161},{257,289},{3... | collective-permute-start | bytes 98312 | tf_op jit(solution)/shard_map/ppermute | solution.py:266
  31.9 9.9 %collective-permute-start.4 = (bf16[32,512]{1,0:T(8,128)(2,1)S(1)}, bf16[32,512]{1,0:T(8,128)(2,1)S(1)}, u32[]{:S(2)}, u32[]{:S(2)}) collective-permute-start(bf16[32,512]{1,0:T(8,128)(2,1)S(1)} %get-tuple-element.90), channel_id=1, source_target_pairs={{0,64},{128,192},{256,320},{384,448},{1,65},{129,193},{257,321},{3... | collective-permute-start | bytes 98312 | tf_op jit(solution)/shard_map/ppermute | solution.py:266
  39.2 2.6 collective-permute-start.3
  46.7 98.0 %all-to-all-start = ((bf16[64,8,1536]{2,1,0:T(8,128)(2,1)}), bf16[64,8,1536]{2,1,0:T(8,128)(2,1)S(1)}, u32[]{:S(2)}, u32[]{:S(2)}) async-start(bf16[64,8,1536]{2,1,0:T(8,128)(2,1)} %pad_maximum_fusion), calls=%async_computation | async-start | bytes 3145728 | tf_op jit(solution)/shard_map/all_to_all | solution.py:252
  60.5 189.5 %all-gather.7.cloned.1.call-start = ((), (), s32[]{:S(2)}) async-start(), calls=%async_computation.3 | async-start | bytes 2949120 | tf_op jit(solution)/shard_map/all_gather | solution.py:330
  141.6 1.3 copy-start.2
  146.7 40.1 %collective-permute-start.7 = (bf16[512,1024]{1,0:T(8,128)(2,1)}, bf16[512,1024]{1,0:T(8,128)(2,1)S(1)}, u32[]{:S(2)}, u32[]{:S(2)}) collective-permute-start(bf16[512,1024]{1,0:T(8,128)(2,1)} %get-tuple-element.41.refs_2_), channel_id=1, source_target_pairs={{8,0},{16,8},{24,16},{32,24},{40,32},{48,40},{56,48},{64,56},{72,6... | collective-permute-start | bytes 3145736 | tf_op jit(solution)/shard_map/ppermute | solution.py:257
  148.0 38.9 %collective-permute-start.6 = (bf16[512,1024]{1,0:T(8,128)(2,1)}, bf16[512,1024]{1,0:T(8,128)(2,1)S(1)}, u32[]{:S(2)}, u32[]{:S(2)}) collective-permute-start(bf16[512,1024]{1,0:T(8,128)(2,1)} %get-tuple-element.41.refs_2_), channel_id=1, source_target_pairs={{0,8},{8,16},{16,24},{24,32},{32,40},{40,48},{48,56},{56,64},{64,7... | collective-permute-start | bytes 3145736 | tf_op jit(solution)/shard_map/ppermute | solution.py:256
  153.7 9.0 %collective-permute-start.10 = (bf16[128,768]{1,0:T(8,128)(2,1)}, bf16[128,768]{1,0:T(8,128)(2,1)S(1)}, u32[]{:S(2)}, u32[]{:S(2)}) collective-permute-start(bf16[128,768]{1,0:T(8,128)(2,1)} %get-tuple-element.50.refs_5_), channel_id=1, source_target_pairs={{0,384},{8,392},{16,400},{24,408},{32,416},{40,424},{48,432},{56,4... | collective-permute-start | bytes 589832 | tf_op jit(solution)/shard_map/ppermute | solution.py:325
  158.0 27.1 %collective-permute-start.9 = (bf16[128,768]{1,0:T(8,128)(2,1)}, bf16[128,768]{1,0:T(8,128)(2,1)}, u32[]{:S(2)}, u32[]{:S(2)}) collective-permute-start(bf16[128,768]{1,0:T(8,128)(2,1)} %get-tuple-element.50.refs_5_), channel_id=1, source_target_pairs={{0,256},{8,264},{16,272},{24,280},{32,288},{40,296},{48,304},{56,3... | collective-permute-start | bytes 589832 | tf_op jit(solution)/shard_map/ppermute | solution.py:325
  160.3 26.6 %collective-permute-start.8 = (bf16[128,768]{1,0:T(8,128)(2,1)}, bf16[128,768]{1,0:T(8,128)(2,1)}, u32[]{:S(2)}, u32[]{:S(2)}) collective-permute-start(bf16[128,768]{1,0:T(8,128)(2,1)} %get-tuple-element.50.refs_5_), channel_id=1, source_target_pairs={{0,128},{8,136},{16,144},{24,152},{32,160},{40,168},{48,176},{56,1... | collective-permute-start | bytes 589832 | tf_op jit(solution)/shard_map/ppermute | solution.py:325
  187.7 17.2 %collective-permute-start.12 = (bf16[512,512]{1,0:T(8,128)(2,1)S(1)}, bf16[512,512]{1,0:T(8,128)(2,1)S(1)}, u32[]{:S(2)}, u32[]{:S(2)}) collective-permute-start(bf16[512,512]{1,0:T(8,128)(2,1)S(1)} %pad_maximum_fusion.4.refs_2_), channel_id=1, source_target_pairs={{8,0},{16,8},{24,16},{32,24},{40,32},{48,40},{56,48},{64,56},{72,6... | collective-permute-start | bytes 1572872 | tf_op jit(solution)/shard_map/ppermute | solution.py:257
  189.0 16.7 %collective-permute-start.11 = (bf16[512,512]{1,0:T(8,128)(2,1)S(1)}, bf16[512,512]{1,0:T(8,128)(2,1)S(1)}, u32[]{:S(2)}, u32[]{:S(2)}) collective-permute-start(bf16[512,512]{1,0:T(8,128)(2,1)S(1)} %pad_maximum_fusion.4.refs_2_), channel_id=1, source_target_pairs={{0,8},{8,16},{16,24},{24,32},{32,40},{40,48},{48,56},{56,64},{64,7... | collective-permute-start | bytes 1572872 | tf_op jit(solution)/shard_map/ppermute | solution.py:256
  204.9 0.8 copy-start.3
  205.7 0.8 copy-start.5
  206.5 14.9 %copy-start.4 = (bf16[512,512]{1,0:T(8,128)(2,1)S(1)}, bf16[512,512]{1,0:T(8,128)(2,1)}, u32[]{:S(2)}) copy-start(bf16[512,512]{1,0:T(8,128)(2,1)} %copy-done.3) | copy-start | bytes 1572868
  206.5 14.9 %copy-start.6 = (bf16[512,512]{1,0:T(8,128)(2,1)S(1)}, bf16[512,512]{1,0:T(8,128)(2,1)}, u32[]{:S(2)}) copy-start(bf16[512,512]{1,0:T(8,128)(2,1)} %copy-done.5) | copy-start | bytes 1572868
  206.5 42.3 %all-to-all-start.1 = ((bf16[64,8,512]{2,1,0:T(8,128)(2,1)}), bf16[64,8,512]{2,1,0:T(8,128)(2,1)S(1)}, u32[]{:S(2)}, u32[]{:S(2)}) async-start(bf16[64,8,512]{2,1,0:T(8,128)(2,1)} %bitcast.14), calls=%async_computation.1 | async-start | bytes 1048576 | tf_op jit(solution)/shard_map/all_to_all | solution.py:252
  219.7 74.6 %all-gather.5.cloned.1.call-start = ((), (), s32[]{:S(2)}) async-start(), calls=%async_computation.2 | async-start | bytes 7077888 | tf_op jit(solution)/shard_map/all_gather | solution.py:342
  250.0 1.7 copy-start.1
  252.4 1.5 copy-start
Sparse Core Ops, SparseCore 0:
  44.4 97.2 all-gather.8
  187.0 40.1 all-gather.6
  250.0 44.1 all-gather.4

commit v8 on v7

--- a/solution.py
+++ b/solution.py
@@ -133,6 +133,39 @@
         out_specs=(VMEM, VMEM),
         compiler_params=pltpu.CompilerParams(vmem_limit_bytes=16 << 20),
     )(moves, moved, *kept)
+
+
+def payload_kernel(w_ref, k0, k1, v0, v1, shares_ref, out_ref):
+    rows = w_ref.shape[0]
+    share = shares_ref.shape[0]
+    at = 0
+    for c in range(w_ref.shape[1] // HEAD_DIM):
+        out_ref[at : at + rows, :] = w_ref[:, lanes(c)]
+        at += rows
+    for a, b in ((k0, k1), (v0, v1)):
+        near = a.shape[0] // 2
+        both = [x[...].astype(F32)[:near] for x in (a, b)]
+        out_ref[at : at + 2 * near, :] = jnp.concatenate(both, axis=0).astype(BF)
+        at += 2 * near
+    for n in range(4):
+        out_ref[at : at + share, :] = shares_ref[:, lanes(n)]
+        at += share
+
+
+def payload(near, w_out, heads, shares):
+    rows = w_out.size // HEAD_DIM + 4 * near + shares.size // HEAD_DIM
+
+    def top(shape):
+        return pl.BlockSpec(shape, lambda i: (0, 0))
+
+    return pl.pallas_call(
+        payload_kernel,
+        out_shape=jax.ShapeDtypeStruct((rows, HEAD_DIM), BF),
+        grid=(1,),
+        in_specs=[top(w_out.shape)] + [top((2 * near, HEAD_DIM))] * 4 + [top(shares.shape)],
+        out_specs=top((rows, HEAD_DIM)),
+        compiler_params=pltpu.CompilerParams(vmem_limit_bytes=16 << 20),
+    )(w_out, *heads, shares)
 
 
 def unpack_kernel(moves, x_ref, quarter_ref, w_ref):
@@ -304,12 +337,7 @@
 
     packs = [position_pack(jnp.concatenate(pair, axis=1), parts) for pair in ((q0, q1), (k0, k1), (v0, v1))]
     near = BLOCK // parts
-    sent = jnp.concatenate(
-        [w_out[:, lanes(c)] for c in range(w_out.shape[1] // HEAD_DIM)]
-        + [x[:near] for x in (k0, k1, v0, v1)]
-        + [shares[:, lanes(c)] for c in range(4)],
-        axis=0,
-    )
+    sent = payload(near, w_out, (k0, k1, v0, v1), shares)
     packed, sent = lax.optimization_barrier((jnp.concatenate(packs, axis=2), sent))
     moved = exchange(packed).reshape(BLOCK, -1)
     rows_z = lax.all_gather(sent, "ctx", axis=0, axis_index_groups=along_z)

time: 309 us -> 300 us (0.971)
  local copies, waits for them, and re-layouts: 21.1 us -> 11.9 us
  Pallas kernels: 29.3 us -> 26.2 us
    unnamed x30 -> x20, local copies, waits for them, and re-layouts: 14.7 us -> 6.03 us
    pallas_call x2, Pallas kernels: 17.4 us -> 13.6 us  [attention(): pl.pallas_call(lambda *refs: attention_kernel(heads, *refs), out_shape=ja...]
  transfers between devices with their start and end apart: 18 -> 18, of which waited for: 5 -> 7; matrix products, arithmetic and copies ran while one was open for 5% -> 2% of each run, Pallas kernels for 6% -> 5%
where the time goes in v8:
time: 300 us; the launch traced here: 299 us
  waiting for transfers between devices  167 us (56%)
  starting transfers between devices  70.8 us (24%)
  Pallas kernels  26.2 us (9%)
  between operations  17.9 us (6%)
  local copies, waits for them, and re-layouts  11.9 us (4%)
  other arithmetic  5.37 us (2%)
    all_gather x1, waiting for transfers between devices, body(): rows_z = lax.all_gather(sent, 'ctx', axis=0, axis_index_groups=along_z)  80.7 us
    all_gather x1, waiting for transfers between devices, body(): lax.all_gather(attn, 'head', axis=1, tiled=True)  40.5 us
    all_to_all x2, starting transfers between devices, exchange(): return lax.all_to_all(x, 'ctx', 0, 0, tiled=True)  28.5 us
    ppermute x3, waiting for transfers between devices, along_y(): lax.ppermute(x, 'ctx', [(i, i ^ deep * k) for i in range(parts)])  23.5 us
    all_to_all x2, waiting for transfers between devices, exchange(): return lax.all_to_all(x, 'ctx', 0, 0, tiled=True)  21.6 us
    ppermute x6, starting transfers between devices, scattered(): lax.ppermute(x[k * rows:(k + 1) * rows], 'ctx', [(i, i + k * unit) for i...  20.4 us
    pallas_call x2, Pallas kernels, attention(): pl.pallas_call(lambda *refs: attention_kernel(heads, *refs), out_shape=ja...  13.6 us
    ppermute x2, starting transfers between devices, both_ways(): left = lax.ppermute(x, 'ctx', [(i, i + 1) for i in range(count - 1)])  10.2 us
  transfers between devices with their start and end apart: 18, of which 7 were waited for; matrix products, arithmetic and copies ran while one was open for 2% of the time, Pallas kernels for 5%

profile of v8, /device:TPU:1, one launch (start us, length us, event | category | flops | bytes accessed | tf_op | source)
XLA Modules:
  0.0 299.5 jit_solution(17103524240736755789)
XLA Ops:
  6.5 0.7 broadcast_compare_fusion.1
  7.2 0.1 eq.57
  7.3 0.1 select_select_fusion.1
  7.4 0.1 broadcast_add_fusion
  7.4 0.7 fusion.14
  10.0 1.5 constant_dynamic-slice_fusion.4
  11.6 0.8 pad_maximum_fusion.9
  12.3 4.0 %collective-permute-start.2 = (bf16[128,512]{1,0:T(8,128)(2,1)}, bf16[128,512]{1,0:T(8,128)(2,1)S(1)}, u32[]{:S(2)}, u32[]{:S(2)}) collective-permute-start(bf16[128,512]{1,0:T(8,128)(2,1)} %get-tuple-element.65), channel_id=1, source_target_pairs={{0,128},{1,129},{2,130},{3,131},{4,132},{5,133},{6,134},{7,135}} | collective-permute-start | bytes 393224 | tf_op jit(solution)/shard_map/ppermute | solution.py:299
  16.4 2.3 collective-permute-start.1
  18.7 1.9 collective-permute-start
  20.6 0.8 constant_dynamic-slice_fusion.8
  21.4 0.1 pad_maximum_fusion.3
  21.5 0.1 pad_maximum_fusion.2
  21.6 0.1 pad_maximum_fusion.1
  21.7 0.5 collective-permute-done
  22.2 0.1 fusion.2
  22.3 3.5 %collective-permute-start.5 = (bf16[32,512]{1,0:T(8,128)(2,1)S(1)}, bf16[32,512]{1,0:T(8,128)(2,1)S(1)}, u32[]{:S(2)}, u32[]{:S(2)}) collective-permute-start(bf16[32,512]{1,0:T(8,128)(2,1)S(1)} %get-tuple-element.89), channel_id=1, source_target_pairs={{0,32},{128,160},{256,288},{384,416},{1,33},{129,161},{257,289},{3... | collective-permute-start | bytes 98312 | tf_op jit(solution)/shard_map/ppermute | solution.py:299
  25.8 7.3 %collective-permute-start.4 = (bf16[32,512]{1,0:T(8,128)(2,1)S(1)}, bf16[32,512]{1,0:T(8,128)(2,1)S(1)}, u32[]{:S(2)}, u32[]{:S(2)}) collective-permute-start(bf16[32,512]{1,0:T(8,128)(2,1)S(1)} %get-tuple-element.90), channel_id=1, source_target_pairs={{0,64},{128,192},{256,320},{384,448},{1,65},{129,193},{257,321},{3... | collective-permute-start | bytes 98312 | tf_op jit(solution)/shard_map/ppermute | solution.py:299
  33.1 1.3 collective-permute-start.3
  34.4 0.0 copy-start.2
  34.5 1.3 pad_maximum_fusion
  35.8 0.7 shard_map.64
  36.4 0.0 all-gather.9.cloned.1.call-update
  38.4 0.6 dynamic_slice.42.moves
  39.0 14.5 %all-to-all-start = ((bf16[64,8,1536]{2,1,0:T(8,128)(2,1)}), bf16[64,8,1536]{2,1,0:T(8,128)(2,1)S(1)}, u32[]{:S(2)}, u32[]{:S(2)}) async-start(bf16[64,8,1536]{2,1,0:T(8,128)(2,1)} %pad_maximum_fusion), calls=%async_computation | async-start | bytes 3145728 | tf_op jit(solution)/shard_map/all_to_all | solution.py:285
  53.5 0.0 all-gather.7.cloned.1.call-start
  53.5 80.7 %all-gather.9.cloned.1.call-done = bf16[4864,128]{1,0:T(8,128)(2,1)} async-done(((bf16[304,128]{1,0:T(8,128)(2,1)}), bf16[4864,128]{1,0:T(8,128)(2,1)}) %all-gather.9.cloned.1.call-update) | async-done | bytes 1245200 | tf_op jit(solution)/shard_map/all_gather | solution.py:343
  134.3 1.3 copy-done.3
  135.6 1.6 shard_map.65
  137.3 0.1 pad_maximum_fusion.4.refs_2_
  137.3 2.0 shard_map.66
  139.4 1.3 collective-permute-start.7
  140.6 6.2 %collective-permute-start.6 = (bf16[512,1024]{1,0:T(8,128)(2,1)}, bf16[512,1024]{1,0:T(8,128)(2,1)S(1)}, u32[]{:S(2)}, u32[]{:S(2)}) collective-permute-start(bf16[512,1024]{1,0:T(8,128)(2,1)} %get-tuple-element.41.refs_2_), channel_id=1, source_target_pairs={{0,8},{8,16},{16,24},{24,32},{32,40},{40,48},{48,56},{56,64},{64,7... | collective-permute-start | bytes 3145736 | tf_op jit(solution)/shard_map/ppermute | solution.py:289
  146.9 3.5 %collective-permute-start.10 = (bf16[128,768]{1,0:T(8,128)(2,1)}, bf16[128,768]{1,0:T(8,128)(2,1)S(1)}, u32[]{:S(2)}, u32[]{:S(2)}) collective-permute-start(bf16[128,768]{1,0:T(8,128)(2,1)} %get-tuple-element.50.refs_5_), channel_id=1, source_target_pairs={{0,384},{8,392},{16,400},{24,408},{32,416},{40,424},{48,432},{56,4... | collective-permute-start | bytes 589832 | tf_op jit(solution)/shard_map/ppermute | solution.py:353
  150.3 2.9 collective-permute-start.9
  153.3 2.6 collective-permute-start.8
  155.9 22.0 %collective-permute-done.9.refs_7_ = bf16[128,768]{1,0:T(8,128)(2,1)} collective-permute-done((bf16[128,768]{1,0:T(8,128)(2,1)}, bf16[128,768]{1,0:T(8,128)(2,1)}, u32[]{:S(2)}, u32[]{:S(2)}) %collective-permute-start.9) | collective-permute-done | bytes 196640 | tf_op jit(solution)/shard_map/ppermute | solution.py:353
  177.9 1.4 collective-permute-done.8.refs_6_
  179.4 0.0 all-gather.7.cloned.1.call-update
  179.4 0.7 broadcast_compare_fusion
  180.1 0.1 broadcast_add_fusion.1
  180.2 1.3 collective-permute-start.12
  181.5 4.0 %collective-permute-start.11 = (bf16[512,512]{1,0:T(8,128)(2,1)S(1)}, bf16[512,512]{1,0:T(8,128)(2,1)S(1)}, u32[]{:S(2)}, u32[]{:S(2)}) collective-permute-start(bf16[512,512]{1,0:T(8,128)(2,1)S(1)} %pad_maximum_fusion.4.refs_2_), channel_id=1, source_target_pairs={{0,8},{8,16},{16,24},{24,32},{32,40},{40,48},{48,56},{56,64},{64,7... | collective-permute-start | bytes 1572872 | tf_op jit(solution)/shard_map/ppermute | solution.py:289
  185.5 0.2 fusion.6
  185.7 0.1 add_convert_fusion.refs_0_
  185.8 9.0 %shard_map.67 = bf16[512,512]{1,0:T(8,128)(2,1)} custom-call(s32[2,6]{1,0:T(2,128)S(1)} %add_convert_fusion.refs_0_, bf16[512,512]{1,0:T(8,128)(2,1)S(1)} %get-tuple-element.40.refs_1_, bf16[512,1024]{1,0:T(8,128)(2,1)} %get-tuple-element.41.refs_2_, bf16[512,1024]{1,0:T(8,128)(2,1)S(1)} %collective-permute-done.6.refs_3_, ...), custom_call_target="tpu_custom_call" | custom-call | flops 3221225472 | bytes 4194304 | tf_op jit(solution)/shard_map/pallas_call | solution.py:80
  194.8 0.4 collective-permute-done.12.refs_4_
  195.2 0.8 copy-done.4
  196.0 0.8 copy-done.6
  196.8 14.1 %all-to-all-start.1 = ((bf16[64,8,512]{2,1,0:T(8,128)(2,1)}), bf16[64,8,512]{2,1,0:T(8,128)(2,1)S(1)}, u32[]{:S(2)}, u32[]{:S(2)}) async-start(bf16[64,8,512]{2,1,0:T(8,128)(2,1)} %bitcast.14), calls=%async_computation.1 | async-start | bytes 1048576 | tf_op jit(solution)/shard_map/all_to_all | solution.py:285
  210.8 0.0 all-gather.5.cloned.1.call-start
  211.5 1.0 fusion.12
  212.6 4.6 %shard_map.68 = bf16[512,256]{1,0:T(8,128)(2,1)S(1)} custom-call(s32[2,6]{1,0:T(2,128)S(1)} %add_convert_fusion.refs_0_, bf16[512,256]{1,0:T(8,128)(2,1)S(1)} %pad_maximum_fusion.5.refs_1_, bf16[512,512]{1,0:T(8,128)(2,1)S(1)} %pad_maximum_fusion.4.refs_2_, bf16[512,512]{1,0:T(8,128)(2,1)S(1)} %copy-done.7, bf16[512,512]{1,0:T(8,128)(2,1)S(1)} %copy-done.5, ...), custom_call_target="tpu_custom_call" | custom-call | flops 1610612736 | bytes 2097152 | tf_op jit(solution)/shard_map/pallas_call | solution.py:80
  217.2 1.0 fusion.8
  218.2 21.6 %all-to-all-done.1 = bf16[64,8,512]{2,1,0:T(8,128)(2,1)S(1)} async-done(((bf16[64,8,512]{2,1,0:T(8,128)(2,1)}), bf16[64,8,512]{2,1,0:T(8,128)(2,1)S(1)}, u32[]{:S(2)}, u32[]{:S(2)}) %all-to-all-start.1) | async-done | bytes 524320 | tf_op jit(solution)/shard_map/all_to_all | solution.py:285
  239.8 0.1 fusion.7
  239.9 1.0 maximum_maximum_fusion
  240.9 0.0 all-gather.5.cloned.1.call-update
  241.0 0.1 add.108.order
  241.0 1.7 copy-done.1
  242.7 0.8 shard_map.69.w_ref
  243.5 1.4 copy-done
  244.9 40.5 %all-gather.5.cloned.1.call-done.attn_ref = bf16[1024,3072]{1,0:T(8,128)(2,1)} async-done(((bf16[1024,384]{1,0:T(8,128)(2,1)}), bf16[1024,3072]{1,0:T(8,128)(2,1)}) %all-gather.5.cloned.1.call-update) | async-done | bytes 6291472 | tf_op jit(solution)/shard_map/all_gather | solution.py:370
  285.5 7.5 %shard_map.70 = bf16[1024,384]{1,0:T(8,128)(2,1)} custom-call(bf16[1024,3072]{1,0:T(8,128)(2,1)} %all-gather.5.cloned.1.call-done.attn_ref, bf16[3072,384]{1,0:T(8,128)(2,1)} %copy-done), custom_call_target="tpu_custom_call" | custom-call | tf_op jit(solution)/shard_map/pallas_call | solution.py:254
  (37 shorter events, 0.2 us)
Async XLA Ops:
  6.5 127.7 %all-gather.9.cloned.1.call-start = ((), (), s32[]{:S(2)}) async-start(), calls=%async_computation.4 | async-start | bytes 1323008 | tf_op jit(solution)/shard_map/all_gather | solution.py:343
  10.0 10.6 %copy-start.8 = (bf16[1024,384]{1,0:T(8,128)(2,1)S(1)}, bf16[1024,384]{1,0:T(8,128)(2,1)}, u32[]{:S(2)}) copy-start(bf16[1024,384]{1,0:T(8,128)(2,1)} %param.6) | copy-start | bytes 2359300
  12.3 9.3 %collective-permute-start.2 = (bf16[128,512]{1,0:T(8,128)(2,1)}, bf16[128,512]{1,0:T(8,128)(2,1)S(1)}, u32[]{:S(2)}, u32[]{:S(2)}) collective-permute-start(bf16[128,512]{1,0:T(8,128)(2,1)} %get-tuple-element.65), channel_id=1, source_target_pairs={{0,128},{1,129},{2,130},{3,131},{4,132},{5,133},{6,134},{7,135}} | collective-permute-start | bytes 393224 | tf_op jit(solution)/shard_map/ppermute | solution.py:299
  16.4 5.3 %collective-permute-start.1 = (bf16[128,512]{1,0:T(8,128)(2,1)}, bf16[128,512]{1,0:T(8,128)(2,1)S(1)}, u32[]{:S(2)}, u32[]{:S(2)}) collective-permute-start(bf16[128,512]{1,0:T(8,128)(2,1)} %get-tuple-element.66), channel_id=1, source_target_pairs={{0,256},{1,257},{2,258},{3,259},{4,260},{5,261},{6,262},{7,263}} | collective-permute-start | bytes 393224 | tf_op jit(solution)/shard_map/ppermute | solution.py:299
  18.7 3.5 %collective-permute-start = (bf16[128,512]{1,0:T(8,128)(2,1)}, bf16[128,512]{1,0:T(8,128)(2,1)}, u32[]{:S(2)}, u32[]{:S(2)}) collective-permute-start(bf16[128,512]{1,0:T(8,128)(2,1)} %get-tuple-element.67), channel_id=1, source_target_pairs={{0,384},{1,385},{2,386},{3,387},{4,388},{5,389},{6,390},{7,391}} | collective-permute-start | bytes 393224 | tf_op jit(solution)/shard_map/ppermute | solution.py:299
  22.3 13.5 %collective-permute-start.5 = (bf16[32,512]{1,0:T(8,128)(2,1)S(1)}, bf16[32,512]{1,0:T(8,128)(2,1)S(1)}, u32[]{:S(2)}, u32[]{:S(2)}) collective-permute-start(bf16[32,512]{1,0:T(8,128)(2,1)S(1)} %get-tuple-element.89), channel_id=1, source_target_pairs={{0,32},{128,160},{256,288},{384,416},{1,33},{129,161},{257,289},{3... | collective-permute-start | bytes 98312 | tf_op jit(solution)/shard_map/ppermute | solution.py:299
  25.8 9.9 %collective-permute-start.4 = (bf16[32,512]{1,0:T(8,128)(2,1)S(1)}, bf16[32,512]{1,0:T(8,128)(2,1)S(1)}, u32[]{:S(2)}, u32[]{:S(2)}) collective-permute-start(bf16[32,512]{1,0:T(8,128)(2,1)S(1)} %get-tuple-element.90), channel_id=1, source_target_pairs={{0,64},{128,192},{256,320},{384,448},{1,65},{129,193},{257,321},{3... | collective-permute-start | bytes 98312 | tf_op jit(solution)/shard_map/ppermute | solution.py:299
  33.1 2.6 collective-permute-start.3
  34.4 1.3 copy-start.2
  34.5 3.9 %copy-start.9 = (s32[24]{0:T(128)S(1)}, s32[24]{0:T(128)}, u32[]{:S(2)}) copy-start(s32[24]{0:T(128)} %param.10) | copy-start | bytes 292
  39.0 98.3 %all-to-all-start = ((bf16[64,8,1536]{2,1,0:T(8,128)(2,1)}), bf16[64,8,1536]{2,1,0:T(8,128)(2,1)S(1)}, u32[]{:S(2)}, u32[]{:S(2)}) async-start(bf16[64,8,1536]{2,1,0:T(8,128)(2,1)} %pad_maximum_fusion), calls=%async_computation | async-start | bytes 3145728 | tf_op jit(solution)/shard_map/all_to_all | solution.py:285
  53.5 187.6 %all-gather.7.cloned.1.call-start = ((), (), s32[]{:S(2)}) async-start(), calls=%async_computation.3 | async-start | bytes 2949120 | tf_op jit(solution)/shard_map/all_gather | solution.py:358
  134.3 1.3 copy-start.3
  139.4 40.0 %collective-permute-start.7 = (bf16[512,1024]{1,0:T(8,128)(2,1)}, bf16[512,1024]{1,0:T(8,128)(2,1)S(1)}, u32[]{:S(2)}, u32[]{:S(2)}) collective-permute-start(bf16[512,1024]{1,0:T(8,128)(2,1)} %get-tuple-element.41.refs_2_), channel_id=1, source_target_pairs={{8,0},{16,8},{24,16},{32,24},{40,32},{48,40},{56,48},{64,56},{72,6... | collective-permute-start | bytes 3145736 | tf_op jit(solution)/shard_map/ppermute | solution.py:290
  140.6 38.7 %collective-permute-start.6 = (bf16[512,1024]{1,0:T(8,128)(2,1)}, bf16[512,1024]{1,0:T(8,128)(2,1)S(1)}, u32[]{:S(2)}, u32[]{:S(2)}) collective-permute-start(bf16[512,1024]{1,0:T(8,128)(2,1)} %get-tuple-element.41.refs_2_), channel_id=1, source_target_pairs={{0,8},{8,16},{16,24},{24,32},{32,40},{40,48},{48,56},{56,64},{64,7... | collective-permute-start | bytes 3145736 | tf_op jit(solution)/shard_map/ppermute | solution.py:289
  146.9 9.0 %collective-permute-start.10 = (bf16[128,768]{1,0:T(8,128)(2,1)}, bf16[128,768]{1,0:T(8,128)(2,1)S(1)}, u32[]{:S(2)}, u32[]{:S(2)}) collective-permute-start(bf16[128,768]{1,0:T(8,128)(2,1)} %get-tuple-element.50.refs_5_), channel_id=1, source_target_pairs={{0,384},{8,392},{16,400},{24,408},{32,416},{40,424},{48,432},{56,4... | collective-permute-start | bytes 589832 | tf_op jit(solution)/shard_map/ppermute | solution.py:353
  150.3 27.6 %collective-permute-start.9 = (bf16[128,768]{1,0:T(8,128)(2,1)}, bf16[128,768]{1,0:T(8,128)(2,1)}, u32[]{:S(2)}, u32[]{:S(2)}) collective-permute-start(bf16[128,768]{1,0:T(8,128)(2,1)} %get-tuple-element.50.refs_5_), channel_id=1, source_target_pairs={{0,256},{8,264},{16,272},{24,280},{32,288},{40,296},{48,304},{56,3... | collective-permute-start | bytes 589832 | tf_op jit(solution)/shard_map/ppermute | solution.py:353
  153.3 26.1 %collective-permute-start.8 = (bf16[128,768]{1,0:T(8,128)(2,1)}, bf16[128,768]{1,0:T(8,128)(2,1)}, u32[]{:S(2)}, u32[]{:S(2)}) collective-permute-start(bf16[128,768]{1,0:T(8,128)(2,1)} %get-tuple-element.50.refs_5_), channel_id=1, source_target_pairs={{0,128},{8,136},{16,144},{24,152},{32,160},{40,168},{48,176},{56,1... | collective-permute-start | bytes 589832 | tf_op jit(solution)/shard_map/ppermute | solution.py:353
  180.2 15.0 %collective-permute-start.12 = (bf16[512,512]{1,0:T(8,128)(2,1)S(1)}, bf16[512,512]{1,0:T(8,128)(2,1)S(1)}, u32[]{:S(2)}, u32[]{:S(2)}) collective-permute-start(bf16[512,512]{1,0:T(8,128)(2,1)S(1)} %pad_maximum_fusion.4.refs_2_), channel_id=1, source_target_pairs={{8,0},{16,8},{24,16},{32,24},{40,32},{48,40},{56,48},{64,56},{72,6... | collective-permute-start | bytes 1572872 | tf_op jit(solution)/shard_map/ppermute | solution.py:290
  181.5 14.5 %collective-permute-start.11 = (bf16[512,512]{1,0:T(8,128)(2,1)S(1)}, bf16[512,512]{1,0:T(8,128)(2,1)S(1)}, u32[]{:S(2)}, u32[]{:S(2)}) collective-permute-start(bf16[512,512]{1,0:T(8,128)(2,1)S(1)} %pad_maximum_fusion.4.refs_2_), channel_id=1, source_target_pairs={{0,8},{8,16},{16,24},{24,32},{32,40},{40,48},{48,56},{56,64},{64,7... | collective-permute-start | bytes 1572872 | tf_op jit(solution)/shard_map/ppermute | solution.py:289
  195.2 0.8 copy-start.4
  196.0 0.8 copy-start.6
  196.8 15.8 %copy-start.5 = (bf16[512,512]{1,0:T(8,128)(2,1)S(1)}, bf16[512,512]{1,0:T(8,128)(2,1)}, u32[]{:S(2)}) copy-start(bf16[512,512]{1,0:T(8,128)(2,1)} %copy-done.4) | copy-start | bytes 1572868
  196.8 15.8 %copy-start.7 = (bf16[512,512]{1,0:T(8,128)(2,1)S(1)}, bf16[512,512]{1,0:T(8,128)(2,1)}, u32[]{:S(2)}) copy-start(bf16[512,512]{1,0:T(8,128)(2,1)} %copy-done.6) | copy-start | bytes 1572868
  196.8 43.1 %all-to-all-start.1 = ((bf16[64,8,512]{2,1,0:T(8,128)(2,1)}), bf16[64,8,512]{2,1,0:T(8,128)(2,1)S(1)}, u32[]{:S(2)}, u32[]{:S(2)}) async-start(bf16[64,8,512]{2,1,0:T(8,128)(2,1)} %bitcast.14), calls=%async_computation.1 | async-start | bytes 1048576 | tf_op jit(solution)/shard_map/all_to_all | solution.py:285
  210.8 74.6 %all-gather.5.cloned.1.call-start = ((), (), s32[]{:S(2)}) async-start(), calls=%async_computation.2 | async-start | bytes 7077888 | tf_op jit(solution)/shard_map/all_gather | solution.py:370
  241.0 1.7 copy-start.1
  243.5 1.5 copy-start
Sparse Core Ops, SparseCore 0:
  36.6 97.6 all-gather.8
  179.5 40.9 all-gather.6
  241.1 44.3 all-gather.4

commit v9 on v8

--- a/solution.py
+++ b/solution.py
@@ -41,35 +41,32 @@
             m_ref[...] = jnp.full_like(m_ref, -jnp.inf)
             l_ref[...] = jnp.zeros_like(l_ref)
             acc_ref[...] = jnp.zeros_like(acc_ref)
+            m = jnp.full_like(m_ref, -jnp.inf)
             for n in range(SPAN + 1):
-
-                @pl.when(bits[b, n] > 0)
-                def _():
-                    s = lax.dot_general(
-                        query, tile(0, b, n, slot), (((1,), (1,)), ((), ())), preferred_element_type=F32
-                    )
-                    s_ref[n] = s
-                    m = m_ref[...]
-                    for c in range(BLOCK // HEAD_DIM):
-                        m = jnp.maximum(m, s[:, lanes(c)])
-                    m_ref[...] = m
+                s = lax.dot_general(
+                    query, tile(0, b, n, slot), (((1,), (1,)), ((), ())), preferred_element_type=F32
+                )
+                s = jnp.where(bits[b, n] > 0, s, -jnp.inf)
+                s_ref[n] = s
+                for c in range(BLOCK // HEAD_DIM):
+                    m = jnp.maximum(m, s[:, lanes(c)])
+            m_ref[...] = m
 
             m_ref[...] = jnp.broadcast_to(jnp.max(m_ref[...], axis=1, keepdims=True), m_ref.shape)
+            peak = m_ref[...]
+            total = jnp.zeros_like(l_ref)
+            mixed = jnp.zeros_like(acc_ref)
             for n in range(SPAN + 1):
-
-                @pl.when(bits[b, n] > 0)
-                def _():
-                    peak = m_ref[...]
-                    total = l_ref[...]
-                    parts = []
-                    for c in range(BLOCK // HEAD_DIM):
-                        w = jnp.exp2((s_ref[n, :, lanes(c)] - peak) * RATE)
-                        total = total + w
-                        parts.append(w.astype(BF))
-                    l_ref[...] = total
-                    acc_ref[...] += jnp.dot(
-                        jnp.concatenate(parts, axis=1), tile(1, b, n, slot), preferred_element_type=F32
-                    )
+                parts = []
+                for c in range(BLOCK // HEAD_DIM):
+                    w = jnp.exp2((s_ref[n, :, lanes(c)] - peak) * RATE)
+                    total = total + w
+                    parts.append(w.astype(BF))
+                mixed = mixed + jnp.dot(
+                    jnp.concatenate(parts, axis=1), tile(1, b, n, slot), preferred_element_type=F32
+                )
+            l_ref[...] = total
+            acc_ref[...] = mixed
 
             total = jnp.sum(l_ref[...], axis=1, keepdims=True)
             out_ref[:, here] = (acc_ref[...] / total).astype(BF)
@@ -229,42 +226,6 @@
     )(order, w)
 
 
-def projection_kernel(attn_ref, w_ref, out_ref, total_ref):
-    part = jnp.dot(attn_ref[...], w_ref[...], preferred_element_type=F32)
-    step = pl.program_id(0)
-    last = pl.num_programs(0) - 1
-
-    @pl.when(step == 0)
-    def _():
-        total_ref[...] = part
-
-    @pl.when((step > 0) & (step < last))
-    def _():
-        total_ref[...] += part
-
-    @pl.when(step == last)
-    def _():
-        out_ref[...] = (total_ref[...] + part).astype(BF)
-
-
-def projection(attn, w):
-    rows, depth = attn.shape
-    cols = w.shape[1]
-    steps = 4
-    return pl.pallas_call(
-        projection_kernel,
-        out_shape=jax.ShapeDtypeStruct((rows, cols), BF),
-        grid=(steps,),
-        in_specs=[
-            pl.BlockSpec((rows, depth // steps), lambda i: (0, i)),
-            pl.BlockSpec((depth // steps, cols), lambda i: (i, 0)),
-        ],
-        out_specs=pl.BlockSpec((rows, cols), lambda i: (0, 0)),
-        scratch_shapes=[pltpu.VMEM((rows, cols), F32)],
-        compiler_params=pltpu.CompilerParams(vmem_limit_bytes=56 << 20),
-    )(attn, w)
-
-
 def slots_of(labels):
     temporal = labels == 1
     a = jnp.where(temporal[:, 0], 0, jnp.where(temporal[:, 1], 1, 2))
@@ -367,7 +328,8 @@
     back = back.reshape(parts, BLOCK // parts, 2, 2 * HEAD_DIM).transpose(0, 2, 1, 3).reshape(2 * BLOCK, 2 * HEAD_DIM)
     still = jnp.concatenate([out[:, lanes(1)], out[:, lanes(3)]], axis=0)
     attn = jnp.concatenate([back[:, lanes(0)], jnp.where(moves[0] > 0, back[:, lanes(1)], still), attn2], axis=1)
-    return projection(lax.all_gather(attn, "head", axis=1, tiled=True), slot_order(order, w))
+    everything = lax.all_gather(attn, "head", axis=1, tiled=True)
+    return jnp.dot(everything, slot_order(order, w), preferred_element_type=F32).astype(BF)
 
 
 def solution(mesh):

time: 300 us -> 296 us (0.987)
  starting transfers between devices: 70.8 us -> 63 us
  matrix products: 0 us -> 6.43 us
    pallas_call x1 -> x0, Pallas kernels: 7.46 us -> none  [projection(): pl.pallas_call(projection_kernel, out_shape=jax.ShapeDtypeStruct((rows, c...]
    all_to_all x2, starting transfers between devices: 28.5 us -> 21.1 us  [exchange(): return lax.all_to_all(x, 'ctx', 0, 0, tiled=True)]
    pallas_call x2, Pallas kernels: 13.6 us -> 20.8 us  [attention(): pl.pallas_call(lambda *refs: attention_kernel(heads, *refs), out_shape=ja...]
    dot_general x0 -> x1, matrix products: none -> 6.43 us  [body(): jnp.dot(everything, slot_order(order, w), preferred_element_type=F32)]
    all_to_all x2, waiting for transfers between devices: 21.6 us -> 18.4 us  [exchange(): return lax.all_to_all(x, 'ctx', 0, 0, tiled=True)]
    unnamed x20 -> x18, local copies, waits for them, and re-layouts: 6.03 us -> 4.58 us
  transfers between devices with their start and end apart: 18 -> 18, of which waited for: 7 -> 6; matrix products, arithmetic and copies ran while one was open for 2% -> 2% of each run, Pallas kernels for 5% -> 8%
where the time goes in v9:
time: 296 us; the launch traced here: 295 us
  waiting for transfers between devices  167 us (56%)
  starting transfers between devices  63 us (21%)
  Pallas kernels  25.8 us (9%)
  between operations  17.4 us (6%)
  local copies, waits for them, and re-layouts  10.3 us (3%)
  matrix products  6.43 us (2%)
  other arithmetic  5.36 us (2%)
    all_gather x1, waiting for transfers between devices, body(): rows_z = lax.all_gather(sent, 'ctx', axis=0, axis_index_groups=along_z)  81.7 us
    all_gather x1, waiting for transfers between devices, body(): everything = lax.all_gather(attn, 'head', axis=1, tiled=True)  42 us
    ppermute x3, waiting for transfers between devices, along_y(): lax.ppermute(x, 'ctx', [(i, i ^ deep * k) for i in range(parts)])  24.2 us
    all_to_all x2, starting transfers between devices, exchange(): return lax.all_to_all(x, 'ctx', 0, 0, tiled=True)  21.1 us
    pallas_call x2, Pallas kernels, attention(): pl.pallas_call(lambda *refs: attention_kernel(heads, *refs), out_shape=ja...  20.8 us
    ppermute x6, starting transfers between devices, scattered(): lax.ppermute(x[k * rows:(k + 1) * rows], 'ctx', [(i, i + k * unit) for i...  20.4 us
    all_to_all x2, waiting for transfers between devices, exchange(): return lax.all_to_all(x, 'ctx', 0, 0, tiled=True)  18.4 us
    ppermute x2, starting transfers between devices, both_ways(): left = lax.ppermute(x, 'ctx', [(i, i + 1) for i in range(count - 1)])  9.69 us
  transfers between devices with their start and end apart: 18, of which 6 were waited for; matrix products, arithmetic and copies ran while one was open for 2% of the time, Pallas kernels for 8%

profile of v9, /device:TPU:1, one launch (start us, length us, event | category | flops | bytes accessed | tf_op | source)
XLA Modules:
  0.0 295.2 jit_solution(1651269312466991451)
XLA Ops:
  6.5 0.7 broadcast_compare_fusion.1
  7.2 0.1 eq.57
  7.3 0.1 select_select_fusion.1
  7.4 0.1 broadcast_add_fusion
  7.4 0.6 fusion.14
  9.8 0.0 copy-start.7
  9.8 1.5 constant_dynamic-slice_fusion.4
  11.3 0.8 pad_maximum_fusion.9
  12.1 4.0 %collective-permute-start.2 = (bf16[128,512]{1,0:T(8,128)(2,1)}, bf16[128,512]{1,0:T(8,128)(2,1)S(1)}, u32[]{:S(2)}, u32[]{:S(2)}) collective-permute-start(bf16[128,512]{1,0:T(8,128)(2,1)} %get-tuple-element.65), channel_id=1, source_target_pairs={{0,128},{1,129},{2,130},{3,131},{4,132},{5,133},{6,134},{7,135}} | collective-permute-start | bytes 393224 | tf_op jit(solution)/shard_map/ppermute | solution.py:260
  16.1 2.3 collective-permute-start.1
  18.4 1.9 collective-permute-start
  20.4 0.8 constant_dynamic-slice_fusion.8
  21.2 0.1 pad_maximum_fusion.3
  21.3 0.1 pad_maximum_fusion.2
  21.4 0.1 pad_maximum_fusion.1
  21.5 0.5 collective-permute-done
  22.0 0.1 fusion.2
  22.1 3.5 %collective-permute-start.5 = (bf16[32,512]{1,0:T(8,128)(2,1)S(1)}, bf16[32,512]{1,0:T(8,128)(2,1)S(1)}, u32[]{:S(2)}, u32[]{:S(2)}) collective-permute-start(bf16[32,512]{1,0:T(8,128)(2,1)S(1)} %get-tuple-element.89), channel_id=1, source_target_pairs={{0,32},{128,160},{256,288},{384,416},{1,33},{129,161},{257,289},{3... | collective-permute-start | bytes 98312 | tf_op jit(solution)/shard_map/ppermute | solution.py:260
  25.6 7.3 %collective-permute-start.4 = (bf16[32,512]{1,0:T(8,128)(2,1)S(1)}, bf16[32,512]{1,0:T(8,128)(2,1)S(1)}, u32[]{:S(2)}, u32[]{:S(2)}) collective-permute-start(bf16[32,512]{1,0:T(8,128)(2,1)S(1)} %get-tuple-element.90), channel_id=1, source_target_pairs={{0,64},{128,192},{256,320},{384,448},{1,65},{129,193},{257,321},{3... | collective-permute-start | bytes 98312 | tf_op jit(solution)/shard_map/ppermute | solution.py:260
  32.9 1.3 collective-permute-start.3
  34.2 0.0 copy-start.1
  34.2 0.0 copy-start.8
  34.2 1.3 pad_maximum_fusion
  35.5 0.7 shard_map.64
  36.2 0.0 all-gather.9.cloned.1.call-update
  37.9 0.6 dynamic_slice.42.moves
  38.4 14.5 %all-to-all-start = ((bf16[64,8,1536]{2,1,0:T(8,128)(2,1)}), bf16[64,8,1536]{2,1,0:T(8,128)(2,1)S(1)}, u32[]{:S(2)}, u32[]{:S(2)}) async-start(bf16[64,8,1536]{2,1,0:T(8,128)(2,1)} %pad_maximum_fusion), calls=%async_computation | async-start | bytes 3145728 | tf_op jit(solution)/shard_map/all_to_all | solution.py:246
  52.9 0.0 all-gather.7.cloned.1.call-start
  53.0 81.7 %all-gather.9.cloned.1.call-done = bf16[4864,128]{1,0:T(8,128)(2,1)} async-done(((bf16[304,128]{1,0:T(8,128)(2,1)}), bf16[4864,128]{1,0:T(8,128)(2,1)}) %all-gather.9.cloned.1.call-update) | async-done | bytes 1245200 | tf_op jit(solution)/shard_map/all_gather | solution.py:304
  134.6 1.3 copy-done.2
  135.9 1.6 shard_map.65
  137.5 0.1 pad_maximum_fusion.4.refs_2_
  137.6 2.0 shard_map.66
  139.6 1.3 collective-permute-start.7
  140.9 5.5 %collective-permute-start.6 = (bf16[512,1024]{1,0:T(8,128)(2,1)}, bf16[512,1024]{1,0:T(8,128)(2,1)S(1)}, u32[]{:S(2)}, u32[]{:S(2)}) collective-permute-start(bf16[512,1024]{1,0:T(8,128)(2,1)} %get-tuple-element.41.refs_2_), channel_id=1, source_target_pairs={{0,8},{8,16},{16,24},{24,32},{32,40},{40,48},{48,56},{56,64},{64,7... | collective-permute-start | bytes 3145736 | tf_op jit(solution)/shard_map/ppermute | solution.py:250
  146.4 4.2 %collective-permute-start.10 = (bf16[128,768]{1,0:T(8,128)(2,1)}, bf16[128,768]{1,0:T(8,128)(2,1)S(1)}, u32[]{:S(2)}, u32[]{:S(2)}) collective-permute-start(bf16[128,768]{1,0:T(8,128)(2,1)} %get-tuple-element.50.refs_5_), channel_id=1, source_target_pairs={{0,384},{8,392},{16,400},{24,408},{32,416},{40,424},{48,432},{56,4... | collective-permute-start | bytes 589832 | tf_op jit(solution)/shard_map/ppermute | solution.py:314
  150.6 2.6 collective-permute-start.9
  153.2 2.2 collective-permute-start.8
  155.4 22.2 %collective-permute-done.9.refs_7_ = bf16[128,768]{1,0:T(8,128)(2,1)} collective-permute-done((bf16[128,768]{1,0:T(8,128)(2,1)}, bf16[128,768]{1,0:T(8,128)(2,1)}, u32[]{:S(2)}, u32[]{:S(2)}) %collective-permute-start.9) | collective-permute-done | bytes 196640 | tf_op jit(solution)/shard_map/ppermute | solution.py:314
  177.6 2.0 collective-permute-done.8.refs_6_
  179.6 0.0 all-gather.7.cloned.1.call-update
  179.6 0.7 broadcast_compare_fusion
  180.3 0.1 broadcast_add_fusion.1
  180.4 1.3 collective-permute-start.12
  181.7 4.2 %collective-permute-start.11 = (bf16[512,512]{1,0:T(8,128)(2,1)S(1)}, bf16[512,512]{1,0:T(8,128)(2,1)S(1)}, u32[]{:S(2)}, u32[]{:S(2)}) collective-permute-start(bf16[512,512]{1,0:T(8,128)(2,1)S(1)} %pad_maximum_fusion.4.refs_2_), channel_id=1, source_target_pairs={{0,8},{8,16},{16,24},{24,32},{32,40},{40,48},{48,56},{56,64},{64,7... | collective-permute-start | bytes 1572872 | tf_op jit(solution)/shard_map/ppermute | solution.py:250
  185.9 0.2 fusion.6
  186.1 0.1 add_convert_fusion.refs_0_
  186.2 13.1 %shard_map.67 = bf16[512,512]{1,0:T(8,128)(2,1)} custom-call(s32[2,6]{1,0:T(2,128)S(1)} %add_convert_fusion.refs_0_, bf16[512,512]{1,0:T(8,128)(2,1)S(1)} %get-tuple-element.40.refs_1_, bf16[512,1024]{1,0:T(8,128)(2,1)} %get-tuple-element.41.refs_2_, bf16[512,1024]{1,0:T(8,128)(2,1)S(1)} %collective-permute-done.6.refs_3_, ...), custom_call_target="tpu_custom_call" | custom-call | flops 3221225472 | bytes 4194304 | tf_op jit(solution)/shard_map/pallas_call | solution.py:77
  199.3 0.8 copy-done.3
  200.1 0.8 copy-done.5
  200.9 6.6 %all-to-all-start.1 = ((bf16[64,8,512]{2,1,0:T(8,128)(2,1)}), bf16[64,8,512]{2,1,0:T(8,128)(2,1)S(1)}, u32[]{:S(2)}, u32[]{:S(2)}) async-start(bf16[64,8,512]{2,1,0:T(8,128)(2,1)} %bitcast.14), calls=%async_computation.1 | async-start | bytes 1048576 | tf_op jit(solution)/shard_map/all_to_all | solution.py:246
  207.5 0.3 all-gather.5.cloned.1.call-start
  208.3 1.0 fusion.12
  209.4 7.7 %shard_map.68 = bf16[512,256]{1,0:T(8,128)(2,1)S(1)} custom-call(s32[2,6]{1,0:T(2,128)S(1)} %add_convert_fusion.refs_0_, bf16[512,256]{1,0:T(8,128)(2,1)S(1)} %pad_maximum_fusion.5.refs_1_, bf16[512,512]{1,0:T(8,128)(2,1)S(1)} %pad_maximum_fusion.4.refs_2_, bf16[512,512]{1,0:T(8,128)(2,1)S(1)} %copy-done.6, bf16[512,512]{1,0:T(8,128)(2,1)S(1)} %copy-done.4, ...), custom_call_target="tpu_custom_call" | custom-call | flops 1610612736 | bytes 2097152 | tf_op jit(solution)/shard_map/pallas_call | solution.py:77
  217.1 1.0 fusion.8
  218.2 18.4 %all-to-all-done.1 = bf16[64,8,512]{2,1,0:T(8,128)(2,1)S(1)} async-done(((bf16[64,8,512]{2,1,0:T(8,128)(2,1)}), bf16[64,8,512]{2,1,0:T(8,128)(2,1)S(1)}, u32[]{:S(2)}, u32[]{:S(2)}) %all-to-all-start.1) | async-done | bytes 524320 | tf_op jit(solution)/shard_map/all_to_all | solution.py:246
  236.6 0.1 fusion.7
  236.7 1.0 maximum_maximum_fusion
  237.7 0.0 all-gather.5.cloned.1.call-update
  237.7 0.1 add.108.order
  237.8 1.7 copy-done
  239.5 0.8 shard_map.69
  240.2 42.0 %all-gather.5.cloned.1.call-done = bf16[1024,3072]{1,0:T(8,128)(2,1)} async-done(((bf16[1024,384]{1,0:T(8,128)(2,1)}), bf16[1024,3072]{1,0:T(8,128)(2,1)}) %all-gather.5.cloned.1.call-update) | async-done | bytes 6291472 | tf_op jit(solution)/shard_map/all_gather | solution.py:331
  282.2 6.4 %convolution_convert_fusion = bf16[1024,384]{1,0:T(8,128)(2,1)} fusion(bf16[1024,3072]{1,0:T(8,128)(2,1)} %all-gather.5.cloned.1.call-done, bf16[3072,384]{1,0:T(8,128)(2,1)S(1)} %shard_map.69), kind=kOutput, calls=%fused_computation.1 | convolution fusion | flops 2416312320 | bytes 9437184 | tf_op jit(solution)/shard_map/dot_general | solution.py:332
  (35 shorter events, 0.2 us)
Async XLA Ops:
  6.5 128.1 %all-gather.9.cloned.1.call-start = ((), (), s32[]{:S(2)}) async-start(), calls=%async_computation.4 | async-start | bytes 1323008 | tf_op jit(solution)/shard_map/all_gather | solution.py:304
  9.8 10.6 %copy-start.7 = (bf16[1024,384]{1,0:T(8,128)(2,1)S(1)}, bf16[1024,384]{1,0:T(8,128)(2,1)}, u32[]{:S(2)}) copy-start(bf16[1024,384]{1,0:T(8,128)(2,1)} %param.6) | copy-start | bytes 2359300
  12.1 9.3 %collective-permute-start.2 = (bf16[128,512]{1,0:T(8,128)(2,1)}, bf16[128,512]{1,0:T(8,128)(2,1)S(1)}, u32[]{:S(2)}, u32[]{:S(2)}) collective-permute-start(bf16[128,512]{1,0:T(8,128)(2,1)} %get-tuple-element.65), channel_id=1, source_target_pairs={{0,128},{1,129},{2,130},{3,131},{4,132},{5,133},{6,134},{7,135}} | collective-permute-start | bytes 393224 | tf_op jit(solution)/shard_map/ppermute | solution.py:260
  16.1 5.3 %collective-permute-start.1 = (bf16[128,512]{1,0:T(8,128)(2,1)}, bf16[128,512]{1,0:T(8,128)(2,1)S(1)}, u32[]{:S(2)}, u32[]{:S(2)}) collective-permute-start(bf16[128,512]{1,0:T(8,128)(2,1)} %get-tuple-element.66), channel_id=1, source_target_pairs={{0,256},{1,257},{2,258},{3,259},{4,260},{5,261},{6,262},{7,263}} | collective-permute-start | bytes 393224 | tf_op jit(solution)/shard_map/ppermute | solution.py:260
  18.4 3.5 %collective-permute-start = (bf16[128,512]{1,0:T(8,128)(2,1)}, bf16[128,512]{1,0:T(8,128)(2,1)}, u32[]{:S(2)}, u32[]{:S(2)}) collective-permute-start(bf16[128,512]{1,0:T(8,128)(2,1)} %get-tuple-element.67), channel_id=1, source_target_pairs={{0,384},{1,385},{2,386},{3,387},{4,388},{5,389},{6,390},{7,391}} | collective-permute-start | bytes 393224 | tf_op jit(solution)/shard_map/ppermute | solution.py:260
  22.1 13.5 %collective-permute-start.5 = (bf16[32,512]{1,0:T(8,128)(2,1)S(1)}, bf16[32,512]{1,0:T(8,128)(2,1)S(1)}, u32[]{:S(2)}, u32[]{:S(2)}) collective-permute-start(bf16[32,512]{1,0:T(8,128)(2,1)S(1)} %get-tuple-element.89), channel_id=1, source_target_pairs={{0,32},{128,160},{256,288},{384,416},{1,33},{129,161},{257,289},{3... | collective-permute-start | bytes 98312 | tf_op jit(solution)/shard_map/ppermute | solution.py:260
  25.6 9.9 %collective-permute-start.4 = (bf16[32,512]{1,0:T(8,128)(2,1)S(1)}, bf16[32,512]{1,0:T(8,128)(2,1)S(1)}, u32[]{:S(2)}, u32[]{:S(2)}) collective-permute-start(bf16[32,512]{1,0:T(8,128)(2,1)S(1)} %get-tuple-element.90), channel_id=1, source_target_pairs={{0,64},{128,192},{256,320},{384,448},{1,65},{129,193},{257,321},{3... | collective-permute-start | bytes 98312 | tf_op jit(solution)/shard_map/ppermute | solution.py:260
  32.9 2.6 collective-permute-start.3
  34.2 1.3 copy-start.1
  34.2 3.7 %copy-start.8 = (s32[24]{0:T(128)S(1)}, s32[24]{0:T(128)}, u32[]{:S(2)}) copy-start(s32[24]{0:T(128)} %param.10) | copy-start | bytes 292
  38.4 99.2 %all-to-all-start = ((bf16[64,8,1536]{2,1,0:T(8,128)(2,1)}), bf16[64,8,1536]{2,1,0:T(8,128)(2,1)S(1)}, u32[]{:S(2)}, u32[]{:S(2)}) async-start(bf16[64,8,1536]{2,1,0:T(8,128)(2,1)} %pad_maximum_fusion), calls=%async_computation | async-start | bytes 3145728 | tf_op jit(solution)/shard_map/all_to_all | solution.py:246
  52.9 184.9 %all-gather.7.cloned.1.call-start = ((), (), s32[]{:S(2)}) async-start(), calls=%async_computation.3 | async-start | bytes 2949120 | tf_op jit(solution)/shard_map/all_gather | solution.py:319
  134.6 1.3 copy-start.2
  139.6 40.0 %collective-permute-start.7 = (bf16[512,1024]{1,0:T(8,128)(2,1)}, bf16[512,1024]{1,0:T(8,128)(2,1)S(1)}, u32[]{:S(2)}, u32[]{:S(2)}) collective-permute-start(bf16[512,1024]{1,0:T(8,128)(2,1)} %get-tuple-element.41.refs_2_), channel_id=1, source_target_pairs={{8,0},{16,8},{24,16},{32,24},{40,32},{48,40},{56,48},{64,56},{72,6... | collective-permute-start | bytes 3145736 | tf_op jit(solution)/shard_map/ppermute | solution.py:251
  140.9 38.7 %collective-permute-start.6 = (bf16[512,1024]{1,0:T(8,128)(2,1)}, bf16[512,1024]{1,0:T(8,128)(2,1)S(1)}, u32[]{:S(2)}, u32[]{:S(2)}) collective-permute-start(bf16[512,1024]{1,0:T(8,128)(2,1)} %get-tuple-element.41.refs_2_), channel_id=1, source_target_pairs={{0,8},{8,16},{16,24},{24,32},{32,40},{40,48},{48,56},{56,64},{64,7... | collective-permute-start | bytes 3145736 | tf_op jit(solution)/shard_map/ppermute | solution.py:250
  146.4 9.0 %collective-permute-start.10 = (bf16[128,768]{1,0:T(8,128)(2,1)}, bf16[128,768]{1,0:T(8,128)(2,1)S(1)}, u32[]{:S(2)}, u32[]{:S(2)}) collective-permute-start(bf16[128,768]{1,0:T(8,128)(2,1)} %get-tuple-element.50.refs_5_), channel_id=1, source_target_pairs={{0,384},{8,392},{16,400},{24,408},{32,416},{40,424},{48,432},{56,4... | collective-permute-start | bytes 589832 | tf_op jit(solution)/shard_map/ppermute | solution.py:314
  150.6 27.0 %collective-permute-start.9 = (bf16[128,768]{1,0:T(8,128)(2,1)}, bf16[128,768]{1,0:T(8,128)(2,1)}, u32[]{:S(2)}, u32[]{:S(2)}) collective-permute-start(bf16[128,768]{1,0:T(8,128)(2,1)} %get-tuple-element.50.refs_5_), channel_id=1, source_target_pairs={{0,256},{8,264},{16,272},{24,280},{32,288},{40,296},{48,304},{56,3... | collective-permute-start | bytes 589832 | tf_op jit(solution)/shard_map/ppermute | solution.py:314
  153.2 26.4 %collective-permute-start.8 = (bf16[128,768]{1,0:T(8,128)(2,1)}, bf16[128,768]{1,0:T(8,128)(2,1)}, u32[]{:S(2)}, u32[]{:S(2)}) collective-permute-start(bf16[128,768]{1,0:T(8,128)(2,1)} %get-tuple-element.50.refs_5_), channel_id=1, source_target_pairs={{0,128},{8,136},{16,144},{24,152},{32,160},{40,168},{48,176},{56,1... | collective-permute-start | bytes 589832 | tf_op jit(solution)/shard_map/ppermute | solution.py:314
  180.4 18.9 %collective-permute-start.12 = (bf16[512,512]{1,0:T(8,128)(2,1)S(1)}, bf16[512,512]{1,0:T(8,128)(2,1)S(1)}, u32[]{:S(2)}, u32[]{:S(2)}) collective-permute-start(bf16[512,512]{1,0:T(8,128)(2,1)S(1)} %pad_maximum_fusion.4.refs_2_), channel_id=1, source_target_pairs={{8,0},{16,8},{24,16},{32,24},{40,32},{48,40},{56,48},{64,56},{72,6... | collective-permute-start | bytes 1572872 | tf_op jit(solution)/shard_map/ppermute | solution.py:251
  181.7 18.4 %collective-permute-start.11 = (bf16[512,512]{1,0:T(8,128)(2,1)S(1)}, bf16[512,512]{1,0:T(8,128)(2,1)S(1)}, u32[]{:S(2)}, u32[]{:S(2)}) collective-permute-start(bf16[512,512]{1,0:T(8,128)(2,1)S(1)} %pad_maximum_fusion.4.refs_2_), channel_id=1, source_target_pairs={{0,8},{8,16},{16,24},{24,32},{32,40},{40,48},{48,56},{56,64},{64,7... | collective-permute-start | bytes 1572872 | tf_op jit(solution)/shard_map/ppermute | solution.py:250
  199.3 0.8 copy-start.3
  200.1 0.8 copy-start.5
  200.9 8.5 %copy-start.4 = (bf16[512,512]{1,0:T(8,128)(2,1)S(1)}, bf16[512,512]{1,0:T(8,128)(2,1)}, u32[]{:S(2)}) copy-start(bf16[512,512]{1,0:T(8,128)(2,1)} %copy-done.3) | copy-start | bytes 1572868
  200.9 8.5 %copy-start.6 = (bf16[512,512]{1,0:T(8,128)(2,1)S(1)}, bf16[512,512]{1,0:T(8,128)(2,1)}, u32[]{:S(2)}) copy-start(bf16[512,512]{1,0:T(8,128)(2,1)} %copy-done.5) | copy-start | bytes 1572868
  200.9 35.7 %all-to-all-start.1 = ((bf16[64,8,512]{2,1,0:T(8,128)(2,1)}), bf16[64,8,512]{2,1,0:T(8,128)(2,1)S(1)}, u32[]{:S(2)}, u32[]{:S(2)}) async-start(bf16[64,8,512]{2,1,0:T(8,128)(2,1)} %bitcast.14), calls=%async_computation.1 | async-start | bytes 1048576 | tf_op jit(solution)/shard_map/all_to_all | solution.py:246
  207.5 74.7 %all-gather.5.cloned.1.call-start = ((), (), s32[]{:S(2)}) async-start(), calls=%async_computation.2 | async-start | bytes 7077888 | tf_op jit(solution)/shard_map/all_gather | solution.py:331
  237.8 1.7 copy-start
Sparse Core Ops, SparseCore 0:
  36.3 98.2 all-gather.8
  179.7 41.9 all-gather.6
  237.8 44.2 all-gather.4
